TPU v7x, 32 devices: a whole 2x2x4 slice. The times are simulated.
32 devices in a mesh: groups: 2 (over y), seq: 16 (over z, x, core).
Axes of the slice: x: 2, y: 2, z: 4, core: 2. Of those that a mesh axis runs over, the one named last changes fastest.
Arguments:
- token_ids: int32 [4096], P('groups'), parts along dimension 0, may hold values from 0 to 511
- vocab_table: bfloat16 [512, 3, 4096], P(None, None, 'seq'), may hold values from -6 to 6
- short_filter: float32 [7, 3, 4096], replicated, may hold values from -2 to 2
- residue: float32 [4096, 16], replicated, may hold values from -1.5 to 1.5
- decay: float32 [4096, 16], replicated, may hold values from 0.2 to 64
- skip_gain: float32 [4096], replicated, may hold values from -3 to 3
Outputs:
- hyena_out: bfloat16 [4096, 4096], P(('groups', 'seq')), parts along dimension 0
There are 2 independent parts, one for each index of `groups`. A program takes and returns all parts, laid end to end along the dimension named above; an argument that names none is the same for every part. Nothing has to cross between parts.
All inputs are finite; a program needn't handle non-finite values.
Results may differ from a plain program's by a relative error of at most 0.012.
Values may be sent and summed in bfloat16 or wider, within the bound.
No kernel may reach another device: no remote copies, remote signals or barrier semaphores. Data moves between devices by JAX's collectives and lax.ppermute only.
A program may use at most 192 MiB of HBM per device.

v0:
```python
import math

import jax
import jax.numpy as jnp
from jax import lax
from jax.sharding import PartitionSpec as P

HIGHEST = lax.Precision.HIGHEST


def angle_tables(first_index, second_index, modulus):
    product = first_index[:, None] * second_index[None, :] % modulus
    angle = product.astype(jnp.float32) * (2.0 * math.pi / modulus)
    return (jnp.cos(angle), jnp.sin(angle))


def short_conv(padded, taps, count):
    width = taps.shape[0]
    total = jnp.zeros((count,) + padded.shape[1:], jnp.float32)
    for lag in range(width):
        start = width - 1 - lag
        total = total + taps[lag] * padded[start : start + count].astype(jnp.float32)
    return total


def filter_spectrum(freq, total, pole, gap, tail, scale):
    theta = freq.astype(jnp.float32) * (2.0 * math.pi / total)
    sine = jnp.sin(theta)[:, :, None, None]
    halfsq = (jnp.sin(0.5 * theta) ** 2)[:, :, None, None]
    parity = (1 - 2 * (freq % 2)).astype(jnp.float32)[:, :, None, None]
    shape_out = freq.shape + (pole.shape[0],)
    real_part = jnp.zeros(shape_out, jnp.float32)
    imag_part = jnp.zeros(shape_out, jnp.float32)
    for first in range(0, pole.shape[1], 4):
        part_pole = pole[:, first : first + 4]
        dreal = gap[:, first : first + 4] + 2.0 * part_pole * halfsq
        dimag = part_pole * sine
        factor = (
            scale[:, first : first + 4]
            * (1.0 - tail[:, first : first + 4] * parity)
            / (dreal * dreal + dimag * dimag)
        )
        real_part = real_part + jnp.sum(factor * dreal, axis=-1)
        imag_part = imag_part - jnp.sum(factor * dimag, axis=-1)
    return (real_part, imag_part)


def convolve(gated, skip, filters, total, move_forward, move_back):
    pieces, block, width = gated.shape
    span = 2 * pieces
    outer_index = jnp.arange(span, dtype=jnp.int32)
    piece_index = jnp.arange(pieces, dtype=jnp.int32)
    outer_cos, outer_sin = angle_tables(outer_index, piece_index, span)
    real_part = jnp.einsum("kp,ptc->ktc", outer_cos, gated, precision=HIGHEST)
    imag_part = -jnp.einsum("kp,ptc->ktc", outer_sin, gated, precision=HIGHEST)
    times = jnp.arange(block, dtype=jnp.int32)
    twist_cos, twist_sin = angle_tables(outer_index, times, total)
    twist_cos = twist_cos[:, :, None]
    twist_sin = twist_sin[:, :, None]
    turned_real = twist_cos * real_part + twist_sin * imag_part
    turned_imag = twist_cos * imag_part - twist_sin * real_part
    moved = move_forward(jnp.stack([turned_real, turned_imag]))
    count = moved.shape[1]
    length = moved.shape[2]
    positions = jnp.arange(length, dtype=jnp.int32)
    inner_cos, inner_sin = angle_tables(positions, positions, length)
    freq_real = jnp.einsum("mt,ktc->kmc", inner_cos, moved[0], precision=HIGHEST) + jnp.einsum(
        "mt,ktc->kmc", inner_sin, moved[1], precision=HIGHEST
    )
    freq_imag = jnp.einsum("mt,ktc->kmc", inner_cos, moved[1], precision=HIGHEST) - jnp.einsum(
        "mt,ktc->kmc", inner_sin, moved[0], precision=HIGHEST
    )
    owned = jnp.arange(count, dtype=jnp.int32)
    freq = (owned[:, None] + span * positions[None, :]) % total
    filt_real, filt_imag = filter_spectrum(freq, total, *filters)
    prod_real = freq_real * filt_real - freq_imag * filt_imag
    prod_imag = freq_real * filt_imag + freq_imag * filt_real
    back_real = jnp.einsum("mt,kmc->ktc", inner_cos, prod_real, precision=HIGHEST) - jnp.einsum(
        "mt,kmc->ktc", inner_sin, prod_imag, precision=HIGHEST
    )
    back_imag = jnp.einsum("mt,kmc->ktc", inner_cos, prod_imag, precision=HIGHEST) + jnp.einsum(
        "mt,kmc->ktc", inner_sin, prod_real, precision=HIGHEST
    )
    undo_cos, undo_sin = angle_tables(owned, positions, total)
    undo_cos = undo_cos[:, :, None]
    undo_sin = undo_sin[:, :, None]
    untwist_real = undo_cos * back_real - undo_sin * back_imag
    untwist_imag = undo_cos * back_imag + undo_sin * back_real
    returned = move_back(jnp.stack([untwist_real, untwist_imag]))
    last_cos, last_sin = angle_tables(piece_index, outer_index, span)
    convolved = (
        jnp.einsum("pk,ktc->ptc", last_cos, returned[0], precision=HIGHEST)
        - jnp.einsum("pk,ktc->ptc", last_sin, returned[1], precision=HIGHEST)
    ) * (1.0 / total)
    return convolved + skip * gated


def unchanged(value):
    return value


def body(token_ids, vocab_table, short_filter, residue, decay, skip_gain):
    pieces = lax.axis_size("seq")
    place = lax.axis_index("seq")
    length = token_ids.shape[0]
    local = length // pieces
    share = vocab_table.shape[2]
    rim = short_filter.shape[0] - 1
    total = 2 * length
    rate = decay / length
    pole = jnp.exp(-rate)
    gap = -jnp.expm1(-rate)
    tail = jnp.exp(-decay)
    scale = residue * jnp.sqrt(2.0 * rate)
    first_channel = place * share
    chan_taps = lax.dynamic_slice_in_dim(short_filter, first_channel, share, 2)
    chan_filters = (
        lax.dynamic_slice_in_dim(pole, first_channel, share, 0),
        lax.dynamic_slice_in_dim(gap, first_channel, share, 0),
        lax.dynamic_slice_in_dim(tail, first_channel, share, 0),
        lax.dynamic_slice_in_dim(scale, first_channel, share, 0),
    )
    chan_skip = lax.dynamic_slice_in_dim(skip_gain, first_channel, share, 0)
    streams = jnp.take(vocab_table, token_ids, axis=0)
    padded = jnp.pad(streams, ((rim, 0), (0, 0), (0, 0)))
    mixed = short_conv(padded, chan_taps, length)
    query = mixed[:, 0]
    gated = (mixed[:, 1] * mixed[:, 2]).reshape(pieces, local, share)
    convolved = convolve(gated, chan_skip, chan_filters, total, unchanged, unchanged)
    output = (query * convolved.reshape(length, share)).astype(jnp.bfloat16)
    return lax.all_to_all(output, "seq", split_axis=0, concat_axis=1, tiled=True)


def solution(mesh):
    placed = (P("groups"), P(None, None, "seq"), P(), P(), P(), P())
    return jax.shard_map(
        body, mesh=mesh, in_specs=placed, out_specs=P(("groups", "seq"), None), check_vma=False
    )
```

profile of v0, /device:TPU:0, one launch (start us, length us, event | category | flops | bytes accessed | tf_op | source)
XLA Modules:
  0.0 295.6 jit_solution(17280626911231516608)
XLA Ops:
  0.0 0.0 copy-start
  0.0 0.8 fusion.84
  0.8 0.7 compare_and_fusion
  1.5 0.1 fusion.77
  1.6 0.1 sine_multiply_fusion
  1.8 1.1 constant_dynamic-slice_fusion.5
  2.9 0.0 copy-done
  2.9 23.5 %gather_fusion = bf16[2048,3,256]{2,0,1:T(8,128)(2,1)} fusion(bf16[512,3,256]{2,0,1:T(8,128)(2,1)S(1)} %copy-done, s32[2048]{0:T(1024)S(1)} %fusion.84), kind=kCustom, calls=%fused_computation | custom fusion | bytes 6299648 | tf_op jit(solution)/shard_map/jit(_take)/gather | solution.py:124
  26.4 2.1 broadcast_select_fusion
  28.6 5.6 %multiply_add_fusion.4 = f32[2048,3,256]{2,0,1:T(8,128)S(1)} fusion(bf16[2048,3,256]{2,0,1:T(8,128)(2,1)S(1)} %broadcast_select_fusion, f32[3,256]{1,0:T(4,128)S(1)} %get-tuple-element.62, f32[3,256]{1,0:T(4,128)S(1)} %get-tuple-element.63, f32[3,256]{1,0:T(4,128)S(1)} %get-tuple-element.64, f32[3,256]{1,0:T(4,128)S(1)} %get-tuple-element.65, ...), kind=kLoop, calls=%fused_computation.29 | loop fusion | flops 31457280 | bytes 9458688 | tf_op jit(solution)/shard_map/add | solution.py:22
  34.2 1.7 slice_multiply_fusion
  35.9 5.6 %fusion.15 = f32[32,128,256]{2,0,1:T(8,128)} fusion(f32[16,128,256]{2,1,0:T(8,128)S(1)} %bitcast.84), kind=kOutput, calls=%fused_computation.54 | convolution fusion | flops 201333760 | bytes 6291456 | tf_op jit(solution)/shard_map/kp,ptc->ktc/dot_general | solution.py:55
  41.5 0.1 copy.173
  41.6 0.1 copy.175
  41.7 9.1 %multiply_add_fusion.5 = (f32[32,128,256]{2,0,1:T(8,128)}, f32[32,128,256]{2,0,1:T(8,128)}) fusion(f32[32,128,256]{2,0,1:T(8,128)} %fusion.15, f32[32,128]{0,1:T(8,128)S(1)} %copy.175, f32[32,128]{0,1:T(8,128)S(1)} %copy.173, f32[16,128,256]{2,1,0:T(8,128)S(1)} %bitcast.85), kind=kOutput, calls=%fused_computation.41 | convolution fusion | flops 208673792 | bytes 14712832 | tf_op jit(solution)/shard_map/kp,ptc->ktc/dot_general | solution.py:54
  50.8 0.0 copy-done.4
  50.8 5.3 %copy.177 = f32[32,128,256]{1,2,0:T(8,128)} copy(f32[32,128,256]{2,0,1:T(8,128)} %get-tuple-element.20) | data formatting | bytes 8388608 | tf_op jit(solution)/shard_map/add | solution.py:60
  56.1 7.0 %fusion.32 = f32[32,256,128]{2,1,0:T(8,128)} fusion(f32[32,128,256]{1,2,0:T(8,128)} %copy.177), kind=kOutput, calls=%fused_computation.75 | convolution fusion | flops 1610842112 | bytes 8388608 | tf_op jit(solution)/shard_map/mt,ktc->kmc/dot_general | solution.py:67
  63.1 5.3 %copy.178 = f32[32,128,256]{1,2,0:T(8,128)} copy(f32[32,128,256]{2,0,1:T(8,128)} %get-tuple-element.21) | data formatting | bytes 8388608 | tf_op jit(solution)/shard_map/sub | solution.py:61
  68.4 18.2 %fusion.30 = f32[32,256,128]{2,1,0:T(8,128)} fusion(f32[32,128,256]{1,2,0:T(8,128)} %copy.178), kind=kOutput, calls=%fused_computation.73 | convolution fusion | flops 1610842112 | bytes 8388608 | tf_op jit(solution)/shard_map/mt,ktc->kmc/dot_general | solution.py:70
  86.6 0.0 copy-done.6
  86.6 5.5 %convolution_add_fusion.1 = f32[32,256,128]{2,1,0:T(8,128)} fusion(f32[32,256,128]{2,1,0:T(8,128)S(1)} %copy-done.6, f32[32,128,256]{1,2,0:T(8,128)S(1)} %copy-done.2), kind=kOutput, calls=%fused_computation.50 | convolution fusion | flops 1611890688 | bytes 12582912 | tf_op jit(solution)/shard_map/mt,ktc->kmc/dot_general | solution.py:67
  92.1 0.7 dynamic-slice_multiply_fusion
  92.9 38.2 %fusion.2 = (f32[32,128,256]{2,1,0:T(8,128)}, f32[32,128,256]{2,1,0:T(8,128)}, f32[32,128,256]{2,1,0:T(8,128)}, f32[32,128,256]{2,1,0:T(8,128)}, f32[32,128,256]{2,1,0:T(8,128)}, /*index=5*/f32[32,128,256]{2,1,0:T(8,128)}) fusion(f32[32,128]{1,0:T(8,128)S(1)} %get-tuple-element.58, f32[256,4]{0,1:T(4,128)S(1)} %get-tuple-element.55, ...), kind=kLoop, calls=%fused_computation.11 | loop fusion | flops 169869312 | bytes 25276416 | tf_op jit(solution)/shard_map/reduce_sum | solution.py:44
  131.1 5.6 %copy.179 = f32[32,128,256]{1,2,0:T(8,128)} copy(f32[32,128,256]{2,1,0:T(8,128)} %get-tuple-element.6) | data formatting | bytes 8388608 | tf_op jit(solution)/shard_map/reduce_sum | solution.py:43
  136.7 5.6 %copy.181 = f32[32,128,256]{1,2,0:T(8,128)} copy(f32[32,128,256]{2,1,0:T(8,128)} %get-tuple-element.15) | data formatting | bytes 8388608 | tf_op jit(solution)/shard_map/reduce_sum | solution.py:43
  142.3 5.6 %copy.182 = f32[32,128,256]{1,2,0:T(8,128)} copy(f32[32,128,256]{2,1,0:T(8,128)} %get-tuple-element.13) | data formatting | bytes 8388608 | tf_op jit(solution)/shard_map/reduce_sum | solution.py:43
  147.8 5.6 %copy.185 = f32[32,128,256]{1,2,0:T(8,128)} copy(f32[32,128,256]{2,1,0:T(8,128)} %get-tuple-element.5) | data formatting | bytes 8388608 | tf_op jit(solution)/shard_map/reduce_sum | solution.py:44
  153.4 5.6 %copy.187 = f32[32,128,256]{1,2,0:T(8,128)} copy(f32[32,128,256]{2,1,0:T(8,128)} %get-tuple-element.16) | data formatting | bytes 8388608 | tf_op jit(solution)/shard_map/reduce_sum | solution.py:44
  159.0 5.6 %copy.188 = f32[32,128,256]{1,2,0:T(8,128)} copy(f32[32,128,256]{2,1,0:T(8,128)} %get-tuple-element.14) | data formatting | bytes 8388608 | tf_op jit(solution)/shard_map/reduce_sum | solution.py:44
  164.6 13.4 %fusion.5 = (f32[32,128,256]{2,1,0:T(8,128)}, f32[32,128,256]{2,1,0:T(8,128)}) fusion(f32[256,4]{0,1:T(4,128)S(1)} %get-tuple-element.54, f32[32,128]{1,0:T(8,128)S(1)} %get-tuple-element.58, f32[32,128]{1,0:T(8,128)S(1)} %get-tuple-element.57, f32[256,4]{0,1:T(4,128)S(1)} %get-tuple-element.49, f32[256,4]{0,1:T(4,128)S(1)} %get-tuple-element.45, ...), kind=kLoop, calls=%fused_computation.14 | loop fusion | flops 56623104 | bytes 8458240 | tf_op jit(solution)/shard_map/reduce_sum | solution.py:44
  177.9 5.6 %copy.180 = f32[32,128,256]{1,2,0:T(8,128)} copy(f32[32,128,256]{2,1,0:T(8,128)} %get-tuple-element.8) | data formatting | bytes 8388608 | tf_op jit(solution)/shard_map/reduce_sum | solution.py:43
  183.5 5.6 %copy.186 = f32[32,128,256]{1,2,0:T(8,128)} copy(f32[32,128,256]{2,1,0:T(8,128)} %get-tuple-element.7) | data formatting | bytes 8388608 | tf_op jit(solution)/shard_map/reduce_sum | solution.py:44
  189.1 22.1 %fusion.12 = (f32[32,128,256]{1,2,0:T(8,128)S(1)}, f32[32,128,256]{1,2,0:T(8,128)}, f32[32,128,256]{1,2,0:T(8,128)}, f32[32,256,128]{2,1,0:T(8,128)}) fusion(f32[32,256,128]{2,1,0:T(8,128)} %convolution_add_fusion.1, f32[32,128,256]{1,2,0:T(8,128)} %copy.188, f32[32,128,256]{1,2,0:T(8,128)} %copy.187, f32[32,128,256]{1,2,0:T(8,128)} %copy.186, ...), kind=kOutput, calls=%fused_computation.32 | convolution fusion | flops 1622376448 | bytes 62914560 | tf_op jit(solution)/shard_map/mt,ktc->kmc/dot_general | solution.py:70
  211.2 6.3 %fusion.13 = f32[32,128,256]{1,2,0:T(8,128)S(1)} fusion(f32[32,128,256]{1,2,0:T(8,128)} %get-tuple-element.19, f32[32,256,128]{2,1,0:T(8,128)} %get-tuple-element.59, f32[32,128,256]{1,2,0:T(8,128)} %get-tuple-element.18, f32[32,256,128]{2,1,0:T(8,128)S(1)} %copy-done.3), kind=kLoop, calls=%fused_computation.33 | loop fusion | flops 3145728 | bytes 20971520 | tf_op jit(solution)/shard_map/add | solution.py:77
  217.5 3.8 %fusion.26 = f32[32,256,128]{2,1,0:T(8,128)S(1)} fusion(f32[32,128,256]{1,2,0:T(8,128)S(1)} %fusion.13), kind=kOutput, calls=%fused_computation.69 | convolution fusion | flops 1610842112 | bytes 8388608 | tf_op jit(solution)/shard_map/mt,kmc->ktc/dot_general | solution.py:81
  221.3 3.8 %fusion.28 = f32[32,256,128]{2,1,0:T(8,128)S(1)} fusion(f32[32,128,256]{1,2,0:T(8,128)S(1)} %get-tuple-element.17), kind=kOutput, calls=%fused_computation.71 | convolution fusion | flops 1610842112 | bytes 8388608 | tf_op jit(solution)/shard_map/mt,kmc->ktc/dot_general | solution.py:78
  225.1 4.0 %convolution_add_fusion = f32[32,256,128]{2,1,0:T(8,128)S(1)} fusion(f32[32,256,128]{2,1,0:T(8,128)S(1)} %fusion.26, f32[32,128,256]{1,2,0:T(8,128)S(1)} %get-tuple-element.17), kind=kOutput, calls=%fused_computation.47 | convolution fusion | flops 1611890688 | bytes 12582912 | tf_op jit(solution)/shard_map/mt,kmc->ktc/dot_general | solution.py:81
  229.1 6.7 %add_bitcast_fusion = (f32[32,128,256]{1,2,0:T(8,128)}, f32[32,128,256]{1,2,0:T(8,128)}) fusion(f32[32,256,128]{2,1,0:T(8,128)S(1)} %convolution_add_fusion, f32[32,128]{1,0:T(8,128)S(1)} %get-tuple-element.68, f32[32,128]{1,0:T(8,128)S(1)} %get-tuple-element.69, f32[32,256,128]{2,1,0:T(8,128)S(1)} %fusion.28, f32[32,128,256]{1,2,0:T(8,128)S(1)} %fusion.13), kind=kOutput, calls=%fused_computation.36 | convolution fusion | flops 1618182144 | bytes 21004288 | tf_op jit(solution)/shard_map/mt,kmc->ktc/dot_general | solution.py:78
  235.7 5.5 %copy.189 = f32[32,128,256]{2,0,1:T(8,128)} copy(f32[32,128,256]{1,2,0:T(8,128)} %get-tuple-element.23) | data formatting | bytes 8388608 | tf_op jit(solution)/shard_map/sub | solution.py:87
  241.2 5.6 %fusion.70 = f32[16,128,256]{2,0,1:T(8,128)} fusion(f32[32,128,256]{2,0,1:T(8,128)} %copy.189), kind=kOutput, calls=%fused_computation.127 | convolution fusion | flops 201333760 | bytes 6291456 | tf_op jit(solution)/shard_map/pk,ktc->ptc/dot_general | solution.py:92
  246.9 5.6 %copy.190 = f32[32,128,256]{2,0,1:T(8,128)} copy(f32[32,128,256]{1,2,0:T(8,128)} %get-tuple-element.22) | data formatting | bytes 8388608 | tf_op jit(solution)/shard_map/add | solution.py:88
  252.5 0.8 dynamic_slice.23
  253.3 7.8 %fusion.14 = bf16[16,128,256]{2,0,1:T(8,128)(2,1)S(1)} fusion(f32[16,128,256]{2,1,0:T(8,128)} %bitcast.87, f32[16,128,256]{2,0,1:T(8,128)} %fusion.70, f32[16,128,256]{2,1,0:T(8,128)S(1)} %bitcast.86, f32[32,128,256]{2,0,1:T(8,128)} %copy.190, f32[256]{0:T(256)S(1)} %dynamic_slice.23), kind=kOutput, calls=%fused_computation.53 | convolution fusion | flops 204479488 | bytes 11535360 | tf_op jit(solution)/shard_map/pk,ktc->ptc/dot_general | solution.py:93
  261.1 0.3 copy.193
  261.4 32.0 %all_to_all.16 = bf16[16,128,256]{2,1,0:T(8,128)(2,1)S(1)} all-to-all(bf16[16,128,256]{2,1,0:T(8,128)(2,1)S(1)} %copy.193), channel_id=1, replica_groups=mesh['groups'=2,'seq'=16] {'seq'}, dimensions={0} | all-to-all | bytes 2097152 | tf_op jit(solution)/shard_map/all_to_all | solution.py:131
  293.4 0.7 copy.194
  294.1 1.3 copy.195
  (23 shorter events, 0.1 us)
Async XLA Ops:
  0.0 2.9 copy-start
  35.9 14.9 %copy-start.4 = (f32[2048,1,256]{2,0,1:T(8,128)}, f32[2048,1,256]{2,0,1:T(8,128)S(1)}, u32[]{:S(2)}) copy-start(f32[2048,1,256]{2,0,1:T(8,128)S(1)} %get-tuple-element.24) | copy-start | bytes 6291460
  68.4 18.2 %copy-start.2 = (f32[32,128,256]{1,2,0:T(8,128)S(1)}, f32[32,128,256]{1,2,0:T(8,128)}, u32[]{:S(2)}) copy-start(f32[32,128,256]{1,2,0:T(8,128)} %copy.178) | copy-start | bytes 12582916
  68.4 18.2 %copy-start.6 = (f32[32,256,128]{2,1,0:T(8,128)S(1)}, f32[32,256,128]{2,1,0:T(8,128)}, u32[]{:S(2)}) copy-start(f32[32,256,128]{2,1,0:T(8,128)} %fusion.32) | copy-start | bytes 12582916
  86.6 5.5 %copy-start.7 = (f32[4096,16]{0,1:T(8,128)S(1)}, f32[4096,16]{0,1:T(8,128)}, u32[]{:S(2)}) copy-start(f32[4096,16]{0,1:T(8,128)} %param.10) | copy-start | bytes 786436
  189.1 22.1 %copy-start.3 = (f32[32,256,128]{2,1,0:T(8,128)S(1)}, f32[32,256,128]{2,1,0:T(8,128)}, u32[]{:S(2)}) copy-start(f32[32,256,128]{2,1,0:T(8,128)} %convolution_add_fusion.1) | copy-start | bytes 12582916
  246.9 6.4 %copy-start.5 = (f32[2048,1,256]{2,0,1:T(8,128)S(1)}, f32[2048,1,256]{2,0,1:T(8,128)}, u32[]{:S(2)}) copy-start(f32[2048,1,256]{2,0,1:T(8,128)} %copy-done.4) | copy-start | bytes 6291460
  253.3 42.1 %copy-start.1 = (bf16[512,3,256]{2,0,1:T(8,128)(2,1)S(1)}, bf16[512,3,256]{2,0,1:T(8,128)(2,1)}, u32[]{:S(2)}) copy-start(bf16[512,3,256]{2,0,1:T(8,128)(2,1)} %param.7) | copy-start | bytes 2359300
where the time goes:
time: 300 us; the launch traced here: 296 us
  matrix products  99.2 us (33%)
  local copies, waits for them, and re-layouts  94.3 us (31%)
  other arithmetic  69.7 us (23%)
  blocking collectives  32 us (11%)
    reduce_sum x2, other arithmetic, filter_spectrum(): imag_part = imag_part - jnp.sum(factor * dimag, axis=-1)  51.5 us
    all_to_all x1, blocking collectives, body(): lax.all_to_all(output, 'seq', split_axis=0, concat_axis=1, tiled=True)  32 us
    gather x1, local copies, waits for them, and re-layouts, body(): streams = jnp.take(vocab_table, token_ids, axis=0)  23.5 us
    reduce_sum x4, local copies, waits for them, and re-layouts, filter_spectrum(): real_part = real_part + jnp.sum(factor * dreal, axis=-1)  22.3 us
    reduce_sum x4, local copies, waits for them, and re-layouts, filter_spectrum(): imag_part = imag_part - jnp.sum(factor * dimag, axis=-1)  22.3 us
    dot_general x1, matrix products, convolve(): jnp.einsum('mt,ktc->kmc', inner_sin, moved[0], precision=HIGHEST)  22.1 us
    dot_general x1, matrix products, convolve(): jnp.einsum('mt,ktc->kmc', inner_cos, moved[1], precision=HIGHEST)  18.2 us
    dot_general x1, matrix products, convolve(): real_part = jnp.einsum('kp,ptc->ktc', outer_cos, gated, precision=HIGHEST)  9.14 us

commit v1 on v0

v1 whole, which is shorter than its diff:
```python
import functools

import jax
import jax.numpy as jnp
from jax import lax
from jax.experimental import pallas as pl
from jax.experimental.pallas import tpu as pltpu
from jax.sharding import PartitionSpec as P

LANES = 128
RUNS = 8


def tree_sum(terms):
    while len(terms) > 1:
        pairs = [a + b for a, b in zip(terms[::2], terms[1::2])]
        terms = pairs + ([terms[-1]] if len(terms) % 2 else [])
    return terms[0]


def delay_runs(value, by):
    moved = pltpu.roll(value, by, 0)
    return jnp.where(lax.broadcasted_iota(jnp.int32, value.shape, 0) < by, 0.0, moved)


def operator(ids, table, taps, residue, decay, skip, out, onehot, streams, query, gated, result):
    steps = ids.shape[1]
    vocab = table.shape[1]
    width = taps.shape[0]
    modes = residue.shape[0]
    rim = width - 1
    length = steps * RUNS
    tile = (RUNS, LANES)

    cols = min(LANES, steps)
    part = min(32, cols)
    word = lax.broadcasted_iota(jnp.int32, (RUNS, vocab), 1)

    def look_up(block, _):
        here = ids[:, pl.ds(pl.multiple_of(block * cols, cols), cols)]
        for first in range(0, cols, part):
            hot = [
                jnp.where(jnp.broadcast_to(here[:, j : j + 1], word.shape) == word, 1.0, 0.0)
                for j in range(first, first + part)
            ]
            onehot[...] = jnp.concatenate(hot, axis=0).astype(jnp.bfloat16)
            row = (rim + block * cols + first) * RUNS
            row = pl.multiple_of(row, RUNS)
            for k in range(3):
                streams[k, pl.ds(row, part * RUNS), :] = jnp.dot(
                    onehot[...], table[k], preferred_element_type=jnp.float32
                )
        return 0

    lax.fori_loop(0, steps // cols, look_up, 0)
    for k in range(3):
        for j in range(rim):
            streams[k, j * RUNS : (j + 1) * RUNS, :] = delay_runs(
                streams[k, (steps + j) * RUNS : (steps + j + 1) * RUNS, :], 1
            )

    def mix(j, _):
        mixed = []
        for k in range(3):
            terms = []
            for lag in range(width):
                row = pl.multiple_of((j + rim - lag) * RUNS, RUNS)
                tap = jnp.broadcast_to(taps[lag, k : k + 1, :], tile)
                terms.append(tap * streams[k, pl.ds(row, RUNS), :])
            mixed.append(tree_sum(terms))
        row = pl.multiple_of(j * RUNS, RUNS)
        query[pl.ds(row, RUNS), :] = mixed[0]
        gated[pl.ds(row, RUNS), :] = mixed[1] * mixed[2]
        return 0

    lax.fori_loop(0, steps, mix, 0, unroll=8)

    rate = decay[...] / length
    weight = residue[...] * jnp.sqrt(2.0 * rate)
    pole = jnp.exp(-rate)
    spread = lambda rows, s: jnp.broadcast_to(rows[s : s + 1, :], tile)
    poles = [spread(pole, s) for s in range(modes)]
    weights = [spread(weight, s) for s in range(modes)]

    def advance(j, state):
        now = gated[pl.ds(pl.multiple_of(j * RUNS, RUNS), RUNS), :]
        return tuple(p * x + now for p, x in zip(poles, state))

    zero = jnp.zeros(tile, jnp.float32)
    ends = lax.fori_loop(0, steps, advance, (zero,) * modes, unroll=8)
    begins = []
    for s in range(modes):
        value = delay_runs(ends[s], 1)
        by = 1
        while by < RUNS:
            leap = spread(jnp.exp(-rate * (steps * by)), s)
            value = value + leap * delay_runs(value, by)
            by *= 2
        begins.append(value)
    direct = jnp.broadcast_to(skip[...], tile)

    def emit(j, state):
        row = pl.multiple_of(j * RUNS, RUNS)
        now = gated[pl.ds(row, RUNS), :]
        state = tuple(p * x + now for p, x in zip(poles, state))
        total = tree_sum([w * x for w, x in zip(weights, state)])
        result[pl.ds(j, RUNS, stride=steps), :] = query[pl.ds(row, RUNS), :] * (total + direct * now)
        return state

    lax.fori_loop(0, steps, emit, tuple(begins), unroll=8)
    out[...] = result[...].astype(jnp.bfloat16)


def run_operator(ids, table, taps, residue, decay, skip, piece):
    steps = ids.shape[1]
    length = steps * RUNS
    rim = taps.shape[0] - 1
    part = min(32, steps)
    chan = lambda *lead: pl.BlockSpec(lead + (LANES,), lambda i: (0,) * len(lead) + (piece,))
    return pl.pallas_call(
        operator,
        grid=(1,),
        out_shape=jax.ShapeDtypeStruct((length, LANES), jnp.bfloat16),
        in_specs=[
            pl.BlockSpec(ids.shape, lambda i: (0, 0)),
            chan(*table.shape[:2]),
            chan(*taps.shape[:2]),
            chan(residue.shape[0]),
            chan(decay.shape[0]),
            chan(1),
        ],
        out_specs=pl.BlockSpec((length, LANES), lambda i: (0, 0)),
        scratch_shapes=[
            pltpu.VMEM((part * RUNS, table.shape[1]), jnp.bfloat16),
            pltpu.VMEM((3, length + rim * RUNS, LANES), jnp.float32),
            pltpu.VMEM((length, LANES), jnp.float32),
            pltpu.VMEM((length, LANES), jnp.float32),
            pltpu.VMEM((length, LANES), jnp.float32),
        ],
        compiler_params=pltpu.CompilerParams(vmem_limit_bytes=56 * 2**20),
        cost_estimate=pl.CostEstimate(flops=length * LANES * 8000, bytes_accessed=4 * 2**20, transcendentals=0),
    )(ids, table, taps, residue, decay, skip)


def body(token_ids, vocab_table, short_filter, residue, decay, skip_gain):
    places = lax.axis_size("seq")
    place = lax.axis_index("seq")
    length = token_ids.shape[0]
    local = length // places
    share = vocab_table.shape[2]
    pieces = -(-share // LANES)
    widen = lambda x: jnp.pad(x, [(0, 0)] * (x.ndim - 1) + [(0, pieces * LANES - share)])
    mine = lambda x, axis: lax.dynamic_slice_in_dim(x, place * share, share, axis)
    ids = token_ids.reshape(RUNS, length // RUNS)
    table = widen(vocab_table.transpose(1, 0, 2))
    taps = widen(mine(short_filter, 2))
    res = widen(mine(residue, 0).T)
    dec = widen(mine(decay, 0).T)
    skip = widen(mine(skip_gain, 0)[None])
    parts = []
    for piece in range(pieces):
        outcome = run_operator(ids, table, taps, res, dec, skip, piece)
        kept = min(LANES, share - piece * LANES)
        sent = outcome[:, :kept].reshape(places, local, kept)
        parts.append(lax.all_to_all(sent, "seq", split_axis=0, concat_axis=0, tiled=True))
    joined = jnp.concatenate(parts, axis=2)
    return joined.transpose(1, 0, 2).reshape(local, places * share)


def solution(mesh):
    placed = (P("groups"), P(None, None, "seq"), P(), P(), P(), P())
    return jax.shard_map(
        body, mesh=mesh, in_specs=placed, out_specs=P(("groups", "seq"), None), check_vma=False
    )
```

time: 300 us -> 56.3 us (0.19); the launches traced: 296 us -> 55.8 us
  matrix products: 99.2 us -> 0 us
  local copies, waits for them, and re-layouts: 94.3 us -> 5.68 us
  other arithmetic: 69.7 us -> 0.14 us
  Pallas kernels: 0 us -> 19.2 us
  blocking collectives: 32 us -> 18.6 us
  starting transfers between devices: 0 us -> 7.36 us
  waiting for transfers between devices: 0 us -> 4.87 us
    dot_general x12 -> x0, matrix products: 99.2 us -> none  [the longest x1 22.1 us: convolve(): jnp.einsum('mt,ktc->kmc', inner_sin, moved[0], precision=HIGHEST)]
    reduce_sum x2 -> x0, other arithmetic: 51.5 us -> none  [filter_spectrum(): imag_part = imag_part - jnp.sum(factor * dimag, axis=-1)]
    reduce_sum x8 -> x0, local copies, waits for them, and re-layouts: 44.6 us -> none  [the longest x4 22.3 us: filter_spectrum(): real_part = real_part + jnp.sum(factor * dreal, axis=-1)]
    gather x1 -> x0, local copies, waits for them, and re-layouts: 23.5 us -> none  [body(): streams = jnp.take(vocab_table, token_ids, axis=0)]
    pallas_call x0 -> x2, Pallas kernels: none -> 19.2 us  [run_operator(): pl.pallas_call(operator, grid=(1,), out_shape=jax.ShapeDtypeStruct((lengt...]
    all_to_all x1, blocking collectives: 32 us -> 18.6 us  [body(): lax.all_to_all(sent, 'seq', split_axis=0, concat_axis=0, tiled=True)]
    add x2 -> x0, other arithmetic: 11.9 us -> none  [the longest x1 6.26 us: convolve(): prod_imag = freq_real * filt_imag + freq_imag * filt_real]
    add x2 -> x0, local copies, waits for them, and re-layouts: 10.9 us -> none  [the longest x1 5.65 us: convolve(): untwist_imag = undo_cos * back_imag + undo_sin * back_real]
  transfers between devices with their start and end apart: 0 -> 1, of which waited for: 0 -> 1; matrix products, arithmetic and copies ran while one was open for 0% -> 0% of each run, Pallas kernels for 0% -> 17%
where the time goes in v1:
time: 56.3 us; the launch traced here: 55.8 us
  Pallas kernels  19.2 us (34%)
  blocking collectives  18.6 us (33%)
  starting transfers between devices  7.36 us (13%)
  local copies, waits for them, and re-layouts  5.68 us (10%)
  waiting for transfers between devices  4.87 us (9%)
    pallas_call x2, Pallas kernels, run_operator(): pl.pallas_call(operator, grid=(1,), out_shape=jax.ShapeDtypeStruct((lengt...  19.2 us
    all_to_all x1, blocking collectives, body(): lax.all_to_all(sent, 'seq', split_axis=0, concat_axis=0, tiled=True)  18.6 us
    all_to_all x1, starting transfers between devices, body(): lax.all_to_all(sent, 'seq', split_axis=0, concat_axis=0, tiled=True)  7.36 us
    all_to_all x1, waiting for transfers between devices, body(): lax.all_to_all(sent, 'seq', split_axis=0, concat_axis=0, tiled=True)  4.87 us
    transpose x1, local copies, waits for them, and re-layouts, body(): dec = widen(mine(decay, 0).T)  1.34 us
    dynamic_slice x2, local copies, waits for them, and re-layouts, body(): lax.dynamic_slice_in_dim(x, place * share, share, axis)  1.33 us
    reshape x1, local copies, waits for them, and re-layouts, body(): ids = token_ids.reshape(RUNS, length // RUNS)  1.32 us
  transfers between devices with their start and end apart: 1, of which 1 were waited for; matrix products, arithmetic and copies ran while one was open for 0% of the time, Pallas kernels for 17%

profile of v1, /device:TPU:0, one launch (start us, length us, event | category | flops | bytes accessed | tf_op | source)
XLA Modules:
  0.0 55.8 jit_solution(1066636644808665372)
XLA Ops:
  0.0 0.0 copy-start
  0.0 1.3 %reshape.12.ids = s32[8,256]{1,0:T(8,128)} reshape(s32[2048]{0:T(1024)} %param.6) | data formatting | bytes 16384 | tf_op jit(solution)/shard_map/reshape | solution.py:154
  1.3 1.3 %dynamic_slice.15 = f32[256]{0:T(256)} dynamic-slice(f32[4096]{0:T(1024)} %param.11, s32[]{:T(128)S(6)} %select_n.2), dynamic_slice_sizes={256} | dynamic-slice | bytes 2052 | tf_op jit(solution)/shard_map/dynamic_slice | solution.py:153
  2.7 0.0 copy-done
  2.7 0.6 %copy.9.taps = f32[7,3,256]{2,1,0:T(4,128)} copy(f32[7,3,256]{2,0,1:T(8,128)S(1)} %constant_dynamic-slice_fusion) | data formatting | bytes 43008
  3.3 1.3 %dynamic-slice_bitcast_fusion = (f32[16,256]{1,0:T(8,128)}, f32[16,256]{1,0:T(8,128)}) fusion(f32[4096,16]{0,1:T(8,128)} %param.10, s32[]{:T(128)S(6)} %select_n.2, f32[4096,16]{0,1:T(8,128)} %param.9), kind=kLoop, calls=%fused_computation.1 | loop fusion | bytes 65540 | tf_op jit(solution)/shard_map/transpose | solution.py:158
  4.6 9.6 %shard_map.65 = bf16[2048,128]{1,0:T(8,128)(2,1)} custom-call(s32[8,256]{1,0:T(8,128)} %reshape.12.ids, bf16[3,512,256]{2,1,0:T(8,128)(2,1)} %bitcast.16, f32[7,3,256]{2,1,0:T(4,128)} %copy.9.taps, f32[16,256]{1,0:T(8,128)} %get-tuple-element.6.residue, f32[16,256]{1,0:T(8,128)} %get-tuple-element.5.decay, f32[1,256]{1,0:T(1,128)} %bitcast.14), custom_call_target="tpu_custom_call" | custom-call | flops 2097152000 | bytes 4194304 | tf_op jit(solution)/shard_map/pallas_call | solution.py:120
  14.2 7.4 %all-to-all-start.1 = ((bf16[16,128,128]{2,1,0:T(8,128)(2,1)}), bf16[16,128,128]{2,1,0:T(8,128)(2,1)S(1)}, u32[]{:S(2)}, u32[]{:S(2)}) async-start(bf16[16,128,128]{2,1,0:T(8,128)(2,1)} %bitcast.12), calls=%async_computation.1 | async-start | bytes 1048576 | tf_op jit(solution)/shard_map/all_to_all | solution.py:165
  21.6 9.6 %shard_map.64 = bf16[2048,128]{1,0:T(8,128)(2,1)} custom-call(s32[8,256]{1,0:T(8,128)} %reshape.12.ids, bf16[3,512,256]{2,1,0:T(8,128)(2,1)} %bitcast.17, f32[7,3,256]{2,1,0:T(4,128)} %copy.9.taps, f32[16,256]{1,0:T(8,128)} %get-tuple-element.6.residue, f32[16,256]{1,0:T(8,128)} %get-tuple-element.5.decay, f32[1,256]{1,0:T(1,128)} %bitcast.15), custom_call_target="tpu_custom_call" | custom-call | flops 2097152000 | bytes 4194304 | tf_op jit(solution)/shard_map/pallas_call | solution.py:120
  31.2 4.9 %all-to-all-done.1 = bf16[16,128,128]{2,1,0:T(8,128)(2,1)S(1)} async-done(((bf16[16,128,128]{2,1,0:T(8,128)(2,1)}), bf16[16,128,128]{2,1,0:T(8,128)(2,1)S(1)}, u32[]{:S(2)}, u32[]{:S(2)}) %all-to-all-start.1) | async-done | bytes 524320 | tf_op jit(solution)/shard_map/all_to_all | solution.py:165
  36.0 18.6 %all_to_all.10 = bf16[16,128,128]{2,1,0:T(8,128)(2,1)S(1)} all-to-all(bf16[16,128,128]{2,1,0:T(8,128)(2,1)} %bitcast.13), channel_id=1, replica_groups=mesh['groups'=2,'seq'=16] {'seq'}, dimensions={0} | all-to-all | bytes 1048576 | tf_op jit(solution)/shard_map/all_to_all | solution.py:165
  54.6 0.1 maximum_bitcast_fusion
  54.7 1.1 %copy.10 = bf16[16,16,8,256]{3,2,0,1:T(8,128)(2,1)} copy(bf16[16,16,8,256]{3,2,1,0:T(8,128)(2,1)S(1)} %maximum_bitcast_fusion) | data formatting | bytes 2097152 | tf_op jit(solution)/shard_map/reshape | solution.py:167
  (1 shorter events, 0.0 us)
Async XLA Ops:
  0.0 2.7 %copy-start = (f32[7,3,4096]{2,0,1:T(8,128)S(1)}, f32[7,3,4096]{2,0,1:T(8,128)}, u32[]{:S(2)}) copy-start(f32[7,3,4096]{2,0,1:T(8,128)} %param.8) | copy-start | bytes 1032196
  14.2 21.8 %all-to-all-start.1 = ((bf16[16,128,128]{2,1,0:T(8,128)(2,1)}), bf16[16,128,128]{2,1,0:T(8,128)(2,1)S(1)}, u32[]{:S(2)}, u32[]{:S(2)}) async-start(bf16[16,128,128]{2,1,0:T(8,128)(2,1)} %bitcast.12), calls=%async_computation.1 | async-start | bytes 1048576 | tf_op jit(solution)/shard_map/all_to_all | solution.py:165

commit v2 on v1

--- a/solution.py
+++ b/solution.py
@@ -1,4 +1,4 @@
-import functools
+import math
 
 import jax
 import jax.numpy as jnp
@@ -23,21 +23,22 @@
     return jnp.where(lax.broadcasted_iota(jnp.int32, value.shape, 0) < by, 0.0, moved)
 
 
-def operator(ids, table, taps, residue, decay, skip, out, onehot, streams, query, gated, result):
-    steps = ids.shape[1]
+def operator(spot, ids, table, taps, residue, decay, skip, *rest):
+    outs, (onehot, streams, query, gated, result) = rest[:-5], rest[-5:]
+    length = ids.shape[0] * ids.shape[1]
+    steps = length // RUNS
     vocab = table.shape[1]
-    width = taps.shape[0]
+    width = taps.shape[1]
     modes = residue.shape[0]
     rim = width - 1
-    length = steps * RUNS
     tile = (RUNS, LANES)
 
-    cols = min(LANES, steps)
-    part = min(32, cols)
+    cols = ids.shape[1]
+    part = onehot.shape[0] // RUNS
     word = lax.broadcasted_iota(jnp.int32, (RUNS, vocab), 1)
 
     def look_up(block, _):
-        here = ids[:, pl.ds(pl.multiple_of(block * cols, cols), cols)]
+        here = ids[pl.ds(block, RUNS, stride=steps // cols), :]
         for first in range(0, cols, part):
             hot = [
                 jnp.where(jnp.broadcast_to(here[:, j : j + 1], word.shape) == word, 1.0, 0.0)
@@ -65,7 +66,7 @@
             terms = []
             for lag in range(width):
                 row = pl.multiple_of((j + rim - lag) * RUNS, RUNS)
-                tap = jnp.broadcast_to(taps[lag, k : k + 1, :], tile)
+                tap = jnp.broadcast_to(taps[k, lag : lag + 1, :], tile)
                 terms.append(tap * streams[k, pl.ds(row, RUNS), :])
             mixed.append(tree_sum(terms))
         row = pl.multiple_of(j * RUNS, RUNS)
@@ -108,38 +109,83 @@
         return state
 
     lax.fori_loop(0, steps, emit, tuple(begins), unroll=8)
-    out[...] = result[...].astype(jnp.bfloat16)
-
-
-def run_operator(ids, table, taps, residue, decay, skip, piece):
-    steps = ids.shape[1]
-    length = steps * RUNS
-    rim = taps.shape[0] - 1
-    part = min(32, steps)
-    chan = lambda *lead: pl.BlockSpec(lead + (LANES,), lambda i: (0,) * len(lead) + (piece,))
+    size = length // len(outs)
+    for d, out in enumerate(outs):
+        first = pl.multiple_of(jnp.bitwise_xor(spot[1], d) * size, size) if len(outs) > 1 else 0
+        out[...] = result[pl.ds(first, size), :].astype(jnp.bfloat16)
+
+
+def run_operator(spot, ids, table, taps, residue, decay, skip, piece, pieces, blocks):
+    length = ids.size
+    rim = taps.shape[1] - 1
+    part = min(32, ids.shape[1])
+    own = lambda *lead: pl.BlockSpec(lead + (LANES,), lambda i, spot: (0,) * len(lead) + (piece,))
+    all_own = lambda *lead: pl.BlockSpec(
+        lead + (LANES,), lambda i, spot: (0,) * len(lead) + (spot[0] * pieces + piece,)
+    )
+    size = length // blocks
     return pl.pallas_call(
         operator,
-        grid=(1,),
-        out_shape=jax.ShapeDtypeStruct((length, LANES), jnp.bfloat16),
-        in_specs=[
-            pl.BlockSpec(ids.shape, lambda i: (0, 0)),
-            chan(*table.shape[:2]),
-            chan(*taps.shape[:2]),
-            chan(residue.shape[0]),
-            chan(decay.shape[0]),
-            chan(1),
-        ],
-        out_specs=pl.BlockSpec((length, LANES), lambda i: (0, 0)),
-        scratch_shapes=[
-            pltpu.VMEM((part * RUNS, table.shape[1]), jnp.bfloat16),
-            pltpu.VMEM((3, length + rim * RUNS, LANES), jnp.float32),
-            pltpu.VMEM((length, LANES), jnp.float32),
-            pltpu.VMEM((length, LANES), jnp.float32),
-            pltpu.VMEM((length, LANES), jnp.float32),
-        ],
+        grid_spec=pltpu.PrefetchScalarGridSpec(
+            num_scalar_prefetch=1,
+            grid=(1,),
+            in_specs=[
+                pl.BlockSpec(ids.shape, lambda i, spot: (0, 0)),
+                own(*table.shape[:2]),
+                all_own(*taps.shape[:2]),
+                all_own(residue.shape[0]),
+                all_own(decay.shape[0]),
+                all_own(1),
+            ],
+            out_specs=[pl.BlockSpec((size, LANES), lambda i, spot: (0, 0))] * blocks,
+            scratch_shapes=[
+                pltpu.VMEM((part * RUNS, table.shape[1]), jnp.bfloat16),
+                pltpu.VMEM((3, length + rim * RUNS, LANES), jnp.float32),
+                pltpu.VMEM((length, LANES), jnp.float32),
+                pltpu.VMEM((length, LANES), jnp.float32),
+                pltpu.VMEM((length, LANES), jnp.float32),
+            ],
+        ),
+        out_shape=[jax.ShapeDtypeStruct((size, LANES), jnp.bfloat16)] * blocks,
         compiler_params=pltpu.CompilerParams(vmem_limit_bytes=56 * 2**20),
         cost_estimate=pl.CostEstimate(flops=length * LANES * 8000, bytes_accessed=4 * 2**20, transcendentals=0),
-    )(ids, table, taps, residue, decay, skip)
+    )(spot, ids, table, taps, residue, decay, skip)
+
+
+def join(spot, *refs):
+    out = refs[-1]
+    last = refs[-2]
+    hops = refs[:-2]
+    places, _, kept = last.shape
+    far = hops[0].shape[0]
+    near = places // far
+    group = (len(hops) // near + 1) * kept
+    for source in range(places):
+        first = source * group + group - kept
+        out[:, first : first + kept] = last[source]
+    for k, hop in enumerate(hops):
+        piece, e = k // near, k % near
+        for d in range(far):
+            source = jnp.bitwise_xor(spot[1], d) * near + jnp.bitwise_xor(spot[2], e)
+            first = pl.multiple_of(source * group + piece * kept, kept)
+            out[:, pl.ds(first, kept)] = hop[d]
+
+
+def spread_far(blocks, far, near, local):
+    kept = blocks[0].shape[1]
+    count = far * near
+    spread = [blocks[0]] + [
+        lax.ppermute(blocks[d], "seq", [(i, i ^ (near * d)) for i in range(count)]) for d in range(1, far)
+    ]
+    return [x.reshape(near, local, kept) for x in spread]
+
+
+def spread_near(spread, near, place, count):
+    hops = []
+    for e in range(near):
+        chosen = jnp.stack([lax.dynamic_index_in_dim(x, (place % near) ^ e, 0, False) for x in spread])
+        hops.append(lax.ppermute(chosen, "seq", [(i, i ^ e) for i in range(count)]) if e else chosen)
+    return hops
 
 
 def body(token_ids, vocab_table, short_filter, residue, decay, skip_gain):
@@ -149,22 +195,46 @@
     local = length // places
     share = vocab_table.shape[2]
     pieces = -(-share // LANES)
-    widen = lambda x: jnp.pad(x, [(0, 0)] * (x.ndim - 1) + [(0, pieces * LANES - share)])
-    mine = lambda x, axis: lax.dynamic_slice_in_dim(x, place * share, share, axis)
-    ids = token_ids.reshape(RUNS, length // RUNS)
-    table = widen(vocab_table.transpose(1, 0, 2))
-    taps = widen(mine(short_filter, 2))
-    res = widen(mine(residue, 0).T)
-    dec = widen(mine(decay, 0).T)
-    skip = widen(mine(skip_gain, 0)[None])
+    near = math.gcd(places, 4)
+    far = places // near
+    ids = token_ids.reshape(-1, min(LANES, length // RUNS))
+    table = vocab_table.transpose(1, 0, 2)
+    rows = [short_filter.transpose(1, 0, 2), residue.T, decay.T, skip_gain[None]]
+    column = place
+    if share % LANES:
+        widen = lambda x: jnp.pad(x, [(0, 0)] * (x.ndim - 1) + [(0, pieces * LANES - share)])
+        rows = [widen(lax.dynamic_slice_in_dim(x, place * share, share, x.ndim - 1)) for x in rows]
+        table = widen(table)
+        column = 0 * place
+    spot = jnp.stack([column, place // near, place % near]).astype(jnp.int32)
+    staged = share % LANES == 0 and far & (far - 1) == 0 and pieces > 1
+    waiting = []
+    hops = []
     parts = []
     for piece in range(pieces):
-        outcome = run_operator(ids, table, taps, res, dec, skip, piece)
+        by_hops = staged and piece < pieces - 1
+        blocks = run_operator(spot, ids, table, *rows, piece, pieces, far if by_hops else 1)
+        if by_hops:
+            *blocks, spot = lax.optimization_barrier((*blocks, spot))
+            waiting.append(spread_far(blocks, far, near, local))
+            continue
         kept = min(LANES, share - piece * LANES)
-        sent = outcome[:, :kept].reshape(places, local, kept)
+        sent = blocks[0][:, :kept].reshape(places, local, kept)
+        if staged:
+            sent, waiting = lax.optimization_barrier((sent, waiting))
         parts.append(lax.all_to_all(sent, "seq", split_axis=0, concat_axis=0, tiled=True))
-    joined = jnp.concatenate(parts, axis=2)
-    return joined.transpose(1, 0, 2).reshape(local, places * share)
+    if not staged:
+        return jnp.concatenate(parts, axis=2).transpose(1, 0, 2).reshape(local, places * share)
+    for spread in waiting:
+        hops += spread_near(spread, near, place, places)
+    whole = pl.BlockSpec(memory_space=pltpu.VMEM)
+    return pl.pallas_call(
+        join,
+        in_specs=[pl.BlockSpec(memory_space=pltpu.SMEM)] + [whole] * (len(hops) + 1),
+        out_specs=whole,
+        out_shape=jax.ShapeDtypeStruct((local, places * share), jnp.bfloat16),
+        compiler_params=pltpu.CompilerParams(vmem_limit_bytes=16 * 2**20),
+    )(spot, *hops, *parts)
 
 
 def solution(mesh):

time: 56.3 us -> 49.7 us (0.88)
  blocking collectives: 18.6 us -> 0 us
  waiting for transfers between devices: 4.87 us -> 12.2 us
  starting transfers between devices: 7.36 us -> 13.9 us
  local copies, waits for them, and re-layouts: 5.68 us -> 0.07 us
  Pallas kernels: 19.2 us -> 22.3 us
  other arithmetic: 0.14 us -> 0.73 us
    all_to_all x1 -> x0, blocking collectives: 18.6 us -> none  [body(): lax.all_to_all(sent, 'seq', split_axis=0, concat_axis=0, tiled=True)]
    ppermute x0 -> x6, waiting for transfers between devices: none -> 10.5 us  [the longest x3 10.3 us: spread_near(): lax.ppermute(chosen, 'seq', [(i, i ^ e) for i in range(count)])]
    ppermute x0 -> x6, starting transfers between devices: none -> 7.88 us  [the longest x3 5.62 us: spread_far(): lax.ppermute(blocks[d], 'seq', [(i, i ^ near * d) for i in range(count)])]
    all_to_all x1, waiting for transfers between devices: 4.87 us -> 1.71 us  [body(): lax.all_to_all(sent, 'seq', split_axis=0, concat_axis=0, tiled=True)]
    pallas_call x2 -> x3, Pallas kernels: 19.2 us -> 22.3 us  [the longest x2 20.5 us: run_operator(): pl.pallas_call(operator, grid_spec=pltpu.PrefetchScalarGridSpec(num_scala...]
    reshape x2 -> x0, local copies, waits for them, and re-layouts: 2.4 us -> none  [the longest x1 1.32 us: body(): ids = token_ids.reshape(RUNS, length // RUNS)]
    transpose x1 -> x0, local copies, waits for them, and re-layouts: 1.34 us -> none  [body(): dec = widen(mine(decay, 0).T)]
    all_to_all x1, starting transfers between devices: 7.36 us -> 6.03 us  [body(): lax.all_to_all(sent, 'seq', split_axis=0, concat_axis=0, tiled=True)]
  transfers between devices with their start and end apart: 1 -> 7, of which waited for: 1 -> 4; matrix products, arithmetic and copies ran while one was open for 0% -> 0% of each run, Pallas kernels for 17% -> 21%
where the time goes in v2:
time: 49.7 us; the launch traced here: 49.4 us
  Pallas kernels  22.3 us (45%)
  starting transfers between devices  13.9 us (28%)
  waiting for transfers between devices  12.2 us (25%)
  other arithmetic  0.73 us (1%)
    pallas_call x2, Pallas kernels, run_operator(): pl.pallas_call(operator, grid_spec=pltpu.PrefetchScalarGridSpec(num_scala...  20.5 us
    ppermute x3, waiting for transfers between devices, spread_near(): lax.ppermute(chosen, 'seq', [(i, i ^ e) for i in range(count)])  10.3 us
    all_to_all x1, starting transfers between devices, body(): lax.all_to_all(sent, 'seq', split_axis=0, concat_axis=0, tiled=True)  6.03 us
    ppermute x3, starting transfers between devices, spread_far(): lax.ppermute(blocks[d], 'seq', [(i, i ^ near * d) for i in range(count)])  5.62 us
    ppermute x3, starting transfers between devices, spread_near(): lax.ppermute(chosen, 'seq', [(i, i ^ e) for i in range(count)])  2.26 us
    pallas_call x1, Pallas kernels, body(): pl.pallas_call(join, in_specs=[pl.BlockSpec(memory_space=pltpu.SMEM)] + [...  1.8 us
    all_to_all x1, waiting for transfers between devices, body(): lax.all_to_all(sent, 'seq', split_axis=0, concat_axis=0, tiled=True)  1.71 us
  transfers between devices with their start and end apart: 7, of which 4 were waited for; matrix products, arithmetic and copies ran while one was open for 0% of the time, Pallas kernels for 21%

profile of v2, /device:TPU:0, one launch (start us, length us, event | category | flops | bytes accessed | tf_op | source)
XLA Modules:
  0.0 49.4 jit_solution(9302461351565297876)
XLA Ops:
  0.0 0.6 %pad_add_fusion.spot = s32[3]{0:T(128)} fusion(s32[1]{0:T(128)} %bitcast.2, s32[1]{0:T(128)} %bitcast.1, s32[1]{0:T(128)} %bitcast), kind=kLoop, calls=%fused_computation.20 | loop fusion | flops 6 | bytes 24 | tf_op jit(solution)/shard_map/stack | solution.py:209
  0.7 10.3 %shard_map.64 = (bf16[512,128]{1,0:T(8,128)(2,1)}, bf16[512,128]{1,0:T(8,128)(2,1)}, bf16[512,128]{1,0:T(8,128)(2,1)}, bf16[512,128]{1,0:T(8,128)(2,1)}) custom-call(s32[3]{0:T(128)} %pad_add_fusion.spot, s32[16,128]{1,0:T(8,128)} %bitcast.29, bf16[3,512,256]{2,1,0:T(8,128)(2,1)} %bitcast.19, f32[3,7,4096]{2,1,0:T(8,128)} %bitcast.21, f32[16,4096]{1,0:T(8,128)} %bitcast.23, ...), custom_call_target="tpu_custom_call" | custom-call | flops 2097152000 | bytes 4194304 | tf_op jit(solution)/shard_map/pallas_call | solution.py:127
  10.9 3.0 %collective-permute-start = (bf16[512,128]{1,0:T(8,128)(2,1)}, bf16[512,128]{1,0:T(8,128)(2,1)S(1)}, u32[]{:S(2)}, u32[]{:S(2)}) collective-permute-start(bf16[512,128]{1,0:T(8,128)(2,1)} %get-tuple-element.25), channel_id=1, source_target_pairs={{0,4},{1,5},{2,6},{3,7},{4,0},{5,1},{6,2},{7,3},{8,12},{9,13},{10,... | collective-permute-start | bytes 393224 | tf_op jit(solution)/shard_map/ppermute | solution.py:178
  14.0 2.6 %collective-permute-start.1 = (bf16[512,128]{1,0:T(8,128)(2,1)}, bf16[512,128]{1,0:T(8,128)(2,1)S(1)}, u32[]{:S(2)}, u32[]{:S(2)}) collective-permute-start(bf16[512,128]{1,0:T(8,128)(2,1)} %get-tuple-element.26), channel_id=1, source_target_pairs={{0,8},{1,9},{2,10},{3,11},{4,12},{5,13},{6,14},{7,15},{8,0},{9,1},... | collective-permute-start | bytes 393224 | tf_op jit(solution)/shard_map/ppermute | solution.py:178
  16.5 0.0 collective-permute-start.2
  16.5 10.3 %shard_map.65 = bf16[2048,128]{1,0:T(8,128)(2,1)} custom-call(s32[3]{0:T(128)} %pad_add_fusion.spot, s32[16,128]{1,0:T(8,128)} %bitcast.30, bf16[3,512,256]{2,1,0:T(8,128)(2,1)} %bitcast.20, f32[3,7,4096]{2,1,0:T(8,128)} %bitcast.22, f32[16,4096]{1,0:T(8,128)} %bitcast.24, f32[16,4096]{1,0:T(8,128)} %bitcast.26, f32[1,4096]{1,0:T(1,128)} %bitcast.28), custom_call_target="tpu_custom_call" | custom-call | flops 2097152000 | bytes 4194304 | tf_op jit(solution)/shard_map/pallas_call | solution.py:127
  26.8 0.0 collective-permute-done
  26.8 0.3 collective-permute-done.1
  27.1 0.0 collective-permute-done.2
  27.1 0.0 copy-start.1
  27.1 6.0 %all-to-all-start = ((bf16[16,128,128]{2,1,0:T(8,128)(2,1)}), bf16[16,128,128]{2,1,0:T(8,128)(2,1)S(1)}, u32[]{:S(2)}, u32[]{:S(2)}) async-start(bf16[16,128,128]{2,1,0:T(8,128)(2,1)} %bitcast.14), calls=%async_computation | async-start | bytes 1048576 | tf_op jit(solution)/shard_map/all_to_all | solution.py:225
  33.2 0.0 copy-done.1
  33.3 0.4 collective-permute-start.3
  33.7 1.7 %collective-permute-start.4 = (bf16[4,128,128]{2,1,0:T(8,128)(2,1)S(1)}, bf16[4,128,128]{2,1,0:T(8,128)(2,1)S(1)}, u32[]{:S(2)}, u32[]{:S(2)}) collective-permute-start(bf16[4,128,128]{2,1,0:T(8,128)(2,1)S(1)} %pad_maximum_fusion.2), channel_id=1, source_target_pairs={{0,2},{1,3},{2,0},{3,1},{4,6},{5,7},{6,4},{7,5},{8,10},{9,11},{10,... | collective-permute-start | bytes 393224 | tf_op jit(solution)/shard_map/ppermute | solution.py:187
  35.5 0.1 collective-permute-start.5
  35.6 0.0 copy-start
  35.6 0.0 collective-permute-done.3.refs_1_
  35.6 8.2 %collective-permute-done.4.refs_2_ = bf16[4,128,128]{2,1,0:T(8,128)(2,1)S(1)} collective-permute-done((bf16[4,128,128]{2,1,0:T(8,128)(2,1)S(1)}, bf16[4,128,128]{2,1,0:T(8,128)(2,1)S(1)}, u32[]{:S(2)}, u32[]{:S(2)}) %collective-permute-start.4) | collective-permute-done | bytes 131104 | tf_op jit(solution)/shard_map/ppermute | solution.py:187
  43.8 2.1 %collective-permute-done.5.refs_3_ = bf16[4,128,128]{2,1,0:T(8,128)(2,1)S(1)} collective-permute-done((bf16[4,128,128]{2,1,0:T(8,128)(2,1)S(1)}, bf16[4,128,128]{2,1,0:T(8,128)(2,1)S(1)}, u32[]{:S(2)}, u32[]{:S(2)}) %collective-permute-start.5) | collective-permute-done | bytes 131104 | tf_op jit(solution)/shard_map/ppermute | solution.py:187
  45.9 1.7 %all-to-all-done.refs_4_ = bf16[16,128,128]{2,1,0:T(8,128)(2,1)S(1)} async-done(((bf16[16,128,128]{2,1,0:T(8,128)(2,1)}), bf16[16,128,128]{2,1,0:T(8,128)(2,1)S(1)}, u32[]{:S(2)}, u32[]{:S(2)}) %all-to-all-start) | async-done | bytes 524320 | tf_op jit(solution)/shard_map/all_to_all | solution.py:225
  47.6 0.0 copy-done
  47.6 1.8 %shard_map.66 = bf16[128,4096]{1,0:T(8,128)(2,1)} custom-call(s32[3]{0:T(128)S(1)} %copy-done, bf16[4,128,128]{2,1,0:T(8,128)(2,1)S(1)} %pad_maximum_fusion.refs_0_, bf16[4,128,128]{2,1,0:T(8,128)(2,1)S(1)} %collective-permute-done.3.refs_1_, bf16[4,128,128]{2,1,0:T(8,128)(2,1)S(1)} %collective-permute-done.4.refs_2_, ...), custom_call_target="tpu_custom_call" | custom-call | tf_op jit(solution)/shard_map/pallas_call | solution.py:231
  (6 shorter events, 0.1 us)
Async XLA Ops:
  10.9 15.9 %collective-permute-start = (bf16[512,128]{1,0:T(8,128)(2,1)}, bf16[512,128]{1,0:T(8,128)(2,1)S(1)}, u32[]{:S(2)}, u32[]{:S(2)}) collective-permute-start(bf16[512,128]{1,0:T(8,128)(2,1)} %get-tuple-element.25), channel_id=1, source_target_pairs={{0,4},{1,5},{2,6},{3,7},{4,0},{5,1},{6,2},{7,3},{8,12},{9,13},{10,... | collective-permute-start | bytes 393224 | tf_op jit(solution)/shard_map/ppermute | solution.py:178
  14.0 13.1 %collective-permute-start.1 = (bf16[512,128]{1,0:T(8,128)(2,1)}, bf16[512,128]{1,0:T(8,128)(2,1)S(1)}, u32[]{:S(2)}, u32[]{:S(2)}) collective-permute-start(bf16[512,128]{1,0:T(8,128)(2,1)} %get-tuple-element.26), channel_id=1, source_target_pairs={{0,8},{1,9},{2,10},{3,11},{4,12},{5,13},{6,14},{7,15},{8,0},{9,1},... | collective-permute-start | bytes 393224 | tf_op jit(solution)/shard_map/ppermute | solution.py:178
  16.5 10.5 %collective-permute-start.2 = (bf16[512,128]{1,0:T(8,128)(2,1)}, bf16[512,128]{1,0:T(8,128)(2,1)S(1)}, u32[]{:S(2)}, u32[]{:S(2)}) collective-permute-start(bf16[512,128]{1,0:T(8,128)(2,1)} %get-tuple-element.27), channel_id=1, source_target_pairs={{0,12},{1,13},{2,14},{3,15},{4,8},{5,9},{6,10},{7,11},{8,4},{9,5},... | collective-permute-start | bytes 393224 | tf_op jit(solution)/shard_map/ppermute | solution.py:178
  27.1 6.1 %copy-start.1 = (bf16[512,128]{1,0:T(8,128)(2,1)S(1)}, bf16[512,128]{1,0:T(8,128)(2,1)}, u32[]{:S(2)}) copy-start(bf16[512,128]{1,0:T(8,128)(2,1)} %get-tuple-element.24) | copy-start | bytes 393220
  27.1 20.5 %all-to-all-start = ((bf16[16,128,128]{2,1,0:T(8,128)(2,1)}), bf16[16,128,128]{2,1,0:T(8,128)(2,1)S(1)}, u32[]{:S(2)}, u32[]{:S(2)}) async-start(bf16[16,128,128]{2,1,0:T(8,128)(2,1)} %bitcast.14), calls=%async_computation | async-start | bytes 1048576 | tf_op jit(solution)/shard_map/all_to_all | solution.py:225
  33.3 2.4 %collective-permute-start.3 = (bf16[4,128,128]{2,1,0:T(8,128)(2,1)S(1)}, bf16[4,128,128]{2,1,0:T(8,128)(2,1)S(1)}, u32[]{:S(2)}, u32[]{:S(2)}) collective-permute-start(bf16[4,128,128]{2,1,0:T(8,128)(2,1)S(1)} %pad_maximum_fusion.1), channel_id=1, source_target_pairs={{0,1},{1,0},{2,3},{3,2},{4,5},{5,4},{6,7},{7,6},{8,9},{9,8},{10,11... | collective-permute-start | bytes 393224 | tf_op jit(solution)/shard_map/ppermute | solution.py:187
  33.7 10.1 %collective-permute-start.4 = (bf16[4,128,128]{2,1,0:T(8,128)(2,1)S(1)}, bf16[4,128,128]{2,1,0:T(8,128)(2,1)S(1)}, u32[]{:S(2)}, u32[]{:S(2)}) collective-permute-start(bf16[4,128,128]{2,1,0:T(8,128)(2,1)S(1)} %pad_maximum_fusion.2), channel_id=1, source_target_pairs={{0,2},{1,3},{2,0},{3,1},{4,6},{5,7},{6,4},{7,5},{8,10},{9,11},{10,... | collective-permute-start | bytes 393224 | tf_op jit(solution)/shard_map/ppermute | solution.py:187
  35.5 10.4 %collective-permute-start.5 = (bf16[4,128,128]{2,1,0:T(8,128)(2,1)S(1)}, bf16[4,128,128]{2,1,0:T(8,128)(2,1)S(1)}, u32[]{:S(2)}, u32[]{:S(2)}) collective-permute-start(bf16[4,128,128]{2,1,0:T(8,128)(2,1)S(1)} %pad_maximum_fusion.3), channel_id=1, source_target_pairs={{0,3},{1,2},{2,1},{3,0},{4,7},{5,6},{6,5},{7,4},{8,11},{9,10},{10,... | collective-permute-start | bytes 393224 | tf_op jit(solution)/shard_map/ppermute | solution.py:187
  35.6 12.0 %copy-start = (s32[3]{0:T(128)S(1)}, s32[3]{0:T(128)}, u32[]{:S(2)}) copy-start(s32[3]{0:T(128)} %pad_add_fusion.spot) | copy-start | bytes 40

commit v3 on v2

v3 whole, which is shorter than its diff:
```python
import functools
import math

import jax
import jax.numpy as jnp
from jax import lax
from jax.experimental import pallas as pl
from jax.experimental.pallas import tpu as pltpu
from jax.sharding import PartitionSpec as P

LANES = 128
RUNS = 8


def tree_sum(terms):
    while len(terms) > 1:
        pairs = [a + b for a, b in zip(terms[::2], terms[1::2])]
        terms = pairs + ([terms[-1]] if len(terms) % 2 else [])
    return terms[0]


def delay_runs(value, by):
    moved = pltpu.roll(value, by, 0)
    return jnp.where(lax.broadcasted_iota(jnp.int32, value.shape, 0) < by, 0.0, moved)


def operator(spot, *refs):
    piece, pieces, near, sliced, blocks, raw, ahead = spot
    place = lax.axis_index("seq")
    refs = list(refs)
    take = lambda count: [refs.pop(0) for _ in range(count)]
    given, outs = take(6), take(blocks)
    ahead = take(6) if ahead else []
    if raw:
        held, sem = take(6), take(1)[0]

        def bring(first, into, which):
            column = first * LANES if sliced else (place * pieces + first) * LANES
            own = pl.ds(pl.multiple_of(column, LANES), LANES)
            ids, table, taps, residue, decay, skip = given
            pairs = [(ids, into[0])]
            for k in range(3):
                pairs.append((table.at[k, :, pl.ds(first * LANES, LANES)], into[1].at[:, pl.ds(k * LANES, LANES)]))
            pairs.append((taps.at[:, :, own], into[2]))
            for ref, target in zip((residue, decay, skip), into[3:]):
                pairs.append((ref.at[:, own], target))
            return [pltpu.make_async_copy(x, y, sem.at[which, n]) for n, (x, y) in enumerate(pairs)]

        now = bring(piece, held, 0)
        later = bring(piece + 1, ahead, 1) if ahead else []
        for copy in now + later:
            copy.start()
        for copy in now:
            copy.wait()
    else:
        held, later = given, []
    compute(place // near, held, outs, *refs)
    for copy in later:
        copy.wait()


def compute(far_place, held, outs, halo, query, gated, inputs, factors, result, *streams):
    ids, table, taps, residue, decay, skip = held
    length = ids.shape[0] * ids.shape[1]
    steps = length // RUNS
    vocab = table.shape[0]
    width = taps.shape[1]
    modes = residue.shape[0]
    rim = width - 1
    tile = (RUNS, LANES)
    spread = lambda row: jnp.broadcast_to(row, tile)

    cols = ids.shape[1]
    part = cols // len(streams)
    word = lax.broadcasted_iota(jnp.int32, (RUNS, vocab), 1)

    def look_up(here, first, count):
        hot = [
            jnp.where(jnp.broadcast_to(here[:, j : j + 1], word.shape) == word, 1.0, 0.0)
            for j in range(first, first + count)
        ]
        hot = jnp.concatenate(hot, axis=0).astype(jnp.bfloat16)
        found = jnp.dot(hot, table[...], preferred_element_type=jnp.float32)
        return [found[:, k * LANES : (k + 1) * LANES] for k in range(3)]

    def ids_of(block):
        return ids[pl.ds(block, RUNS, stride=steps // cols), :]

    tail = look_up(ids_of(steps // cols - 1), cols - rim, rim)
    for k in range(3):
        for j in range(rim):
            rows = slice(j * RUNS, (j + 1) * RUNS)
            halo[k, rows, :] = delay_runs(tail[k][rows], 1)

    filters = [[spread(taps[k, lag : lag + 1, :]) for lag in range(width)] for k in range(3)]

    def block_step(block, _):
        here = ids_of(block)
        seen = {}

        def row(k, j):
            if (k, j) not in seen:
                if j < 0:
                    seen[k, j] = halo[k, (rim + j) * RUNS : (rim + j + 1) * RUNS, :]
                else:
                    first = j % part * RUNS
                    seen[k, j] = streams[j // part][k, first : first + RUNS, :]
            return seen[k, j]

        def mix(first):
            for j in range(first, first + part):
                mixed = [
                    tree_sum([filters[k][lag] * row(k, j - lag) for lag in range(width)]) for k in range(3)
                ]
                at = pl.ds(pl.multiple_of((block * cols + j) * RUNS, RUNS), RUNS)
                query[at, :] = mixed[0]
                gated[at, :] = mixed[1] * mixed[2]

        for n, stream in enumerate(streams):
            for k, found in enumerate(look_up(here, n * part, part)):
                stream[k] = found
            if n > 0:
                mix((n - 1) * part)
        mix(cols - part)
        for k in range(3):
            halo[k] = streams[-1][k, (part - rim) * RUNS :, :]
        return 0

    lax.fori_loop(0, steps // cols, block_step, 0)

    batch = factors.shape[0] // modes
    rate = decay[...] / length
    weight = residue[...] * jnp.sqrt(2.0 * rate)
    pole = jnp.exp(-rate)
    power = weight
    early = []
    for n in range(batch):
        early.append(spread(jnp.sum(power, axis=0, keepdims=True)))
        power = weight * jnp.exp(-rate * (n + 1))
        for s in range(modes):
            factors[n * modes + s] = spread(power[s : s + 1])
    early[0] = early[0] + spread(skip[...])
    poles = [spread(pole[s : s + 1]) for s in range(modes)]
    leap = jnp.exp(-rate * batch)
    leaps = [spread(leap[s : s + 1]) for s in range(modes)]

    def tokens(ref, m):
        first = m * batch
        return [ref[pl.ds(pl.multiple_of((first + n) * RUNS, RUNS), RUNS), :] for n in range(batch)]

    def advance(m, state):
        values = tokens(gated, m)
        after = []
        for s in range(modes):
            taken = values[0]
            for value in values[1:]:
                taken = poles[s] * taken + value
            inputs[s, pl.ds(pl.multiple_of(m * RUNS, RUNS), RUNS), :] = taken
            after.append(leaps[s] * state[s] + taken)
        return tuple(after)

    zero = jnp.zeros(tile, jnp.float32)
    ends = lax.fori_loop(0, steps // batch, advance, (zero,) * modes, unroll=4)
    begins = []
    for s in range(modes):
        value = delay_runs(ends[s], 1)
        by = 1
        while by < RUNS:
            value = value + spread(jnp.exp(-rate[s : s + 1] * (steps * by))) * delay_runs(value, by)
            by *= 2
        begins.append(value)

    def emit(m, state):
        values = tokens(gated, m)
        for n, asked in enumerate(tokens(query, m)):
            terms = [early[lag] * values[n - lag] for lag in range(n + 1)]
            terms += [factors[n * modes + s] * state[s] for s in range(modes)]
            result[pl.ds(m * batch + n, RUNS, stride=steps), :] = asked * tree_sum(terms)
        at = pl.ds(pl.multiple_of(m * RUNS, RUNS), RUNS)
        return tuple(leaps[s] * state[s] + inputs[s, at, :] for s in range(modes))

    lax.fori_loop(0, steps // batch, emit, tuple(begins), unroll=4)
    size = length // len(outs)
    for d, out in enumerate(outs):
        first = pl.multiple_of(jnp.bitwise_xor(far_place, d) * size, size) if len(outs) > 1 else 0
        out[...] = result[pl.ds(first, size), :].astype(jnp.bfloat16)


def run_operator(given, piece, pieces, near, sliced, blocks):
    ids, table, taps, residue = given[:4]
    raw = piece == 0 or pieces > 2
    ahead = piece == 0 and pieces == 2
    vocab, modes, width = table.shape[-2], residue.shape[0], taps.shape[1]
    length = ids.size
    steps = length // RUNS
    cols = ids.shape[1]
    parts = max(cols // 32, 1)
    batch = max(4, steps // 128)
    inside = pl.BlockSpec(memory_space=pltpu.VMEM)
    outside = pl.BlockSpec(memory_space=pl.ANY)
    floats = lambda *shape: pltpu.VMEM(shape + (LANES,), jnp.float32)
    own = [
        jax.ShapeDtypeStruct(ids.shape, jnp.int32),
        jax.ShapeDtypeStruct((vocab, 3 * LANES), jnp.bfloat16),
        jax.ShapeDtypeStruct((3, width, LANES), jnp.float32),
        jax.ShapeDtypeStruct((modes, LANES), jnp.float32),
        jax.ShapeDtypeStruct((modes, LANES), jnp.float32),
        jax.ShapeDtypeStruct((1, LANES), jnp.float32),
    ]
    out_shape = [jax.ShapeDtypeStruct((length // blocks, LANES), jnp.bfloat16)] * blocks
    scratch = []
    if raw:
        scratch = [pltpu.VMEM(x.shape, x.dtype) for x in own] + [pltpu.SemaphoreType.DMA((2, 8))]
        out_shape = out_shape + (own if ahead else [])
    results = pl.pallas_call(
        functools.partial(operator, (piece, pieces, near, sliced, blocks, raw, ahead)),
        in_specs=[outside if raw else inside] * 6,
        out_specs=[inside] * len(out_shape),
        out_shape=out_shape,
        scratch_shapes=scratch
        + [
            floats(3, (width - 1) * RUNS),
            floats(length),
            floats(length),
            floats(modes, steps // batch * RUNS),
            floats(batch * modes, RUNS),
            floats(length),
        ]
        + [floats(3, cols // parts * RUNS)] * parts,
        compiler_params=pltpu.CompilerParams(vmem_limit_bytes=56 * 2**20),
        cost_estimate=pl.CostEstimate(flops=length * LANES * 8000, bytes_accessed=4 * 2**20, transcendentals=0),
    )(*given)
    return results[:blocks], results[blocks:]


def join(piece, pieces, *refs):
    refs, out, sem = refs[:-2], refs[-2], refs[-1]
    place = lax.axis_index("seq")
    copies = []
    kept = refs[0].shape[-1]
    for e, ref in enumerate(refs):
        for d in range(ref.shape[0]):
            source = d if piece == pieces - 1 else jnp.bitwise_xor(place, d * len(refs) + e)
            first = pl.multiple_of((source * pieces + piece) * kept, kept)
            copies.append(pltpu.make_async_copy(ref.at[d], out.at[:, pl.ds(first, kept)], sem.at[len(copies)]))
    for copy in copies:
        copy.start()
    for copy in copies:
        copy.wait()


def run_join(piece, pieces, blocks, out):
    count = sum(x.shape[0] for x in blocks)
    inside = pl.BlockSpec(memory_space=pltpu.VMEM)
    outside = pl.BlockSpec(memory_space=pl.ANY)
    into = [] if out is None else [out]

    def kernel(*refs):
        refs = list(refs)
        if into:
            refs.pop(len(blocks))
        join(piece, pieces, *refs)

    local, kept = blocks[0].shape[1:]
    return pl.pallas_call(
        kernel,
        in_specs=[inside] * len(blocks) + [outside] * len(into),
        out_specs=outside,
        out_shape=jax.ShapeDtypeStruct((local, count * pieces * kept), blocks[0].dtype),
        scratch_shapes=[pltpu.SemaphoreType.DMA((count,))],
        input_output_aliases={len(blocks): 0} if into else {},
        compiler_params=pltpu.CompilerParams(vmem_limit_bytes=2**20),
    )(*blocks, *into)


def spread_far(blocks, far, near, local):
    kept = blocks[0].shape[1]
    count = far * near
    spread = [blocks[0]] + [
        lax.ppermute(blocks[d], "seq", [(i, i ^ (near * d)) for i in range(count)]) for d in range(1, far)
    ]
    return [x.reshape(near, local, kept) for x in spread]


def spread_near(spread, near, place, count):
    hops = []
    for e in range(near):
        chosen = jnp.stack([lax.dynamic_index_in_dim(x, (place % near) ^ e, 0, False) for x in spread])
        hops.append(lax.ppermute(chosen, "seq", [(i, i ^ e) for i in range(count)]) if e else chosen)
    return hops


def body(token_ids, vocab_table, short_filter, residue, decay, skip_gain):
    places = lax.axis_size("seq")
    place = lax.axis_index("seq")
    length = token_ids.shape[0]
    local = length // places
    share = vocab_table.shape[2]
    pieces = -(-share // LANES)
    near = math.gcd(places, 4)
    far = places // near
    ids = token_ids.reshape(-1, min(LANES, length // RUNS))
    table = vocab_table.transpose(1, 0, 2)
    rows = [short_filter.transpose(1, 0, 2), residue.T, decay.T, skip_gain[None]]
    sliced = share % LANES != 0
    if sliced:
        widen = lambda x: jnp.pad(x, [(0, 0)] * (x.ndim - 1) + [(0, pieces * LANES - share)])
        rows = [widen(lax.dynamic_slice_in_dim(x, place * share, share, x.ndim - 1)) for x in rows]
        table = widen(table)
    staged = not sliced and far & (far - 1) == 0 and pieces > 1
    given = (ids, table, *rows)
    waiting = []
    parts = []
    for piece in range(pieces):
        by_hops = staged and piece < pieces - 1
        blocks, ahead = run_operator(given, piece, pieces, near, sliced, far if by_hops else 1)
        given = ahead or given
        if by_hops:
            waiting.append(spread_far(blocks, far, near, local))
            continue
        kept = min(LANES, share - piece * LANES)
        sent = blocks[0][:, :kept].reshape(places, local, kept)
        if staged:
            sent, waiting = lax.optimization_barrier((sent, waiting))
        parts.append(lax.all_to_all(sent, "seq", split_axis=0, concat_axis=0, tiled=True))
    if not staged:
        return jnp.concatenate(parts, axis=2).transpose(1, 0, 2).reshape(local, places * share)
    out = None
    for piece, spread in enumerate(waiting):
        out = run_join(piece, pieces, spread_near(spread, near, place, places), out)
    return run_join(pieces - 1, pieces, parts, out)


def solution(mesh):
    placed = (P("groups"), P(None, None, "seq"), P(), P(), P(), P())
    return jax.shard_map(
        body, mesh=mesh, in_specs=placed, out_specs=P(("groups", "seq"), None), check_vma=False
    )
```

time: 49.7 us -> 45.7 us (0.920)
  Pallas kernels: 22.3 us -> 18.4 us
  waiting for transfers between devices: 12.2 us -> 13.4 us
  other arithmetic: 0.73 us -> 0.08 us
  starting transfers between devices: 13.9 us -> 13.3 us
    pallas_call x3 -> x4, Pallas kernels: 22.3 us -> 18.4 us  [the longest x2 16.5 us: run_operator(): pl.pallas_call(functools.partial(operator, (piece, pieces, near, sliced,...]
    ppermute x3, waiting for transfers between devices: 0.28 us -> 2.38 us  [spread_far(): lax.ppermute(blocks[d], 'seq', [(i, i ^ near * d) for i in range(count)])]
    all_to_all x1, waiting for transfers between devices: 1.71 us -> 0.78 us  [body(): lax.all_to_all(sent, 'seq', split_axis=0, concat_axis=0, tiled=True)]
    another operation x1 -> x0, other arithmetic: 0.65 us -> none  [body(): spot = jnp.stack([column, place // near, place % near]).astype(jnp.int32)]
    all_to_all x1, starting transfers between devices: 6.03 us -> 5.41 us  [body(): lax.all_to_all(sent, 'seq', split_axis=0, concat_axis=0, tiled=True)]
  transfers between devices with their start and end apart: 7 -> 7, of which waited for: 4 -> 4; matrix products, arithmetic and copies ran while one was open for 0% -> 0% of each run, Pallas kernels for 21% -> 20%
where the time goes in v3:
time: 45.7 us; the launch traced here: 45.4 us
  Pallas kernels  18.4 us (40%)
  waiting for transfers between devices  13.4 us (29%)
  starting transfers between devices  13.3 us (29%)
    pallas_call x2, Pallas kernels, run_operator(): pl.pallas_call(functools.partial(operator, (piece, pieces, near, sliced,...  16.5 us
    ppermute x3, waiting for transfers between devices, spread_near(): lax.ppermute(chosen, 'seq', [(i, i ^ e) for i in range(count)])  10.3 us
    ppermute x3, starting transfers between devices, spread_far(): lax.ppermute(blocks[d], 'seq', [(i, i ^ near * d) for i in range(count)])  5.68 us
    all_to_all x1, starting transfers between devices, body(): lax.all_to_all(sent, 'seq', split_axis=0, concat_axis=0, tiled=True)  5.41 us
    ppermute x3, waiting for transfers between devices, spread_far(): lax.ppermute(blocks[d], 'seq', [(i, i ^ near * d) for i in range(count)])  2.38 us
    ppermute x3, starting transfers between devices, spread_near(): lax.ppermute(chosen, 'seq', [(i, i ^ e) for i in range(count)])  2.25 us
    pallas_call x2, Pallas kernels, run_join(): pl.pallas_call(kernel, in_specs=[inside] * len(blocks) + [outside] * len(...  1.83 us
  transfers between devices with their start and end apart: 7, of which 4 were waited for; matrix products, arithmetic and copies ran while one was open for 0% of the time, Pallas kernels for 20%

profile of v3, /device:TPU:0, one launch (start us, length us, event | category | flops | bytes accessed | tf_op | source)
XLA Modules:
  0.0 45.4 jit_solution(1464539556302526395)
XLA Ops:
  0.0 8.4 %shard_map.64 = (bf16[512,128]{1,0:T(8,128)(2,1)}, bf16[512,128]{1,0:T(8,128)(2,1)}, bf16[512,128]{1,0:T(8,128)(2,1)}, bf16[512,128]{1,0:T(8,128)(2,1)}, s32[16,...) custom-call(s32[16,128]{1,0:T(8,128)} %bitcast.21, ...), custom_call_target="tpu_custom_call" | custom-call | flops 2097152000 | bytes 4194304 | tf_op jit(solution)/shard_map/pallas_call | solution.py:215
  8.4 3.1 %collective-permute-start = (bf16[512,128]{1,0:T(8,128)(2,1)}, bf16[512,128]{1,0:T(8,128)(2,1)S(1)}, u32[]{:S(2)}, u32[]{:S(2)}) collective-permute-start(bf16[512,128]{1,0:T(8,128)(2,1)} %get-tuple-element.27), channel_id=1, source_target_pairs={{0,4},{1,5},{2,6},{3,7},{4,0},{5,1},{6,2},{7,3},{8,12},{9,13},{10,... | collective-permute-start | bytes 393224 | tf_op jit(solution)/shard_map/ppermute | solution.py:280
  11.5 2.6 %collective-permute-start.1 = (bf16[512,128]{1,0:T(8,128)(2,1)}, bf16[512,128]{1,0:T(8,128)(2,1)S(1)}, u32[]{:S(2)}, u32[]{:S(2)}) collective-permute-start(bf16[512,128]{1,0:T(8,128)(2,1)} %get-tuple-element.28), channel_id=1, source_target_pairs={{0,8},{1,9},{2,10},{3,11},{4,12},{5,13},{6,14},{7,15},{8,0},{9,1},... | collective-permute-start | bytes 393224 | tf_op jit(solution)/shard_map/ppermute | solution.py:280
  14.0 0.0 collective-permute-start.2
  14.0 8.2 %shard_map.65 = bf16[2048,128]{1,0:T(8,128)(2,1)} custom-call(s32[16,128]{1,0:T(8,128)} %get-tuple-element.20.refs_0_, bf16[512,384]{1,0:T(8,128)(2,1)} %get-tuple-element.21.refs_1_, f32[3,7,128]{2,1,0:T(8,128)} %get-tuple-element.22.refs_2_, f32[16,128]{1,0:T(8,128)} %get-tuple-element.23.refs_3_, f32[16,128]{1,0:T(8,128)} %get-tuple-element.24.refs_4_, ...), custom_call_target="tpu_custom_call" | custom-call | flops 2097152000 | bytes 4194304 | tf_op jit(solution)/shard_map/pallas_call | solution.py:215
  22.2 0.0 collective-permute-done
  22.2 2.4 %collective-permute-done.1 = bf16[512,128]{1,0:T(8,128)(2,1)S(1)} collective-permute-done((bf16[512,128]{1,0:T(8,128)(2,1)}, bf16[512,128]{1,0:T(8,128)(2,1)S(1)}, u32[]{:S(2)}, u32[]{:S(2)}) %collective-permute-start.1) | collective-permute-done | bytes 131104 | tf_op jit(solution)/shard_map/ppermute | solution.py:280
  24.6 0.0 collective-permute-done.2
  24.6 0.0 copy-start
  24.6 5.4 %all-to-all-start = ((bf16[16,128,128]{2,1,0:T(8,128)(2,1)}), bf16[16,128,128]{2,1,0:T(8,128)(2,1)S(1)}, u32[]{:S(2)}, u32[]{:S(2)}) async-start(bf16[16,128,128]{2,1,0:T(8,128)(2,1)} %bitcast.11), calls=%async_computation | async-start | bytes 1048576 | tf_op jit(solution)/shard_map/all_to_all | solution.py:325
  30.1 0.0 copy-done
  30.2 0.4 collective-permute-start.3
  30.6 1.7 %collective-permute-start.4 = (bf16[4,128,128]{2,1,0:T(8,128)(2,1)S(1)}, bf16[4,128,128]{2,1,0:T(8,128)(2,1)S(1)}, u32[]{:S(2)}, u32[]{:S(2)}) collective-permute-start(bf16[4,128,128]{2,1,0:T(8,128)(2,1)S(1)} %pad_maximum_fusion.2), channel_id=1, source_target_pairs={{0,2},{1,3},{2,0},{3,1},{4,6},{5,7},{6,4},{7,5},{8,10},{9,11},{10,... | collective-permute-start | bytes 393224 | tf_op jit(solution)/shard_map/ppermute | solution.py:289
  32.4 0.1 collective-permute-start.5
  32.5 0.0 collective-permute-done.3.refs_1_
  32.5 8.2 %collective-permute-done.4.refs_2_ = bf16[4,128,128]{2,1,0:T(8,128)(2,1)S(1)} collective-permute-done((bf16[4,128,128]{2,1,0:T(8,128)(2,1)S(1)}, bf16[4,128,128]{2,1,0:T(8,128)(2,1)S(1)}, u32[]{:S(2)}, u32[]{:S(2)}) %collective-permute-start.4) | collective-permute-done | bytes 131104 | tf_op jit(solution)/shard_map/ppermute | solution.py:289
  40.7 2.1 %collective-permute-done.5.refs_3_ = bf16[4,128,128]{2,1,0:T(8,128)(2,1)S(1)} collective-permute-done((bf16[4,128,128]{2,1,0:T(8,128)(2,1)S(1)}, bf16[4,128,128]{2,1,0:T(8,128)(2,1)S(1)}, u32[]{:S(2)}, u32[]{:S(2)}) %collective-permute-start.5) | collective-permute-done | bytes 131104 | tf_op jit(solution)/shard_map/ppermute | solution.py:289
  42.8 0.9 %shard_map.66.refs_1_ = bf16[128,4096]{1,0:T(8,128)(2,1)} custom-call(bf16[4,128,128]{2,1,0:T(8,128)(2,1)S(1)} %pad_maximum_fusion.refs_0_, bf16[4,128,128]{2,1,0:T(8,128)(2,1)S(1)} %collective-permute-done.3.refs_1_, bf16[4,128,128]{2,1,0:T(8,128)(2,1)S(1)} %collective-permute-done.4.refs_2_, bf16[4,128,128]{2,1,0:T(8,128)(2,1)S(1)} %collective-permute-done.5.refs_3_), custom_call_target="tpu_custom_call" | custom-call | tf_op jit(solution)/shard_map/pallas_call | solution.py:265
  43.7 0.8 %all-to-all-done.refs_0_ = bf16[16,128,128]{2,1,0:T(8,128)(2,1)S(1)} async-done(((bf16[16,128,128]{2,1,0:T(8,128)(2,1)}), bf16[16,128,128]{2,1,0:T(8,128)(2,1)S(1)}, u32[]{:S(2)}, u32[]{:S(2)}) %all-to-all-start) | async-done | bytes 524320 | tf_op jit(solution)/shard_map/all_to_all | solution.py:325
  44.5 0.9 %shard_map.67 = bf16[128,4096]{1,0:T(8,128)(2,1)} custom-call(bf16[16,128,128]{2,1,0:T(8,128)(2,1)S(1)} %all-to-all-done.refs_0_, bf16[128,4096]{1,0:T(8,128)(2,1)} %shard_map.66.refs_1_), custom_call_target="tpu_custom_call", output_to_operand_aliasing={{}: (1, {})} | custom-call | tf_op jit(solution)/shard_map/pallas_call | solution.py:265
  (6 shorter events, 0.1 us)
Async XLA Ops:
  8.4 13.9 %collective-permute-start = (bf16[512,128]{1,0:T(8,128)(2,1)}, bf16[512,128]{1,0:T(8,128)(2,1)S(1)}, u32[]{:S(2)}, u32[]{:S(2)}) collective-permute-start(bf16[512,128]{1,0:T(8,128)(2,1)} %get-tuple-element.27), channel_id=1, source_target_pairs={{0,4},{1,5},{2,6},{3,7},{4,0},{5,1},{6,2},{7,3},{8,12},{9,13},{10,... | collective-permute-start | bytes 393224 | tf_op jit(solution)/shard_map/ppermute | solution.py:280
  11.5 13.1 %collective-permute-start.1 = (bf16[512,128]{1,0:T(8,128)(2,1)}, bf16[512,128]{1,0:T(8,128)(2,1)S(1)}, u32[]{:S(2)}, u32[]{:S(2)}) collective-permute-start(bf16[512,128]{1,0:T(8,128)(2,1)} %get-tuple-element.28), channel_id=1, source_target_pairs={{0,8},{1,9},{2,10},{3,11},{4,12},{5,13},{6,14},{7,15},{8,0},{9,1},... | collective-permute-start | bytes 393224 | tf_op jit(solution)/shard_map/ppermute | solution.py:280
  14.0 10.6 %collective-permute-start.2 = (bf16[512,128]{1,0:T(8,128)(2,1)}, bf16[512,128]{1,0:T(8,128)(2,1)S(1)}, u32[]{:S(2)}, u32[]{:S(2)}) collective-permute-start(bf16[512,128]{1,0:T(8,128)(2,1)} %get-tuple-element.29), channel_id=1, source_target_pairs={{0,12},{1,13},{2,14},{3,15},{4,8},{5,9},{6,10},{7,11},{8,4},{9,5},... | collective-permute-start | bytes 393224 | tf_op jit(solution)/shard_map/ppermute | solution.py:280
  24.6 5.5 %copy-start = (bf16[512,128]{1,0:T(8,128)(2,1)S(1)}, bf16[512,128]{1,0:T(8,128)(2,1)}, u32[]{:S(2)}) copy-start(bf16[512,128]{1,0:T(8,128)(2,1)} %get-tuple-element.26) | copy-start | bytes 393220
  24.6 19.9 %all-to-all-start = ((bf16[16,128,128]{2,1,0:T(8,128)(2,1)}), bf16[16,128,128]{2,1,0:T(8,128)(2,1)S(1)}, u32[]{:S(2)}, u32[]{:S(2)}) async-start(bf16[16,128,128]{2,1,0:T(8,128)(2,1)} %bitcast.11), calls=%async_computation | async-start | bytes 1048576 | tf_op jit(solution)/shard_map/all_to_all | solution.py:325
  30.2 2.3 %collective-permute-start.3 = (bf16[4,128,128]{2,1,0:T(8,128)(2,1)S(1)}, bf16[4,128,128]{2,1,0:T(8,128)(2,1)S(1)}, u32[]{:S(2)}, u32[]{:S(2)}) collective-permute-start(bf16[4,128,128]{2,1,0:T(8,128)(2,1)S(1)} %pad_maximum_fusion.1), channel_id=1, source_target_pairs={{0,1},{1,0},{2,3},{3,2},{4,5},{5,4},{6,7},{7,6},{8,9},{9,8},{10,11... | collective-permute-start | bytes 393224 | tf_op jit(solution)/shard_map/ppermute | solution.py:289
  30.6 10.1 %collective-permute-start.4 = (bf16[4,128,128]{2,1,0:T(8,128)(2,1)S(1)}, bf16[4,128,128]{2,1,0:T(8,128)(2,1)S(1)}, u32[]{:S(2)}, u32[]{:S(2)}) collective-permute-start(bf16[4,128,128]{2,1,0:T(8,128)(2,1)S(1)} %pad_maximum_fusion.2), channel_id=1, source_target_pairs={{0,2},{1,3},{2,0},{3,1},{4,6},{5,7},{6,4},{7,5},{8,10},{9,11},{10,... | collective-permute-start | bytes 393224 | tf_op jit(solution)/shard_map/ppermute | solution.py:289
  32.4 10.4 %collective-permute-start.5 = (bf16[4,128,128]{2,1,0:T(8,128)(2,1)S(1)}, bf16[4,128,128]{2,1,0:T(8,128)(2,1)S(1)}, u32[]{:S(2)}, u32[]{:S(2)}) collective-permute-start(bf16[4,128,128]{2,1,0:T(8,128)(2,1)S(1)} %pad_maximum_fusion.3), channel_id=1, source_target_pairs={{0,3},{1,2},{2,1},{3,0},{4,7},{5,6},{6,5},{7,4},{8,11},{9,10},{10,... | collective-permute-start | bytes 393224 | tf_op jit(solution)/shard_map/ppermute | solution.py:289

commit v4 on v3

--- a/solution.py
+++ b/solution.py
@@ -197,7 +197,7 @@
     parts = max(cols // 32, 1)
     batch = max(4, steps // 128)
     inside = pl.BlockSpec(memory_space=pltpu.VMEM)
-    outside = pl.BlockSpec(memory_space=pl.ANY)
+    outside = pl.BlockSpec(memory_space=pltpu.HBM)
     floats = lambda *shape: pltpu.VMEM(shape + (LANES,), jnp.float32)
     own = [
         jax.ShapeDtypeStruct(ids.shape, jnp.int32),
@@ -212,24 +212,26 @@
     if raw:
         scratch = [pltpu.VMEM(x.shape, x.dtype) for x in own] + [pltpu.SemaphoreType.DMA((2, 8))]
         out_shape = out_shape + (own if ahead else [])
+    scratch += [
+        floats(3, (width - 1) * RUNS),
+        floats(length),
+        floats(length),
+        floats(modes, steps // batch * RUNS),
+        floats(batch * modes, RUNS),
+        floats(length),
+    ]
+    scratch += [floats(3, cols // parts * RUNS)] * parts
+    held = scratch + own * 2 + out_shape
+    room = sum(math.prod(x.shape) * jnp.dtype(x.dtype).itemsize for x in held if x.dtype in (jnp.float32, jnp.bfloat16))
     results = pl.pallas_call(
         functools.partial(operator, (piece, pieces, near, sliced, blocks, raw, ahead)),
         in_specs=[outside if raw else inside] * 6,
         out_specs=[inside] * len(out_shape),
         out_shape=out_shape,
-        scratch_shapes=scratch
-        + [
-            floats(3, (width - 1) * RUNS),
-            floats(length),
-            floats(length),
-            floats(modes, steps // batch * RUNS),
-            floats(batch * modes, RUNS),
-            floats(length),
-        ]
-        + [floats(3, cols // parts * RUNS)] * parts,
-        compiler_params=pltpu.CompilerParams(vmem_limit_bytes=56 * 2**20),
+        scratch_shapes=scratch,
+        compiler_params=pltpu.CompilerParams(vmem_limit_bytes=room + 4 * 2**20),
         cost_estimate=pl.CostEstimate(flops=length * LANES * 8000, bytes_accessed=4 * 2**20, transcendentals=0),
-    )(*given)
+    )(*(given if not raw else [pltpu.with_memory_space_constraint(x, pltpu.HBM) for x in given]))
     return results[:blocks], results[blocks:]
 
 

time: 45.7 us -> 44.3 us (0.969)
  Pallas kernels: 18.4 us -> 16.4 us
  waiting for transfers between devices: 13.4 us -> 14.2 us
    pallas_call x2, Pallas kernels: 16.5 us -> 14.6 us  [run_operator(): pl.pallas_call(functools.partial(operator, (piece, pieces, near, sliced,...]
    ppermute x3, waiting for transfers between devices: 2.38 us -> 3.09 us  [spread_far(): lax.ppermute(blocks[d], 'seq', [(i, i ^ near * d) for i in range(count)])]
  transfers between devices with their start and end apart: 7 -> 7, of which waited for: 4 -> 4; matrix products, arithmetic and copies ran while one was open for 0% -> 0% of each run, Pallas kernels for 20% -> 19%
where the time goes in v4:
time: 44.3 us; the launch traced here: 44 us
  Pallas kernels  16.4 us (37%)
  waiting for transfers between devices  14.2 us (32%)
  starting transfers between devices  13.2 us (30%)
    pallas_call x2, Pallas kernels, run_operator(): pl.pallas_call(functools.partial(operator, (piece, pieces, near, sliced,...  14.6 us
    ppermute x3, waiting for transfers between devices, spread_near(): lax.ppermute(chosen, 'seq', [(i, i ^ e) for i in range(count)])  10.3 us
    ppermute x3, starting transfers between devices, spread_far(): lax.ppermute(blocks[d], 'seq', [(i, i ^ near * d) for i in range(count)])  5.68 us
    all_to_all x1, starting transfers between devices, body(): lax.all_to_all(sent, 'seq', split_axis=0, concat_axis=0, tiled=True)  5.28 us
    ppermute x3, waiting for transfers between devices, spread_far(): lax.ppermute(blocks[d], 'seq', [(i, i ^ near * d) for i in range(count)])  3.09 us
    ppermute x3, starting transfers between devices, spread_near(): lax.ppermute(chosen, 'seq', [(i, i ^ e) for i in range(count)])  2.24 us
    pallas_call x2, Pallas kernels, run_join(): pl.pallas_call(kernel, in_specs=[inside] * len(blocks) + [outside] * len(...  1.83 us
  transfers between devices with their start and end apart: 7, of which 4 were waited for; matrix products, arithmetic and copies ran while one was open for 0% of the time, Pallas kernels for 19%

profile of v4, /device:TPU:0, one launch (start us, length us, event | category | flops | bytes accessed | tf_op | source)
XLA Modules:
  0.0 44.0 jit_solution(890617775386722404)
XLA Ops:
  0.0 7.3 %shard_map.64 = (bf16[512,128]{1,0:T(8,128)(2,1)S(1)}, bf16[512,128]{1,0:T(8,128)(2,1)S(1)}, bf16[512,128]{1,0:T(8,128)(2,1)S(1)}, bf16[512,128]{1,0:T(8,128)(2,...) custom-call(s32[16,128]{1,0:T(8,128)} %bitcast.20, ...), custom_call_target="tpu_custom_call" | custom-call | flops 2097152000 | bytes 4194304 | tf_op jit(solution)/shard_map/pallas_call | solution.py:226
  7.3 3.1 %collective-permute-start = (bf16[512,128]{1,0:T(8,128)(2,1)S(1)}, bf16[512,128]{1,0:T(8,128)(2,1)S(1)}, u32[]{:S(2)}, u32[]{:S(2)}) collective-permute-start(bf16[512,128]{1,0:T(8,128)(2,1)S(1)} %get-tuple-element.27), channel_id=1, source_target_pairs={{0,4},{1,5},{2,6},{3,7},{4,0},{5,1},{6,2},{7,3},{8,12},{9,13},{10,... | collective-permute-start | bytes 393224 | tf_op jit(solution)/shard_map/ppermute | solution.py:282
  10.4 2.6 %collective-permute-start.1 = (bf16[512,128]{1,0:T(8,128)(2,1)S(1)}, bf16[512,128]{1,0:T(8,128)(2,1)S(1)}, u32[]{:S(2)}, u32[]{:S(2)}) collective-permute-start(bf16[512,128]{1,0:T(8,128)(2,1)S(1)} %get-tuple-element.28), channel_id=1, source_target_pairs={{0,8},{1,9},{2,10},{3,11},{4,12},{5,13},{6,14},{7,15},{8,0},{9,1},... | collective-permute-start | bytes 393224 | tf_op jit(solution)/shard_map/ppermute | solution.py:282
  13.0 0.0 collective-permute-start.2
  13.0 7.2 %shard_map.65 = bf16[2048,128]{1,0:T(8,128)(2,1)} custom-call(s32[16,128]{1,0:T(8,128)S(1)} %get-tuple-element.20.refs_0_, bf16[512,384]{1,0:T(8,128)(2,1)S(1)} %get-tuple-element.21.refs_1_, f32[3,7,128]{2,1,0:T(8,128)S(1)} %get-tuple-element.22.refs_2_, f32[16,128]{1,0:T(8,128)S(1)} %get-tuple-element.23.refs_3_, f32[16,128]{1,0:T(8,128)S(1)} %get-tuple-element.24.refs_4_, ...), custom_call_target="tpu_custom_call" | custom-call | flops 2097152000 | bytes 4194304 | tf_op jit(solution)/shard_map/pallas_call | solution.py:226
  20.3 0.0 collective-permute-done
  20.3 3.1 %collective-permute-done.1 = bf16[512,128]{1,0:T(8,128)(2,1)S(1)} collective-permute-done((bf16[512,128]{1,0:T(8,128)(2,1)S(1)}, bf16[512,128]{1,0:T(8,128)(2,1)S(1)}, u32[]{:S(2)}, u32[]{:S(2)}) %collective-permute-start.1) | collective-permute-done | bytes 131104 | tf_op jit(solution)/shard_map/ppermute | solution.py:282
  23.3 0.0 collective-permute-done.2
  23.3 5.3 %all-to-all-start = ((bf16[16,128,128]{2,1,0:T(8,128)(2,1)}), bf16[16,128,128]{2,1,0:T(8,128)(2,1)S(1)}, u32[]{:S(2)}, u32[]{:S(2)}) async-start(bf16[16,128,128]{2,1,0:T(8,128)(2,1)} %bitcast.6), calls=%async_computation | async-start | bytes 1048576 | tf_op jit(solution)/shard_map/all_to_all | solution.py:327
  28.8 0.4 collective-permute-start.3
  29.2 1.7 %collective-permute-start.4 = (bf16[4,128,128]{2,1,0:T(8,128)(2,1)S(1)}, bf16[4,128,128]{2,1,0:T(8,128)(2,1)S(1)}, u32[]{:S(2)}, u32[]{:S(2)}) collective-permute-start(bf16[4,128,128]{2,1,0:T(8,128)(2,1)S(1)} %pad_maximum_fusion.2), channel_id=1, source_target_pairs={{0,2},{1,3},{2,0},{3,1},{4,6},{5,7},{6,4},{7,5},{8,10},{9,11},{10,... | collective-permute-start | bytes 393224 | tf_op jit(solution)/shard_map/ppermute | solution.py:291
  31.0 0.1 collective-permute-start.5
  31.1 0.0 collective-permute-done.3.refs_1_
  31.1 8.2 %collective-permute-done.4.refs_2_ = bf16[4,128,128]{2,1,0:T(8,128)(2,1)S(1)} collective-permute-done((bf16[4,128,128]{2,1,0:T(8,128)(2,1)S(1)}, bf16[4,128,128]{2,1,0:T(8,128)(2,1)S(1)}, u32[]{:S(2)}, u32[]{:S(2)}) %collective-permute-start.4) | collective-permute-done | bytes 131104 | tf_op jit(solution)/shard_map/ppermute | solution.py:291
  39.3 2.1 %collective-permute-done.5.refs_3_ = bf16[4,128,128]{2,1,0:T(8,128)(2,1)S(1)} collective-permute-done((bf16[4,128,128]{2,1,0:T(8,128)(2,1)S(1)}, bf16[4,128,128]{2,1,0:T(8,128)(2,1)S(1)}, u32[]{:S(2)}, u32[]{:S(2)}) %collective-permute-start.5) | collective-permute-done | bytes 131104 | tf_op jit(solution)/shard_map/ppermute | solution.py:291
  41.4 0.9 %shard_map.66.refs_1_ = bf16[128,4096]{1,0:T(8,128)(2,1)} custom-call(bf16[4,128,128]{2,1,0:T(8,128)(2,1)S(1)} %pad_maximum_fusion.refs_0_, bf16[4,128,128]{2,1,0:T(8,128)(2,1)S(1)} %collective-permute-done.3.refs_1_, bf16[4,128,128]{2,1,0:T(8,128)(2,1)S(1)} %collective-permute-done.4.refs_2_, bf16[4,128,128]{2,1,0:T(8,128)(2,1)S(1)} %collective-permute-done.5.refs_3_), custom_call_target="tpu_custom_call" | custom-call | tf_op jit(solution)/shard_map/pallas_call | solution.py:267
  42.3 0.8 %all-to-all-done.refs_0_ = bf16[16,128,128]{2,1,0:T(8,128)(2,1)S(1)} async-done(((bf16[16,128,128]{2,1,0:T(8,128)(2,1)}), bf16[16,128,128]{2,1,0:T(8,128)(2,1)S(1)}, u32[]{:S(2)}, u32[]{:S(2)}) %all-to-all-start) | async-done | bytes 524320 | tf_op jit(solution)/shard_map/all_to_all | solution.py:327
  43.1 0.9 %shard_map.67 = bf16[128,4096]{1,0:T(8,128)(2,1)} custom-call(bf16[16,128,128]{2,1,0:T(8,128)(2,1)S(1)} %all-to-all-done.refs_0_, bf16[128,4096]{1,0:T(8,128)(2,1)} %shard_map.66.refs_1_), custom_call_target="tpu_custom_call", output_to_operand_aliasing={{}: (1, {})} | custom-call | tf_op jit(solution)/shard_map/pallas_call | solution.py:267
  (6 shorter events, 0.1 us)
Async XLA Ops:
  7.3 12.9 %collective-permute-start = (bf16[512,128]{1,0:T(8,128)(2,1)S(1)}, bf16[512,128]{1,0:T(8,128)(2,1)S(1)}, u32[]{:S(2)}, u32[]{:S(2)}) collective-permute-start(bf16[512,128]{1,0:T(8,128)(2,1)S(1)} %get-tuple-element.27), channel_id=1, source_target_pairs={{0,4},{1,5},{2,6},{3,7},{4,0},{5,1},{6,2},{7,3},{8,12},{9,13},{10,... | collective-permute-start | bytes 393224 | tf_op jit(solution)/shard_map/ppermute | solution.py:282
  10.4 12.9 %collective-permute-start.1 = (bf16[512,128]{1,0:T(8,128)(2,1)S(1)}, bf16[512,128]{1,0:T(8,128)(2,1)S(1)}, u32[]{:S(2)}, u32[]{:S(2)}) collective-permute-start(bf16[512,128]{1,0:T(8,128)(2,1)S(1)} %get-tuple-element.28), channel_id=1, source_target_pairs={{0,8},{1,9},{2,10},{3,11},{4,12},{5,13},{6,14},{7,15},{8,0},{9,1},... | collective-permute-start | bytes 393224 | tf_op jit(solution)/shard_map/ppermute | solution.py:282
  13.0 10.3 %collective-permute-start.2 = (bf16[512,128]{1,0:T(8,128)(2,1)S(1)}, bf16[512,128]{1,0:T(8,128)(2,1)S(1)}, u32[]{:S(2)}, u32[]{:S(2)}) collective-permute-start(bf16[512,128]{1,0:T(8,128)(2,1)S(1)} %get-tuple-element.29), channel_id=1, source_target_pairs={{0,12},{1,13},{2,14},{3,15},{4,8},{5,9},{6,10},{7,11},{8,4},{9,5},... | collective-permute-start | bytes 393224 | tf_op jit(solution)/shard_map/ppermute | solution.py:282
  23.3 19.8 %all-to-all-start = ((bf16[16,128,128]{2,1,0:T(8,128)(2,1)}), bf16[16,128,128]{2,1,0:T(8,128)(2,1)S(1)}, u32[]{:S(2)}, u32[]{:S(2)}) async-start(bf16[16,128,128]{2,1,0:T(8,128)(2,1)} %bitcast.6), calls=%async_computation | async-start | bytes 1048576 | tf_op jit(solution)/shard_map/all_to_all | solution.py:327
  28.8 2.3 %collective-permute-start.3 = (bf16[4,128,128]{2,1,0:T(8,128)(2,1)S(1)}, bf16[4,128,128]{2,1,0:T(8,128)(2,1)S(1)}, u32[]{:S(2)}, u32[]{:S(2)}) collective-permute-start(bf16[4,128,128]{2,1,0:T(8,128)(2,1)S(1)} %pad_maximum_fusion.1), channel_id=1, source_target_pairs={{0,1},{1,0},{2,3},{3,2},{4,5},{5,4},{6,7},{7,6},{8,9},{9,8},{10,11... | collective-permute-start | bytes 393224 | tf_op jit(solution)/shard_map/ppermute | solution.py:291
  29.2 10.1 %collective-permute-start.4 = (bf16[4,128,128]{2,1,0:T(8,128)(2,1)S(1)}, bf16[4,128,128]{2,1,0:T(8,128)(2,1)S(1)}, u32[]{:S(2)}, u32[]{:S(2)}) collective-permute-start(bf16[4,128,128]{2,1,0:T(8,128)(2,1)S(1)} %pad_maximum_fusion.2), channel_id=1, source_target_pairs={{0,2},{1,3},{2,0},{3,1},{4,6},{5,7},{6,4},{7,5},{8,10},{9,11},{10,... | collective-permute-start | bytes 393224 | tf_op jit(solution)/shard_map/ppermute | solution.py:291
  31.0 10.4 %collective-permute-start.5 = (bf16[4,128,128]{2,1,0:T(8,128)(2,1)S(1)}, bf16[4,128,128]{2,1,0:T(8,128)(2,1)S(1)}, u32[]{:S(2)}, u32[]{:S(2)}) collective-permute-start(bf16[4,128,128]{2,1,0:T(8,128)(2,1)S(1)} %pad_maximum_fusion.3), channel_id=1, source_target_pairs={{0,3},{1,2},{2,1},{3,0},{4,7},{5,6},{6,5},{7,4},{8,11},{9,10},{10,... | collective-permute-start | bytes 393224 | tf_op jit(solution)/shard_map/ppermute | solution.py:291

commit v5 on v4

--- a/solution.py
+++ b/solution.py
@@ -25,11 +25,11 @@
 
 
 def operator(spot, *refs):
-    piece, pieces, near, sliced, blocks, raw, ahead = spot
+    piece, pieces, sends, sliced, raw, ahead = spot
     place = lax.axis_index("seq")
     refs = list(refs)
     take = lambda count: [refs.pop(0) for _ in range(count)]
-    given, outs = take(6), take(blocks)
+    given, outs = take(6), take(len(sends))
     ahead = take(6) if ahead else []
     if raw:
         held, sem = take(6), take(1)[0]
@@ -54,12 +54,12 @@
             copy.wait()
     else:
         held, later = given, []
-    compute(place // near, held, outs, *refs)
+    compute(place, sends, held, outs, *refs)
     for copy in later:
         copy.wait()
 
 
-def compute(far_place, held, outs, halo, query, gated, inputs, factors, result, *streams):
+def compute(place, sends, held, outs, halo, query, gated, inputs, factors, result, *streams):
     ids, table, taps, residue, decay, skip = held
     length = ids.shape[0] * ids.shape[1]
     steps = length // RUNS
@@ -180,13 +180,14 @@
         return tuple(leaps[s] * state[s] + inputs[s, at, :] for s in range(modes))
 
     lax.fori_loop(0, steps // batch, emit, tuple(begins), unroll=4)
-    size = length // len(outs)
-    for d, out in enumerate(outs):
-        first = pl.multiple_of(jnp.bitwise_xor(far_place, d) * size, size) if len(outs) > 1 else 0
-        out[...] = result[pl.ds(first, size), :].astype(jnp.bfloat16)
-
-
-def run_operator(given, piece, pieces, near, sliced, blocks):
+    for out, hops in zip(outs, sends):
+        size = out.shape[0] // len(hops)
+        for n, hop in enumerate(hops):
+            first = 0 if hop is None else pl.multiple_of(jnp.bitwise_xor(place, hop) * size, size)
+            out[n * size : (n + 1) * size, :] = result[pl.ds(first, size), :].astype(jnp.bfloat16)
+
+
+def run_operator(given, piece, pieces, sends, places, sliced):
     ids, table, taps, residue = given[:4]
     raw = piece == 0 or pieces > 2
     ahead = piece == 0 and pieces == 2
@@ -207,7 +208,8 @@
         jax.ShapeDtypeStruct((modes, LANES), jnp.float32),
         jax.ShapeDtypeStruct((1, LANES), jnp.float32),
     ]
-    out_shape = [jax.ShapeDtypeStruct((length // blocks, LANES), jnp.bfloat16)] * blocks
+    rows = [length if hops == [None] else length // places * len(hops) for hops in sends]
+    out_shape = [jax.ShapeDtypeStruct((count, LANES), jnp.bfloat16) for count in rows]
     scratch = []
     if raw:
         scratch = [pltpu.VMEM(x.shape, x.dtype) for x in own] + [pltpu.SemaphoreType.DMA((2, 8))]
@@ -224,7 +226,7 @@
     held = scratch + own * 2 + out_shape
     room = sum(math.prod(x.shape) * jnp.dtype(x.dtype).itemsize for x in held if x.dtype in (jnp.float32, jnp.bfloat16))
     results = pl.pallas_call(
-        functools.partial(operator, (piece, pieces, near, sliced, blocks, raw, ahead)),
+        functools.partial(operator, (piece, pieces, sends, sliced, raw, ahead)),
         in_specs=[outside if raw else inside] * 6,
         out_specs=[inside] * len(out_shape),
         out_shape=out_shape,
@@ -232,64 +234,80 @@
         compiler_params=pltpu.CompilerParams(vmem_limit_bytes=room + 4 * 2**20),
         cost_estimate=pl.CostEstimate(flops=length * LANES * 8000, bytes_accessed=4 * 2**20, transcendentals=0),
     )(*(given if not raw else [pltpu.with_memory_space_constraint(x, pltpu.HBM) for x in given]))
-    return results[:blocks], results[blocks:]
-
-
-def join(piece, pieces, *refs):
-    refs, out, sem = refs[:-2], refs[-2], refs[-1]
-    place = lax.axis_index("seq")
-    copies = []
-    kept = refs[0].shape[-1]
-    for e, ref in enumerate(refs):
-        for d in range(ref.shape[0]):
-            source = d if piece == pieces - 1 else jnp.bitwise_xor(place, d * len(refs) + e)
-            first = pl.multiple_of((source * pieces + piece) * kept, kept)
-            copies.append(pltpu.make_async_copy(ref.at[d], out.at[:, pl.ds(first, kept)], sem.at[len(copies)]))
-    for copy in copies:
-        copy.start()
-    for copy in copies:
-        copy.wait()
-
-
-def run_join(piece, pieces, blocks, out):
-    count = sum(x.shape[0] for x in blocks)
-    inside = pl.BlockSpec(memory_space=pltpu.VMEM)
-    outside = pl.BlockSpec(memory_space=pl.ANY)
+    return results[: len(sends)], results[len(sends) :]
+
+
+def run_join(places, blocks, out):
+    arrays = [array for array, _ in blocks]
     into = [] if out is None else [out]
+    local, kept = arrays[0].shape[-2:]
+    count = sum(len(marks) - marks.count(None) for _, marks in blocks)
 
     def kernel(*refs):
         refs = list(refs)
         if into:
-            refs.pop(len(blocks))
-        join(piece, pieces, *refs)
-
-    local, kept = blocks[0].shape[1:]
+            refs.pop(len(arrays))
+        *refs, out, sem = refs
+        place = lax.axis_index("seq")
+        copies = []
+        for ref, (_, marks) in zip(refs, blocks):
+            for n, mark in enumerate(marks):
+                if mark is None:
+                    continue
+                piece, hop, *plain = mark
+                first = ((hop if plain else jnp.bitwise_xor(place, hop)) * 2 + piece) * kept
+                target = out.at[:, pl.ds(first if plain else pl.multiple_of(first, kept), kept)]
+                copies.append(pltpu.make_async_copy(ref.at[n], target, sem.at[len(copies)]))
+        for copy in copies:
+            copy.start()
+        for copy in copies:
+            copy.wait()
+
+    anywhere = pl.BlockSpec(memory_space=pl.ANY)
     return pl.pallas_call(
         kernel,
-        in_specs=[inside] * len(blocks) + [outside] * len(into),
-        out_specs=outside,
-        out_shape=jax.ShapeDtypeStruct((local, count * pieces * kept), blocks[0].dtype),
+        in_specs=[anywhere] * (len(arrays) + len(into)),
+        out_specs=anywhere,
+        out_shape=jax.ShapeDtypeStruct((local, places * 2 * kept), arrays[0].dtype),
         scratch_shapes=[pltpu.SemaphoreType.DMA((count,))],
-        input_output_aliases={len(blocks): 0} if into else {},
+        input_output_aliases={len(arrays): 0} if into else {},
         compiler_params=pltpu.CompilerParams(vmem_limit_bytes=2**20),
-    )(*blocks, *into)
-
-
-def spread_far(blocks, far, near, local):
-    kept = blocks[0].shape[1]
-    count = far * near
-    spread = [blocks[0]] + [
-        lax.ppermute(blocks[d], "seq", [(i, i ^ (near * d)) for i in range(count)]) for d in range(1, far)
+    )(*(pltpu.with_memory_space_constraint(x, pltpu.VMEM) for x in arrays), *into)
+
+
+def by_hops(given, places, local):
+    far = list(range(0, places, 4))
+    hop = lambda x, by: lax.ppermute(x, "seq", [(i, i ^ by) for i in range(places)])
+
+    def run(given, piece, sends):
+        results, ahead = run_operator(given, piece, 2, sends, places, False)
+        return [x.reshape(-1, local, x.shape[-1]) for x in results], ahead
+
+    first, given = run(given, 0, [[d + e for e in range(4)] for d in far])
+    landed = first[:1] + [hop(x, d) for x, d in zip(first[1:], far[1:])]
+    (*straight, across), _ = run(given, 1, [[d, d + 1] for d in far] + [[d + e for d in far for e in (2, 3)]])
+    landed, straight = lax.optimization_barrier((landed, straight))
+    crossed = hop(across, 2)
+    final = [
+        hop(jnp.concatenate([straight[n], crossed[2 * n : 2 * n + 2]]), d) for n, d in enumerate(far) if d > 0
     ]
-    return [x.reshape(near, local, kept) for x in spread]
-
-
-def spread_near(spread, near, place, count):
-    hops = []
-    for e in range(near):
-        chosen = jnp.stack([lax.dynamic_index_in_dim(x, (place % near) ^ e, 0, False) for x in spread])
-        hops.append(lax.ppermute(chosen, "seq", [(i, i ^ e) for i in range(count)]) if e else chosen)
-    return hops
+    turned = hop(jnp.concatenate([x[2:] for x in landed]), 2)
+    odd = [x[1:2] for x in landed] + [turned[2 * n + 1 : 2 * n + 2] for n in range(len(far))]
+    out = run_join(
+        places,
+        [(x, [(0, d)]) for x, d in zip(landed, far)]
+        + [(turned, [mark for d in far for mark in ((0, d + 2), None)])]
+        + [(hop(jnp.concatenate(odd), 1), [(0, d + 1) for d in far] + [(0, d + 3) for d in far])],
+        None,
+    )
+    odd = [straight[0][1:2], crossed[1:2]] + [x[n : n + 1] for x in final for n in (1, 3)]
+    return run_join(
+        places,
+        [(straight[0], [(1, 0)]), (crossed, [(1, 2)])]
+        + [(x, [(1, d), None, (1, d + 2)]) for x, d in zip(final, far[1:])]
+        + [(hop(jnp.concatenate(odd), 1), [(1, d + e) for d in far for e in (1, 3)])],
+        out,
+    )
 
 
 def body(token_ids, vocab_table, short_filter, residue, decay, skip_gain):
@@ -299,8 +317,6 @@
     local = length // places
     share = vocab_table.shape[2]
     pieces = -(-share // LANES)
-    near = math.gcd(places, 4)
-    far = places // near
     ids = token_ids.reshape(-1, min(LANES, length // RUNS))
     table = vocab_table.transpose(1, 0, 2)
     rows = [short_filter.transpose(1, 0, 2), residue.T, decay.T, skip_gain[None]]
@@ -309,28 +325,17 @@
         widen = lambda x: jnp.pad(x, [(0, 0)] * (x.ndim - 1) + [(0, pieces * LANES - share)])
         rows = [widen(lax.dynamic_slice_in_dim(x, place * share, share, x.ndim - 1)) for x in rows]
         table = widen(table)
-    staged = not sliced and far & (far - 1) == 0 and pieces > 1
     given = (ids, table, *rows)
-    waiting = []
+    if not sliced and pieces == 2 and places % 4 == 0 and places & (places - 1) == 0 and places > 4:
+        return by_hops(given, places, local)
     parts = []
     for piece in range(pieces):
-        by_hops = staged and piece < pieces - 1
-        blocks, ahead = run_operator(given, piece, pieces, near, sliced, far if by_hops else 1)
+        blocks, ahead = run_operator(given, piece, pieces, [[None]], places, sliced)
         given = ahead or given
-        if by_hops:
-            waiting.append(spread_far(blocks, far, near, local))
-            continue
         kept = min(LANES, share - piece * LANES)
         sent = blocks[0][:, :kept].reshape(places, local, kept)
-        if staged:
-            sent, waiting = lax.optimization_barrier((sent, waiting))
         parts.append(lax.all_to_all(sent, "seq", split_axis=0, concat_axis=0, tiled=True))
-    if not staged:
-        return jnp.concatenate(parts, axis=2).transpose(1, 0, 2).reshape(local, places * share)
-    out = None
-    for piece, spread in enumerate(waiting):
-        out = run_join(piece, pieces, spread_near(spread, near, place, places), out)
-    return run_join(pieces - 1, pieces, parts, out)
+    return jnp.concatenate(parts, axis=2).transpose(1, 0, 2).reshape(local, places * share)
 
 
 def solution(mesh):

time: 44.3 us -> 43 us (0.971)
  waiting for transfers between devices: 14.2 us -> 11.6 us
  local copies, waits for them, and re-layouts: 0.06 us -> 1.63 us
  Pallas kernels: 16.4 us -> 15.6 us
  starting transfers between devices: 13.2 us -> 13.7 us
    ppermute x6 -> x10, starting transfers between devices: 7.92 us -> 13.7 us  [by_hops(): lax.ppermute(x, 'seq', [(i, i ^ by) for i in range(places)])]
    all_to_all x1 -> x0, starting transfers between devices: 5.28 us -> none  [body(): lax.all_to_all(sent, 'seq', split_axis=0, concat_axis=0, tiled=True)]
    ppermute x6 -> x10, waiting for transfers between devices: 13.4 us -> 11.6 us  [by_hops(): lax.ppermute(x, 'seq', [(i, i ^ by) for i in range(places)])]
    slice x0 -> x7, local copies, waits for them, and re-layouts: none -> 0.86 us  [the longest x6 0.85 us: by_hops(): turned = hop(jnp.concatenate([x[2:] for x in landed]), 2)]
    pallas_call x4, Pallas kernels: 16.4 us -> 15.6 us  [the longest x2 13.8 us: run_operator(): pl.pallas_call(functools.partial(operator, (piece, pieces, sends, sliced,...]
    all_to_all x1 -> x0, waiting for transfers between devices: 0.78 us -> none  [body(): lax.all_to_all(sent, 'seq', split_axis=0, concat_axis=0, tiled=True)]
    unnamed x0 -> x22, local copies, waits for them, and re-layouts: none -> 0.75 us
  transfers between devices with their start and end apart: 7 -> 10, of which waited for: 4 -> 6; matrix products, arithmetic and copies ran while one was open for 0% -> 1% of each run, Pallas kernels for 19% -> 17%
where the time goes in v5:
time: 43 us; the launch traced here: 42.8 us
  Pallas kernels  15.6 us (36%)
  starting transfers between devices  13.7 us (32%)
  waiting for transfers between devices  11.6 us (27%)
  local copies, waits for them, and re-layouts  1.63 us (4%)
    pallas_call x2, Pallas kernels, run_operator(): pl.pallas_call(functools.partial(operator, (piece, pieces, sends, sliced,...  13.8 us
    ppermute x10, starting transfers between devices, by_hops(): lax.ppermute(x, 'seq', [(i, i ^ by) for i in range(places)])  13.7 us
    ppermute x10, waiting for transfers between devices, by_hops(): lax.ppermute(x, 'seq', [(i, i ^ by) for i in range(places)])  11.6 us
    pallas_call x2, Pallas kernels, run_join(): pl.pallas_call(kernel, in_specs=[anywhere] * (len(arrays) + len(into)), o...  1.84 us
  transfers between devices with their start and end apart: 10, of which 6 were waited for; matrix products, arithmetic and copies ran while one was open for 1% of the time, Pallas kernels for 17%

profile of v5, /device:TPU:0, one launch (start us, length us, event | category | flops | bytes accessed | tf_op | source)
XLA Modules:
  0.0 42.8 jit_solution(1467111149966228439)
XLA Ops:
  0.0 7.3 %shard_map.64 = (bf16[512,128]{1,0:T(8,128)(2,1)S(1)}, bf16[512,128]{1,0:T(8,128)(2,1)S(1)}, bf16[512,128]{1,0:T(8,128)(2,1)S(1)}, bf16[512,128]{1,0:T(8,128)(2,...) custom-call(s32[16,128]{1,0:T(8,128)} %bitcast.32, ...), custom_call_target="tpu_custom_call" | custom-call | flops 2097152000 | bytes 4194304 | tf_op jit(solution)/shard_map/pallas_call | solution.py:228
  7.3 3.1 %collective-permute-start = (bf16[4,128,128]{2,1,0:T(8,128)(2,1)S(1)}, bf16[4,128,128]{2,1,0:T(8,128)(2,1)S(1)}, u32[]{:S(2)}, u32[]{:S(2)}) collective-permute-start(bf16[4,128,128]{2,1,0:T(8,128)(2,1)S(1)} %bitcast.26), channel_id=1, source_target_pairs={{0,4},{1,5},{2,6},{3,7},{4,0},{5,1},{6,2},{7,3},{8,12},{9,13},{10,... | collective-permute-start | bytes 393224 | tf_op jit(solution)/shard_map/ppermute | solution.py:280
  10.4 2.6 %collective-permute-start.1 = (bf16[4,128,128]{2,1,0:T(8,128)(2,1)S(1)}, bf16[4,128,128]{2,1,0:T(8,128)(2,1)S(1)}, u32[]{:S(2)}, u32[]{:S(2)}) collective-permute-start(bf16[4,128,128]{2,1,0:T(8,128)(2,1)S(1)} %bitcast.25), channel_id=1, source_target_pairs={{0,8},{1,9},{2,10},{3,11},{4,12},{5,13},{6,14},{7,15},{8,0},{9,1},... | collective-permute-start | bytes 393224 | tf_op jit(solution)/shard_map/ppermute | solution.py:280
  13.0 0.0 collective-permute-start.2
  13.0 6.4 %shard_map.65 = (bf16[256,128]{1,0:T(8,128)(2,1)S(1)}, bf16[256,128]{1,0:T(8,128)(2,1)S(1)}, bf16[256,128]{1,0:T(8,128)(2,1)S(1)}, bf16[256,128]{1,0:T(8,128)(2,1)S(1)}, bf16[1024,128]{1,0:T(8,128)(2,1)S(1)}) custom-call(s32[16,128]{1,0:T(8,128)S(1)} %get-tuple-element.32.refs_0_, bf16[512,384]{1,0:T(8,128)(2,1)S(1)} %get-tuple-element.33.refs_1_, ...), custom_call_target="tpu_custom_call" | custom-call | flops 2097152000 | bytes 4194304 | tf_op jit(solution)/shard_map/pallas_call | solution.py:228
  19.5 1.8 %collective-permute-start.3 = (bf16[8,128,128]{2,1,0:T(8,128)(2,1)S(1)}, bf16[8,128,128]{2,1,0:T(8,128)(2,1)S(1)}, u32[]{:S(2)}, u32[]{:S(2)}) collective-permute-start(bf16[8,128,128]{2,1,0:T(8,128)(2,1)S(1)} %bitcast.23), channel_id=1, source_target_pairs={{0,2},{1,3},{2,0},{3,1},{4,6},{5,7},{6,4},{7,5},{8,10},{9,11},{10,... | collective-permute-start | bytes 786440 | tf_op jit(solution)/shard_map/ppermute | solution.py:280
  21.2 0.0 collective-permute-done.refs_1_
  21.2 0.0 copy-start
  21.2 2.1 %collective-permute-done.1.refs_2_ = bf16[4,128,128]{2,1,0:T(8,128)(2,1)S(1)} collective-permute-done((bf16[4,128,128]{2,1,0:T(8,128)(2,1)S(1)}, bf16[4,128,128]{2,1,0:T(8,128)(2,1)S(1)}, u32[]{:S(2)}, u32[]{:S(2)}) %collective-permute-start.1) | collective-permute-done | bytes 131104 | tf_op jit(solution)/shard_map/ppermute | solution.py:280
  23.3 0.0 collective-permute-done.2.refs_3_
  23.3 0.0 copy-start.2
  23.4 0.6 %copy-done.2 = bf16[4,128,128]{2,1,0:T(8,128)(2,1)} copy-done((bf16[4,128,128]{2,1,0:T(8,128)(2,1)}, bf16[4,128,128]{2,1,0:T(8,128)(2,1)S(1)}, u32[]{:S(2)}) %copy-start.2) | copy-done | bytes 131096
  24.0 0.0 copy-done
  24.0 0.0 slice-start.1
  24.0 0.0 slice-start
  24.1 0.8 %slice-done.1 = bf16[2,128,128]{2,1,0:T(8,128)(2,1)S(1)} async-done(((bf16[4,128,128]{2,1,0:T(8,128)(2,1)}), bf16[2,128,128]{2,1,0:T(8,128)(2,1)S(1)}, s32[]{:S(2)}) %slice-start.1) | async-done | bytes 65560 | tf_op jit(solution)/shard_map/slice | solution.py:294
  24.8 0.0 slice-done
  24.9 0.0 copy-start.3
  24.9 1.6 %collective-permute-start.8 = (bf16[8,128,128]{2,1,0:T(8,128)(2,1)S(1)}, bf16[8,128,128]{2,1,0:T(8,128)(2,1)S(1)}, u32[]{:S(2)}, u32[]{:S(2)}) collective-permute-start(bf16[8,128,128]{2,1,0:T(8,128)(2,1)S(1)} %pad_maximum_fusion), channel_id=1, source_target_pairs={{0,2},{1,3},{2,0},{3,1},{4,6},{5,7},{6,4},{7,5},{8,10},{9,11},{10,... | collective-permute-start | bytes 786440 | tf_op jit(solution)/shard_map/ppermute | solution.py:280
  26.5 0.0 copy-done.3
  26.5 2.3 %collective-permute-done.3.refs_1_ = bf16[8,128,128]{2,1,0:T(8,128)(2,1)S(1)} collective-permute-done((bf16[8,128,128]{2,1,0:T(8,128)(2,1)S(1)}, bf16[8,128,128]{2,1,0:T(8,128)(2,1)S(1)}, u32[]{:S(2)}, u32[]{:S(2)}) %collective-permute-start.3) | collective-permute-done | bytes 262176 | tf_op jit(solution)/shard_map/ppermute | solution.py:280
  28.8 0.1 collective-permute-start.4
  28.9 4.4 %collective-permute-start.5 = (bf16[4,128,128]{2,1,0:T(8,128)(2,1)S(1)}, bf16[4,128,128]{2,1,0:T(8,128)(2,1)S(1)}, u32[]{:S(2)}, u32[]{:S(2)}) collective-permute-start(bf16[4,128,128]{2,1,0:T(8,128)(2,1)S(1)} %pad_maximum_fusion.2), channel_id=1, source_target_pairs={{0,8},{1,9},{2,10},{3,11},{4,12},{5,13},{6,14},{7,15},{8,0},{9,1},... | collective-permute-start | bytes 393224 | tf_op jit(solution)/shard_map/ppermute | solution.py:280
  33.4 0.1 collective-permute-start.6
  33.5 0.0 collective-permute-done.8.refs_4_
  33.5 0.1 collective-permute-start.9
  33.6 1.8 %collective-permute-done.4.refs_2_ = bf16[4,128,128]{2,1,0:T(8,128)(2,1)S(1)} collective-permute-done((bf16[4,128,128]{2,1,0:T(8,128)(2,1)S(1)}, bf16[4,128,128]{2,1,0:T(8,128)(2,1)S(1)}, u32[]{:S(2)}, u32[]{:S(2)}) %collective-permute-start.4) | collective-permute-done | bytes 131104 | tf_op jit(solution)/shard_map/ppermute | solution.py:280
  35.4 0.0 copy-start.1
  35.4 3.2 %collective-permute-done.5.refs_3_ = bf16[4,128,128]{2,1,0:T(8,128)(2,1)S(1)} collective-permute-done((bf16[4,128,128]{2,1,0:T(8,128)(2,1)S(1)}, bf16[4,128,128]{2,1,0:T(8,128)(2,1)S(1)}, u32[]{:S(2)}, u32[]{:S(2)}) %collective-permute-start.5) | collective-permute-done | bytes 131104 | tf_op jit(solution)/shard_map/ppermute | solution.py:280
  38.7 1.6 %collective-permute-done.6.refs_4_ = bf16[4,128,128]{2,1,0:T(8,128)(2,1)S(1)} collective-permute-done((bf16[4,128,128]{2,1,0:T(8,128)(2,1)S(1)}, bf16[4,128,128]{2,1,0:T(8,128)(2,1)S(1)}, u32[]{:S(2)}, u32[]{:S(2)}) %collective-permute-start.6) | collective-permute-done | bytes 131104 | tf_op jit(solution)/shard_map/ppermute | solution.py:280
  40.3 0.1 collective-permute-start.7
  40.4 0.0 collective-permute-done.9.refs_5_
  40.4 0.0 copy-done.1
  40.4 0.9 %shard_map.66.refs_6_ = bf16[128,4096]{1,0:T(8,128)(2,1)} custom-call(bf16[4,128,128]{2,1,0:T(8,128)(2,1)S(1)} %bitcast.17, bf16[4,128,128]{2,1,0:T(8,128)(2,1)S(1)} %copy-done.1, bf16[4,128,128]{2,1,0:T(8,128)(2,1)S(1)} %collective-permute-done.1.refs_2_, bf16[4,128,128]{2,1,0:T(8,128)(2,1)S(1)} %copy-done.3, ...), custom_call_target="tpu_custom_call" | custom-call | tf_op jit(solution)/shard_map/pallas_call | solution.py:267
  41.3 0.6 %collective-permute-done.7.refs_5_ = bf16[8,128,128]{2,1,0:T(8,128)(2,1)S(1)} collective-permute-done((bf16[8,128,128]{2,1,0:T(8,128)(2,1)S(1)}, bf16[8,128,128]{2,1,0:T(8,128)(2,1)S(1)}, u32[]{:S(2)}, u32[]{:S(2)}) %collective-permute-start.7) | collective-permute-done | bytes 262176 | tf_op jit(solution)/shard_map/ppermute | solution.py:280
  41.9 0.9 %shard_map.67 = bf16[128,4096]{1,0:T(8,128)(2,1)} custom-call(bf16[2,128,128]{2,1,0:T(8,128)(2,1)S(1)} %bitcast.19, bf16[8,128,128]{2,1,0:T(8,128)(2,1)S(1)} %collective-permute-done.3.refs_1_, bf16[4,128,128]{2,1,0:T(8,128)(2,1)S(1)} %collective-permute-done.4.refs_2_, ...), custom_call_target="tpu_custom_call", output_to_operand_aliasing={{}: (6, {})} | custom-call | tf_op jit(solution)/shard_map/pallas_call | solution.py:267
  (23 shorter events, 0.2 us)
Async XLA Ops:
  7.3 13.9 %collective-permute-start = (bf16[4,128,128]{2,1,0:T(8,128)(2,1)S(1)}, bf16[4,128,128]{2,1,0:T(8,128)(2,1)S(1)}, u32[]{:S(2)}, u32[]{:S(2)}) collective-permute-start(bf16[4,128,128]{2,1,0:T(8,128)(2,1)S(1)} %bitcast.26), channel_id=1, source_target_pairs={{0,4},{1,5},{2,6},{3,7},{4,0},{5,1},{6,2},{7,3},{8,12},{9,13},{10,... | collective-permute-start | bytes 393224 | tf_op jit(solution)/shard_map/ppermute | solution.py:280
  10.4 12.9 %collective-permute-start.1 = (bf16[4,128,128]{2,1,0:T(8,128)(2,1)S(1)}, bf16[4,128,128]{2,1,0:T(8,128)(2,1)S(1)}, u32[]{:S(2)}, u32[]{:S(2)}) collective-permute-start(bf16[4,128,128]{2,1,0:T(8,128)(2,1)S(1)} %bitcast.25), channel_id=1, source_target_pairs={{0,8},{1,9},{2,10},{3,11},{4,12},{5,13},{6,14},{7,15},{8,0},{9,1},... | collective-permute-start | bytes 393224 | tf_op jit(solution)/shard_map/ppermute | solution.py:280
  13.0 10.3 %collective-permute-start.2 = (bf16[4,128,128]{2,1,0:T(8,128)(2,1)S(1)}, bf16[4,128,128]{2,1,0:T(8,128)(2,1)S(1)}, u32[]{:S(2)}, u32[]{:S(2)}) collective-permute-start(bf16[4,128,128]{2,1,0:T(8,128)(2,1)S(1)} %bitcast.24), channel_id=1, source_target_pairs={{0,12},{1,13},{2,14},{3,15},{4,8},{5,9},{6,10},{7,11},{8,4},{9,5},... | collective-permute-start | bytes 393224 | tf_op jit(solution)/shard_map/ppermute | solution.py:280
  19.5 9.3 %collective-permute-start.3 = (bf16[8,128,128]{2,1,0:T(8,128)(2,1)S(1)}, bf16[8,128,128]{2,1,0:T(8,128)(2,1)S(1)}, u32[]{:S(2)}, u32[]{:S(2)}) collective-permute-start(bf16[8,128,128]{2,1,0:T(8,128)(2,1)S(1)} %bitcast.23), channel_id=1, source_target_pairs={{0,2},{1,3},{2,0},{3,1},{4,6},{5,7},{6,4},{7,5},{8,10},{9,11},{10,... | collective-permute-start | bytes 786440 | tf_op jit(solution)/shard_map/ppermute | solution.py:280
  21.2 2.8 %copy-start = (bf16[4,128,128]{2,1,0:T(8,128)(2,1)}, bf16[4,128,128]{2,1,0:T(8,128)(2,1)S(1)}, u32[]{:S(2)}) copy-start(bf16[4,128,128]{2,1,0:T(8,128)(2,1)S(1)} %collective-permute-done.refs_1_) | copy-start | bytes 393220
  23.3 0.6 %copy-start.2 = (bf16[4,128,128]{2,1,0:T(8,128)(2,1)}, bf16[4,128,128]{2,1,0:T(8,128)(2,1)S(1)}, u32[]{:S(2)}) copy-start(bf16[4,128,128]{2,1,0:T(8,128)(2,1)S(1)} %collective-permute-done.2.refs_3_) | copy-start | bytes 393220
  24.0 0.8 %slice-start.1 = ((bf16[4,128,128]{2,1,0:T(8,128)(2,1)}), bf16[2,128,128]{2,1,0:T(8,128)(2,1)S(1)}, s32[]{:S(2)}) async-start(bf16[4,128,128]{2,1,0:T(8,128)(2,1)} %copy-done.2), calls=%async_computation.1 | async-start | bytes 131072 | tf_op jit(solution)/shard_map/slice | solution.py:294
  24.0 0.9 %slice-start = ((bf16[4,128,128]{2,1,0:T(8,128)(2,1)}), bf16[2,128,128]{2,1,0:T(8,128)(2,1)S(1)}, s32[]{:S(2)}) async-start(bf16[4,128,128]{2,1,0:T(8,128)(2,1)} %copy-done), calls=%async_computation | async-start | bytes 131072 | tf_op jit(solution)/shard_map/slice | solution.py:294
  24.9 1.6 %copy-start.3 = (bf16[4,128,128]{2,1,0:T(8,128)(2,1)S(1)}, bf16[4,128,128]{2,1,0:T(8,128)(2,1)}, u32[]{:S(2)}) copy-start(bf16[4,128,128]{2,1,0:T(8,128)(2,1)} %copy-done.2) | copy-start | bytes 393220
  24.9 8.5 %collective-permute-start.8 = (bf16[8,128,128]{2,1,0:T(8,128)(2,1)S(1)}, bf16[8,128,128]{2,1,0:T(8,128)(2,1)S(1)}, u32[]{:S(2)}, u32[]{:S(2)}) collective-permute-start(bf16[8,128,128]{2,1,0:T(8,128)(2,1)S(1)} %pad_maximum_fusion), channel_id=1, source_target_pairs={{0,2},{1,3},{2,0},{3,1},{4,6},{5,7},{6,4},{7,5},{8,10},{9,11},{10,... | collective-permute-start | bytes 786440 | tf_op jit(solution)/shard_map/ppermute | solution.py:280
  28.8 6.6 %collective-permute-start.4 = (bf16[4,128,128]{2,1,0:T(8,128)(2,1)S(1)}, bf16[4,128,128]{2,1,0:T(8,128)(2,1)S(1)}, u32[]{:S(2)}, u32[]{:S(2)}) collective-permute-start(bf16[4,128,128]{2,1,0:T(8,128)(2,1)S(1)} %pad_maximum_fusion.1), channel_id=1, source_target_pairs={{0,4},{1,5},{2,6},{3,7},{4,0},{5,1},{6,2},{7,3},{8,12},{9,13},{10,... | collective-permute-start | bytes 393224 | tf_op jit(solution)/shard_map/ppermute | solution.py:280
  28.9 9.7 %collective-permute-start.5 = (bf16[4,128,128]{2,1,0:T(8,128)(2,1)S(1)}, bf16[4,128,128]{2,1,0:T(8,128)(2,1)S(1)}, u32[]{:S(2)}, u32[]{:S(2)}) collective-permute-start(bf16[4,128,128]{2,1,0:T(8,128)(2,1)S(1)} %pad_maximum_fusion.2), channel_id=1, source_target_pairs={{0,8},{1,9},{2,10},{3,11},{4,12},{5,13},{6,14},{7,15},{8,0},{9,1},... | collective-permute-start | bytes 393224 | tf_op jit(solution)/shard_map/ppermute | solution.py:280
  33.4 6.9 %collective-permute-start.6 = (bf16[4,128,128]{2,1,0:T(8,128)(2,1)S(1)}, bf16[4,128,128]{2,1,0:T(8,128)(2,1)S(1)}, u32[]{:S(2)}, u32[]{:S(2)}) collective-permute-start(bf16[4,128,128]{2,1,0:T(8,128)(2,1)S(1)} %pad_maximum_fusion.3), channel_id=1, source_target_pairs={{0,12},{1,13},{2,14},{3,15},{4,8},{5,9},{6,10},{7,11},{8,4},{9,5},... | collective-permute-start | bytes 393224 | tf_op jit(solution)/shard_map/ppermute | solution.py:280
  33.5 6.9 %collective-permute-start.9 = (bf16[8,128,128]{2,1,0:T(8,128)(2,1)S(1)}, bf16[8,128,128]{2,1,0:T(8,128)(2,1)S(1)}, u32[]{:S(2)}, u32[]{:S(2)}) collective-permute-start(bf16[8,128,128]{2,1,0:T(8,128)(2,1)S(1)} %constant_dynamic-update-slice_fusion.8), channel_id=1, source_target_pairs={{0,1},{1,0},{2,3},{3,2},{4,5},{5,4},{6,7},{7,6},{8,9},{9,8},{10,11... | collective-permute-start | bytes 786440 | tf_op jit(solution)/shard_map/ppermute | solution.py:280
  35.4 5.0 %copy-start.1 = (bf16[4,128,128]{2,1,0:T(8,128)(2,1)S(1)}, bf16[4,128,128]{2,1,0:T(8,128)(2,1)}, u32[]{:S(2)}) copy-start(bf16[4,128,128]{2,1,0:T(8,128)(2,1)} %copy-done) | copy-start | bytes 393220
  40.3 1.6 %collective-permute-start.7 = (bf16[8,128,128]{2,1,0:T(8,128)(2,1)S(1)}, bf16[8,128,128]{2,1,0:T(8,128)(2,1)S(1)}, u32[]{:S(2)}, u32[]{:S(2)}) collective-permute-start(bf16[8,128,128]{2,1,0:T(8,128)(2,1)S(1)} %constant_dynamic-update-slice_fusion), channel_id=1, source_target_pairs={{0,1},{1,0},{2,3},{3,2},{4,5},{5,4},{6,7},{7,6},{8,9},{9,8},{10,11... | collective-permute-start | bytes 786440 | tf_op jit(solution)/shard_map/ppermute | solution.py:280

commit v6 on v5

--- a/solution.py
+++ b/solution.py
@@ -39,8 +39,10 @@
             own = pl.ds(pl.multiple_of(column, LANES), LANES)
             ids, table, taps, residue, decay, skip = given
             pairs = [(ids, into[0])]
-            for k in range(3):
-                pairs.append((table.at[k, :, pl.ds(first * LANES, LANES)], into[1].at[:, pl.ds(k * LANES, LANES)]))
+            half = into[1].shape[0]
+            for n in range(6):
+                words, column = pl.ds(n // 3 * half, half), pl.ds(first * LANES, LANES)
+                pairs.append((table.at[n % 3, words, column], into[1].at[:, pl.ds(n * LANES, LANES)]))
             pairs.append((taps.at[:, :, own], into[2]))
             for ref, target in zip((residue, decay, skip), into[3:]):
                 pairs.append((ref.at[:, own], target))
@@ -59,11 +61,11 @@
         copy.wait()
 
 
-def compute(place, sends, held, outs, halo, query, gated, inputs, factors, result, *streams):
+def compute(place, sends, held, outs, halo, query, gated, inputs, result, *streams):
     ids, table, taps, residue, decay, skip = held
     length = ids.shape[0] * ids.shape[1]
     steps = length // RUNS
-    vocab = table.shape[0]
+    half = table.shape[0]
     width = taps.shape[1]
     modes = residue.shape[0]
     rim = width - 1
@@ -72,25 +74,31 @@
 
     cols = ids.shape[1]
     part = cols // len(streams)
-    word = lax.broadcasted_iota(jnp.int32, (RUNS, vocab), 1)
-
-    def look_up(here, first, count):
+    word = lax.broadcasted_iota(jnp.int32, (RUNS, half), 1)
+
+    def look_up(here, first, count, place_row):
+        upper = here >= half
+        within = jnp.where(upper, here - half, here)
         hot = [
-            jnp.where(jnp.broadcast_to(here[:, j : j + 1], word.shape) == word, 1.0, 0.0)
+            jnp.where(jnp.broadcast_to(within[:, j : j + 1], word.shape) == word, 1.0, 0.0)
             for j in range(first, first + count)
         ]
         hot = jnp.concatenate(hot, axis=0).astype(jnp.bfloat16)
         found = jnp.dot(hot, table[...], preferred_element_type=jnp.float32)
-        return [found[:, k * LANES : (k + 1) * LANES] for k in range(3)]
+        for j in range(count):
+            above = spread(here[:, first + j : first + j + 1]) >= half
+            rows = found[j * RUNS : (j + 1) * RUNS]
+            for k in range(3):
+                low, high = (rows[:, n * LANES : (n + 1) * LANES] for n in (k, k + 3))
+                place_row(k, j, jnp.where(above, high, low))
 
     def ids_of(block):
         return ids[pl.ds(block, RUNS, stride=steps // cols), :]
 
-    tail = look_up(ids_of(steps // cols - 1), cols - rim, rim)
-    for k in range(3):
-        for j in range(rim):
-            rows = slice(j * RUNS, (j + 1) * RUNS)
-            halo[k, rows, :] = delay_runs(tail[k][rows], 1)
+    def place_tail(k, j, row):
+        halo[k, j * RUNS : (j + 1) * RUNS, :] = delay_runs(row, 1)
+
+    look_up(ids_of(steps // cols - 1), cols - rim, rim, place_tail)
 
     filters = [[spread(taps[k, lag : lag + 1, :]) for lag in range(width)] for k in range(3)]
 
@@ -117,8 +125,11 @@
                 gated[at, :] = mixed[1] * mixed[2]
 
         for n, stream in enumerate(streams):
-            for k, found in enumerate(look_up(here, n * part, part)):
-                stream[k] = found
+
+            def place_row(k, j, row, stream=stream):
+                stream[k, j * RUNS : (j + 1) * RUNS, :] = row
+
+            look_up(here, n * part, part, place_row)
             if n > 0:
                 mix((n - 1) * part)
         mix(cols - part)
@@ -128,7 +139,7 @@
 
     lax.fori_loop(0, steps // cols, block_step, 0)
 
-    batch = factors.shape[0] // modes
+    batch = steps // inputs.shape[0]
     rate = decay[...] / length
     weight = residue[...] * jnp.sqrt(2.0 * rate)
     pole = jnp.exp(-rate)
@@ -137,8 +148,6 @@
     for n in range(batch):
         early.append(spread(jnp.sum(power, axis=0, keepdims=True)))
         power = weight * jnp.exp(-rate * (n + 1))
-        for s in range(modes):
-            factors[n * modes + s] = spread(power[s : s + 1])
     early[0] = early[0] + spread(skip[...])
     poles = [spread(pole[s : s + 1]) for s in range(modes)]
     leap = jnp.exp(-rate * batch)
@@ -155,7 +164,7 @@
             taken = values[0]
             for value in values[1:]:
                 taken = poles[s] * taken + value
-            inputs[s, pl.ds(pl.multiple_of(m * RUNS, RUNS), RUNS), :] = taken
+            inputs[m, s * RUNS : (s + 1) * RUNS, :] = taken
             after.append(leaps[s] * state[s] + taken)
         return tuple(after)
 
@@ -170,16 +179,20 @@
             by *= 2
         begins.append(value)
 
-    def emit(m, state):
+    weights = [spread(weight[s : s + 1]) for s in range(modes)]
+
+    def emit(m, terms):
         values = tokens(gated, m)
+        answers = []
         for n, asked in enumerate(tokens(query, m)):
-            terms = [early[lag] * values[n - lag] for lag in range(n + 1)]
-            terms += [factors[n * modes + s] * state[s] for s in range(modes)]
-            result[pl.ds(m * batch + n, RUNS, stride=steps), :] = asked * tree_sum(terms)
-        at = pl.ds(pl.multiple_of(m * RUNS, RUNS), RUNS)
-        return tuple(leaps[s] * state[s] + inputs[s, at, :] for s in range(modes))
-
-    lax.fori_loop(0, steps // batch, emit, tuple(begins), unroll=4)
+            terms = [p * x for p, x in zip(poles, terms)]
+            close = [early[lag] * values[n - lag] for lag in range(n + 1)]
+            answers.append(asked * tree_sum(close + terms))
+        for n, answer in enumerate(answers):
+            result[pl.ds(m * batch + n, RUNS, stride=steps), :] = answer
+        return tuple(x + w * inputs[m, s * RUNS : (s + 1) * RUNS, :] for s, (w, x) in enumerate(zip(weights, terms)))
+
+    lax.fori_loop(0, steps // batch, emit, tuple(w * x for w, x in zip(weights, begins)), unroll=4)
     for out, hops in zip(outs, sends):
         size = out.shape[0] // len(hops)
         for n, hop in enumerate(hops):
@@ -202,7 +215,7 @@
     floats = lambda *shape: pltpu.VMEM(shape + (LANES,), jnp.float32)
     own = [
         jax.ShapeDtypeStruct(ids.shape, jnp.int32),
-        jax.ShapeDtypeStruct((vocab, 3 * LANES), jnp.bfloat16),
+        jax.ShapeDtypeStruct((vocab // 2, 6 * LANES), jnp.bfloat16),
         jax.ShapeDtypeStruct((3, width, LANES), jnp.float32),
         jax.ShapeDtypeStruct((modes, LANES), jnp.float32),
         jax.ShapeDtypeStruct((modes, LANES), jnp.float32),
@@ -212,14 +225,13 @@
     out_shape = [jax.ShapeDtypeStruct((count, LANES), jnp.bfloat16) for count in rows]
     scratch = []
     if raw:
-        scratch = [pltpu.VMEM(x.shape, x.dtype) for x in own] + [pltpu.SemaphoreType.DMA((2, 8))]
+        scratch = [pltpu.VMEM(x.shape, x.dtype) for x in own] + [pltpu.SemaphoreType.DMA((2, 11))]
         out_shape = out_shape + (own if ahead else [])
     scratch += [
         floats(3, (width - 1) * RUNS),
         floats(length),
         floats(length),
-        floats(modes, steps // batch * RUNS),
-        floats(batch * modes, RUNS),
+        floats(steps // batch, modes * RUNS),
         floats(length),
     ]
     scratch += [floats(3, cols // parts * RUNS)] * parts
@@ -271,6 +283,7 @@
         out_shape=jax.ShapeDtypeStruct((local, places * 2 * kept), arrays[0].dtype),
         scratch_shapes=[pltpu.SemaphoreType.DMA((count,))],
         input_output_aliases={len(arrays): 0} if into else {},
+        cost_estimate=pl.CostEstimate(flops=0, bytes_accessed=2**23, transcendentals=0),
         compiler_params=pltpu.CompilerParams(vmem_limit_bytes=2**20),
     )(*(pltpu.with_memory_space_constraint(x, pltpu.VMEM) for x in arrays), *into)
 
@@ -285,27 +298,27 @@
 
     first, given = run(given, 0, [[d + e for e in range(4)] for d in far])
     landed = first[:1] + [hop(x, d) for x, d in zip(first[1:], far[1:])]
-    (*straight, across), _ = run(given, 1, [[d, d + 1] for d in far] + [[d + e for d in far for e in (2, 3)]])
+    sends = [[d, d + 1] for d in far] + [[d + e for d in far[1:] for e in (2, 3)], [2, 3]]
+    (*straight, across, beside), _ = run(given, 1, sends)
     landed, straight = lax.optimization_barrier((landed, straight))
     crossed = hop(across, 2)
-    final = [
-        hop(jnp.concatenate([straight[n], crossed[2 * n : 2 * n + 2]]), d) for n, d in enumerate(far) if d > 0
-    ]
-    turned = hop(jnp.concatenate([x[2:] for x in landed]), 2)
-    odd = [x[1:2] for x in landed] + [turned[2 * n + 1 : 2 * n + 2] for n in range(len(far))]
+    final = [hop(jnp.concatenate([straight[n], crossed[2 * n - 2 : 2 * n]]), far[n]) for n in range(1, len(far))]
+    turn = jnp.concatenate([x[2:] for x in landed] + [beside])
+    turn, crossed = lax.optimization_barrier((turn, crossed))
+    turned = hop(turn, 2)
+    paired = hop(jnp.concatenate([straight[0][1:2]] + [x[n : n + 1] for x in final for n in (1, 3)]), 1)
     out = run_join(
         places,
-        [(x, [(0, d)]) for x, d in zip(landed, far)]
-        + [(turned, [mark for d in far for mark in ((0, d + 2), None)])]
-        + [(hop(jnp.concatenate(odd), 1), [(0, d + 1) for d in far] + [(0, d + 3) for d in far])],
+        [(straight[0], [(1, 0)])] + [(x, [(1, d), None, (1, d + 2)]) for x, d in zip(final, far[1:])],
         None,
     )
-    odd = [straight[0][1:2], crossed[1:2]] + [x[n : n + 1] for x in final for n in (1, 3)]
+    odd = [x[1:2] for x in landed] + [turned[n : n + 1] for n in range(1, turn.shape[0], 2)]
     return run_join(
         places,
-        [(straight[0], [(1, 0)]), (crossed, [(1, 2)])]
-        + [(x, [(1, d), None, (1, d + 2)]) for x, d in zip(final, far[1:])]
-        + [(hop(jnp.concatenate(odd), 1), [(1, d + e) for d in far for e in (1, 3)])],
+        [(x, [(0, d)]) for x, d in zip(landed, far)]
+        + [(turned, [mark for d in far for mark in ((0, d + 2), None)] + [(1, 2)])]
+        + [(paired, [(1, 1)] + [(1, d + e) for d in far[1:] for e in (1, 3)])]
+        + [(hop(jnp.concatenate(odd), 1), [(0, d + 1) for d in far] + [(0, d + 3) for d in far] + [(1, 3)])],
         out,
     )
 

time: 43 us -> 40.7 us (0.947)
  local copies, waits for them, and re-layouts: 1.63 us -> 0.23 us
  Pallas kernels: 15.6 us -> 14.5 us
    pallas_call x2, Pallas kernels: 13.8 us -> 12.7 us  [run_operator(): pl.pallas_call(functools.partial(operator, (piece, pieces, sends, sliced,...]
    slice x7 -> x1, local copies, waits for them, and re-layouts: 0.86 us -> 0.01 us  [by_hops(): crossed[2 * n - 2:2 * n]]
    unnamed x22 -> x17, local copies, waits for them, and re-layouts: 0.75 us -> 0.18 us
  transfers between devices with their start and end apart: 10 -> 10, of which waited for: 6 -> 4; matrix products, arithmetic and copies ran while one was open for 1% -> 0% of each run, Pallas kernels for 17% -> 16%
where the time goes in v6:
time: 40.7 us; the launch traced here: 40.5 us
  Pallas kernels  14.5 us (36%)
  starting transfers between devices  14.1 us (35%)
  waiting for transfers between devices  11.5 us (28%)
    ppermute x10, starting transfers between devices, by_hops(): lax.ppermute(x, 'seq', [(i, i ^ by) for i in range(places)])  14.1 us
    pallas_call x2, Pallas kernels, run_operator(): pl.pallas_call(functools.partial(operator, (piece, pieces, sends, sliced,...  12.7 us
    ppermute x10, waiting for transfers between devices, by_hops(): lax.ppermute(x, 'seq', [(i, i ^ by) for i in range(places)])  11.5 us
    pallas_call x2, Pallas kernels, run_join(): pl.pallas_call(kernel, in_specs=[anywhere] * (len(arrays) + len(into)), o...  1.83 us
  transfers between devices with their start and end apart: 10, of which 4 were waited for; matrix products, arithmetic and copies ran while one was open for 0% of the time, Pallas kernels for 16%

profile of v6, /device:TPU:0, one launch (start us, length us, event | category | flops | bytes accessed | tf_op | source)
XLA Modules:
  0.0 40.5 jit_solution(16124316918729199723)
XLA Ops:
  0.0 6.9 %shard_map.64 = (bf16[512,128]{1,0:T(8,128)(2,1)S(1)}, bf16[512,128]{1,0:T(8,128)(2,1)S(1)}, bf16[512,128]{1,0:T(8,128)(2,1)S(1)}, bf16[512,128]{1,0:T(8,128)(2,...) custom-call(s32[16,128]{1,0:T(8,128)} %bitcast.34, ...), custom_call_target="tpu_custom_call" | custom-call | flops 2097152000 | bytes 4194304 | tf_op jit(solution)/shard_map/pallas_call | solution.py:240
  6.9 3.1 %collective-permute-start = (bf16[4,128,128]{2,1,0:T(8,128)(2,1)S(1)}, bf16[4,128,128]{2,1,0:T(8,128)(2,1)S(1)}, u32[]{:S(2)}, u32[]{:S(2)}) collective-permute-start(bf16[4,128,128]{2,1,0:T(8,128)(2,1)S(1)} %bitcast.28), channel_id=1, source_target_pairs={{0,4},{1,5},{2,6},{3,7},{4,0},{5,1},{6,2},{7,3},{8,12},{9,13},{10,... | collective-permute-start | bytes 393224 | tf_op jit(solution)/shard_map/ppermute | solution.py:293
  10.0 2.6 %collective-permute-start.1 = (bf16[4,128,128]{2,1,0:T(8,128)(2,1)S(1)}, bf16[4,128,128]{2,1,0:T(8,128)(2,1)S(1)}, u32[]{:S(2)}, u32[]{:S(2)}) collective-permute-start(bf16[4,128,128]{2,1,0:T(8,128)(2,1)S(1)} %bitcast.27), channel_id=1, source_target_pairs={{0,8},{1,9},{2,10},{3,11},{4,12},{5,13},{6,14},{7,15},{8,0},{9,1},... | collective-permute-start | bytes 393224 | tf_op jit(solution)/shard_map/ppermute | solution.py:293
  12.6 0.0 collective-permute-start.2
  12.6 5.8 %shard_map.65 = (bf16[256,128]{1,0:T(8,128)(2,1)S(1)}, bf16[256,128]{1,0:T(8,128)(2,1)S(1)}, bf16[256,128]{1,0:T(8,128)(2,1)S(1)}, bf16[256,128]{1,0:T(8,128)(2,...) custom-call(s32[16,128]{1,0:T(8,128)S(1)} %get-tuple-element.34.refs_0_, ...), custom_call_target="tpu_custom_call" | custom-call | flops 2097152000 | bytes 4194304 | tf_op jit(solution)/shard_map/pallas_call | solution.py:240
  18.4 1.8 %collective-permute-start.3 = (bf16[6,128,128]{2,1,0:T(8,128)(2,1)S(1)}, bf16[6,128,128]{2,1,0:T(8,128)(2,1)S(1)}, u32[]{:S(2)}, u32[]{:S(2)}) collective-permute-start(bf16[6,128,128]{2,1,0:T(8,128)(2,1)S(1)} %bitcast.25), channel_id=1, source_target_pairs={{0,2},{1,3},{2,0},{3,1},{4,6},{5,7},{6,4},{7,5},{8,10},{9,11},{10,... | collective-permute-start | bytes 589832 | tf_op jit(solution)/shard_map/ppermute | solution.py:293
  20.2 0.0 collective-permute-done.refs_1_
  20.2 2.8 %collective-permute-done.1.refs_2_ = bf16[4,128,128]{2,1,0:T(8,128)(2,1)S(1)} collective-permute-done((bf16[4,128,128]{2,1,0:T(8,128)(2,1)S(1)}, bf16[4,128,128]{2,1,0:T(8,128)(2,1)S(1)}, u32[]{:S(2)}, u32[]{:S(2)}) %collective-permute-start.1) | collective-permute-done | bytes 131104 | tf_op jit(solution)/shard_map/ppermute | solution.py:293
  22.9 0.0 collective-permute-done.2.refs_3_
  23.1 1.5 %collective-permute-done.3 = bf16[6,128,128]{2,1,0:T(8,128)(2,1)S(1)} collective-permute-done((bf16[6,128,128]{2,1,0:T(8,128)(2,1)S(1)}, bf16[6,128,128]{2,1,0:T(8,128)(2,1)S(1)}, u32[]{:S(2)}, u32[]{:S(2)}) %collective-permute-start.3) | collective-permute-done | bytes 196640 | tf_op jit(solution)/shard_map/ppermute | solution.py:293
  24.6 0.7 %collective-permute-start.5 = (bf16[4,128,128]{2,1,0:T(8,128)(2,1)S(1)}, bf16[4,128,128]{2,1,0:T(8,128)(2,1)S(1)}, u32[]{:S(2)}, u32[]{:S(2)}) collective-permute-start(bf16[4,128,128]{2,1,0:T(8,128)(2,1)S(1)} %pad_maximum_fusion), channel_id=1, source_target_pairs={{0,4},{1,5},{2,6},{3,7},{4,0},{5,1},{6,2},{7,3},{8,12},{9,13},{10,... | collective-permute-start | bytes 393224 | tf_op jit(solution)/shard_map/ppermute | solution.py:293
  25.3 3.6 %collective-permute-start.6 = (bf16[4,128,128]{2,1,0:T(8,128)(2,1)S(1)}, bf16[4,128,128]{2,1,0:T(8,128)(2,1)S(1)}, u32[]{:S(2)}, u32[]{:S(2)}) collective-permute-start(bf16[4,128,128]{2,1,0:T(8,128)(2,1)S(1)} %pad_maximum_fusion.1), channel_id=1, source_target_pairs={{0,8},{1,9},{2,10},{3,11},{4,12},{5,13},{6,14},{7,15},{8,0},{9,1},... | collective-permute-start | bytes 393224 | tf_op jit(solution)/shard_map/ppermute | solution.py:293
  28.9 0.3 collective-permute-start.7
  29.2 1.5 %collective-permute-start.4 = (bf16[10,128,128]{2,1,0:T(8,128)(2,1)S(1)}, bf16[10,128,128]{2,1,0:T(8,128)(2,1)S(1)}, u32[]{:S(2)}, u32[]{:S(2)}) collective-permute-start(bf16[10,128,128]{2,1,0:T(8,128)(2,1)S(1)} %constant_dynamic-update-slice_fusion), channel_id=1, source_target_pairs={{0,2},{1,3},{2,0},{3,1},{4,6},{5,7},{6,4},{7,5},{8,10},{9,11},{10,... | collective-permute-start | bytes 983048 | tf_op jit(solution)/shard_map/ppermute | solution.py:293
  30.7 0.0 collective-permute-done.5.refs_1_
  30.7 6.6 %collective-permute-done.6.refs_2_ = bf16[4,128,128]{2,1,0:T(8,128)(2,1)S(1)} collective-permute-done((bf16[4,128,128]{2,1,0:T(8,128)(2,1)S(1)}, bf16[4,128,128]{2,1,0:T(8,128)(2,1)S(1)}, u32[]{:S(2)}, u32[]{:S(2)}) %collective-permute-start.6) | collective-permute-done | bytes 131104 | tf_op jit(solution)/shard_map/ppermute | solution.py:293
  37.4 0.0 collective-permute-done.7.refs_3_
  37.4 0.0 collective-permute-done.4.refs_4_
  37.5 0.1 collective-permute-start.9
  37.6 0.5 %collective-permute-start.8 = (bf16[7,128,128]{2,1,0:T(8,128)(2,1)S(1)}, bf16[7,128,128]{2,1,0:T(8,128)(2,1)S(1)}, u32[]{:S(2)}, u32[]{:S(2)}) collective-permute-start(bf16[7,128,128]{2,1,0:T(8,128)(2,1)S(1)} %constant_dynamic-update-slice_fusion.1), channel_id=1, source_target_pairs={{0,1},{1,0},{2,3},{3,2},{4,5},{5,4},{6,7},{7,6},{8,9},{9,8},{10,11... | collective-permute-start | bytes 688136 | tf_op jit(solution)/shard_map/ppermute | solution.py:293
  38.0 0.7 %shard_map.66.refs_7_ = bf16[128,4096]{1,0:T(8,128)(2,1)} custom-call(bf16[2,128,128]{2,1,0:T(8,128)(2,1)S(1)} %bitcast.20, bf16[4,128,128]{2,1,0:T(8,128)(2,1)S(1)} %collective-permute-done.5.refs_1_, bf16[4,128,128]{2,1,0:T(8,128)(2,1)S(1)} %collective-permute-done.6.refs_2_, bf16[4,128,128]{2,1,0:T(8,128)(2,1)S(1)} %collective-permute-done.7.refs_3_), custom_call_target="tpu_custom_call" | custom-call | bytes 8388608 | tf_op jit(solution)/shard_map/pallas_call | solution.py:279
  38.8 0.6 %collective-permute-done.8.refs_5_ = bf16[7,128,128]{2,1,0:T(8,128)(2,1)S(1)} collective-permute-done((bf16[7,128,128]{2,1,0:T(8,128)(2,1)S(1)}, bf16[7,128,128]{2,1,0:T(8,128)(2,1)S(1)}, u32[]{:S(2)}, u32[]{:S(2)}) %collective-permute-start.8) | collective-permute-done | bytes 229408 | tf_op jit(solution)/shard_map/ppermute | solution.py:293
  39.4 0.0 collective-permute-done.9.refs_6_
  39.4 1.1 %shard_map.67 = bf16[128,4096]{1,0:T(8,128)(2,1)} custom-call(bf16[4,128,128]{2,1,0:T(8,128)(2,1)S(1)} %bitcast.18, bf16[4,128,128]{2,1,0:T(8,128)(2,1)S(1)} %collective-permute-done.refs_1_, bf16[4,128,128]{2,1,0:T(8,128)(2,1)S(1)} %collective-permute-done.1.refs_2_, ...), custom_call_target="tpu_custom_call", output_to_operand_aliasing={{}: (7, {})} | custom-call | bytes 8388608 | tf_op jit(solution)/shard_map/pallas_call | solution.py:279
  (24 shorter events, 0.3 us)
Async XLA Ops:
  6.9 13.3 %collective-permute-start = (bf16[4,128,128]{2,1,0:T(8,128)(2,1)S(1)}, bf16[4,128,128]{2,1,0:T(8,128)(2,1)S(1)}, u32[]{:S(2)}, u32[]{:S(2)}) collective-permute-start(bf16[4,128,128]{2,1,0:T(8,128)(2,1)S(1)} %bitcast.28), channel_id=1, source_target_pairs={{0,4},{1,5},{2,6},{3,7},{4,0},{5,1},{6,2},{7,3},{8,12},{9,13},{10,... | collective-permute-start | bytes 393224 | tf_op jit(solution)/shard_map/ppermute | solution.py:293
  10.0 12.9 %collective-permute-start.1 = (bf16[4,128,128]{2,1,0:T(8,128)(2,1)S(1)}, bf16[4,128,128]{2,1,0:T(8,128)(2,1)S(1)}, u32[]{:S(2)}, u32[]{:S(2)}) collective-permute-start(bf16[4,128,128]{2,1,0:T(8,128)(2,1)S(1)} %bitcast.27), channel_id=1, source_target_pairs={{0,8},{1,9},{2,10},{3,11},{4,12},{5,13},{6,14},{7,15},{8,0},{9,1},... | collective-permute-start | bytes 393224 | tf_op jit(solution)/shard_map/ppermute | solution.py:293
  12.6 10.3 %collective-permute-start.2 = (bf16[4,128,128]{2,1,0:T(8,128)(2,1)S(1)}, bf16[4,128,128]{2,1,0:T(8,128)(2,1)S(1)}, u32[]{:S(2)}, u32[]{:S(2)}) collective-permute-start(bf16[4,128,128]{2,1,0:T(8,128)(2,1)S(1)} %bitcast.26), channel_id=1, source_target_pairs={{0,12},{1,13},{2,14},{3,15},{4,8},{5,9},{6,10},{7,11},{8,4},{9,5},... | collective-permute-start | bytes 393224 | tf_op jit(solution)/shard_map/ppermute | solution.py:293
  18.4 6.2 %collective-permute-start.3 = (bf16[6,128,128]{2,1,0:T(8,128)(2,1)S(1)}, bf16[6,128,128]{2,1,0:T(8,128)(2,1)S(1)}, u32[]{:S(2)}, u32[]{:S(2)}) collective-permute-start(bf16[6,128,128]{2,1,0:T(8,128)(2,1)S(1)} %bitcast.25), channel_id=1, source_target_pairs={{0,2},{1,3},{2,0},{3,1},{4,6},{5,7},{6,4},{7,5},{8,10},{9,11},{10,... | collective-permute-start | bytes 589832 | tf_op jit(solution)/shard_map/ppermute | solution.py:293
  24.6 6.1 %collective-permute-start.5 = (bf16[4,128,128]{2,1,0:T(8,128)(2,1)S(1)}, bf16[4,128,128]{2,1,0:T(8,128)(2,1)S(1)}, u32[]{:S(2)}, u32[]{:S(2)}) collective-permute-start(bf16[4,128,128]{2,1,0:T(8,128)(2,1)S(1)} %pad_maximum_fusion), channel_id=1, source_target_pairs={{0,4},{1,5},{2,6},{3,7},{4,0},{5,1},{6,2},{7,3},{8,12},{9,13},{10,... | collective-permute-start | bytes 393224 | tf_op jit(solution)/shard_map/ppermute | solution.py:293
  25.3 12.0 %collective-permute-start.6 = (bf16[4,128,128]{2,1,0:T(8,128)(2,1)S(1)}, bf16[4,128,128]{2,1,0:T(8,128)(2,1)S(1)}, u32[]{:S(2)}, u32[]{:S(2)}) collective-permute-start(bf16[4,128,128]{2,1,0:T(8,128)(2,1)S(1)} %pad_maximum_fusion.1), channel_id=1, source_target_pairs={{0,8},{1,9},{2,10},{3,11},{4,12},{5,13},{6,14},{7,15},{8,0},{9,1},... | collective-permute-start | bytes 393224 | tf_op jit(solution)/shard_map/ppermute | solution.py:293
  28.9 8.5 %collective-permute-start.7 = (bf16[4,128,128]{2,1,0:T(8,128)(2,1)S(1)}, bf16[4,128,128]{2,1,0:T(8,128)(2,1)S(1)}, u32[]{:S(2)}, u32[]{:S(2)}) collective-permute-start(bf16[4,128,128]{2,1,0:T(8,128)(2,1)S(1)} %pad_maximum_fusion.2), channel_id=1, source_target_pairs={{0,12},{1,13},{2,14},{3,15},{4,8},{5,9},{6,10},{7,11},{8,4},{9,5},... | collective-permute-start | bytes 393224 | tf_op jit(solution)/shard_map/ppermute | solution.py:293
  29.2 8.2 %collective-permute-start.4 = (bf16[10,128,128]{2,1,0:T(8,128)(2,1)S(1)}, bf16[10,128,128]{2,1,0:T(8,128)(2,1)S(1)}, u32[]{:S(2)}, u32[]{:S(2)}) collective-permute-start(bf16[10,128,128]{2,1,0:T(8,128)(2,1)S(1)} %constant_dynamic-update-slice_fusion), channel_id=1, source_target_pairs={{0,2},{1,3},{2,0},{3,1},{4,6},{5,7},{6,4},{7,5},{8,10},{9,11},{10,... | collective-permute-start | bytes 983048 | tf_op jit(solution)/shard_map/ppermute | solution.py:293
  37.5 2.0 %collective-permute-start.9 = (bf16[9,128,128]{2,1,0:T(8,128)(2,1)S(1)}, bf16[9,128,128]{2,1,0:T(8,128)(2,1)S(1)}, u32[]{:S(2)}, u32[]{:S(2)}) collective-permute-start(bf16[9,128,128]{2,1,0:T(8,128)(2,1)S(1)} %constant_dynamic-update-slice_fusion.8), channel_id=1, source_target_pairs={{0,1},{1,0},{2,3},{3,2},{4,5},{5,4},{6,7},{7,6},{8,9},{9,8},{10,11... | collective-permute-start | bytes 884744 | tf_op jit(solution)/shard_map/ppermute | solution.py:293
  37.6 1.9 %collective-permute-start.8 = (bf16[7,128,128]{2,1,0:T(8,128)(2,1)S(1)}, bf16[7,128,128]{2,1,0:T(8,128)(2,1)S(1)}, u32[]{:S(2)}, u32[]{:S(2)}) collective-permute-start(bf16[7,128,128]{2,1,0:T(8,128)(2,1)S(1)} %constant_dynamic-update-slice_fusion.1), channel_id=1, source_target_pairs={{0,1},{1,0},{2,3},{3,2},{4,5},{5,4},{6,7},{7,6},{8,9},{9,8},{10,11... | collective-permute-start | bytes 688136 | tf_op jit(solution)/shard_map/ppermute | solution.py:293

commit v7 on v6

--- a/solution.py
+++ b/solution.py
@@ -50,10 +50,12 @@
 
         now = bring(piece, held, 0)
         later = bring(piece + 1, ahead, 1) if ahead else []
-        for copy in now + later:
+        for copy in now:
             copy.start()
         for copy in now:
             copy.wait()
+        for copy in later:
+            copy.start()
     else:
         held, later = given, []
     compute(place, sends, held, outs, *refs)
@@ -61,7 +63,7 @@
         copy.wait()
 
 
-def compute(place, sends, held, outs, halo, query, gated, inputs, result, *streams):
+def compute(place, sends, held, outs, halo, query, gated, inputs, gains, result, *streams):
     ids, table, taps, residue, decay, skip = held
     length = ids.shape[0] * ids.shape[1]
     steps = length // RUNS
@@ -140,6 +142,7 @@
     lax.fori_loop(0, steps // cols, block_step, 0)
 
     batch = steps // inputs.shape[0]
+    unroll = max(32 // batch, 1)
     rate = decay[...] / length
     weight = residue[...] * jnp.sqrt(2.0 * rate)
     pole = jnp.exp(-rate)
@@ -169,7 +172,7 @@
         return tuple(after)
 
     zero = jnp.zeros(tile, jnp.float32)
-    ends = lax.fori_loop(0, steps // batch, advance, (zero,) * modes, unroll=4)
+    ends = lax.fori_loop(0, steps // batch, advance, (zero,) * modes, unroll=unroll)
     begins = []
     for s in range(modes):
         value = delay_runs(ends[s], 1)
@@ -180,6 +183,8 @@
         begins.append(value)
 
     weights = [spread(weight[s : s + 1]) for s in range(modes)]
+    for s in range(modes):
+        gains[s] = weights[s]
 
     def emit(m, terms):
         values = tokens(gated, m)
@@ -190,9 +195,9 @@
             answers.append(asked * tree_sum(close + terms))
         for n, answer in enumerate(answers):
             result[pl.ds(m * batch + n, RUNS, stride=steps), :] = answer
-        return tuple(x + w * inputs[m, s * RUNS : (s + 1) * RUNS, :] for s, (w, x) in enumerate(zip(weights, terms)))
-
-    lax.fori_loop(0, steps // batch, emit, tuple(w * x for w, x in zip(weights, begins)), unroll=4)
+        return tuple(x + gains[s] * inputs[m, s * RUNS : (s + 1) * RUNS, :] for s, x in enumerate(terms))
+
+    lax.fori_loop(0, steps // batch, emit, tuple(w * x for w, x in zip(weights, begins)), unroll=unroll)
     for out, hops in zip(outs, sends):
         size = out.shape[0] // len(hops)
         for n, hop in enumerate(hops):
@@ -232,6 +237,7 @@
         floats(length),
         floats(length),
         floats(steps // batch, modes * RUNS),
+        floats(modes, RUNS),
         floats(length),
     ]
     scratch += [floats(3, cols // parts * RUNS)] * parts
@@ -297,12 +303,15 @@
         return [x.reshape(-1, local, x.shape[-1]) for x in results], ahead
 
     first, given = run(given, 0, [[d + e for e in range(4)] for d in far])
-    landed = first[:1] + [hop(x, d) for x, d in zip(first[1:], far[1:])]
+    landed = [hop(x, d) for x, d in zip(first[:0:-1], far[:0:-1])]
+    landed = first[:1] + landed[::-1]
     sends = [[d, d + 1] for d in far] + [[d + e for d in far[1:] for e in (2, 3)], [2, 3]]
     (*straight, across, beside), _ = run(given, 1, sends)
     landed, straight = lax.optimization_barrier((landed, straight))
     crossed = hop(across, 2)
-    final = [hop(jnp.concatenate([straight[n], crossed[2 * n - 2 : 2 * n]]), far[n]) for n in range(1, len(far))]
+    final = [
+        hop(jnp.concatenate([straight[n], crossed[2 * n - 2 : 2 * n]]), far[n]) for n in range(len(far) - 1, 0, -1)
+    ][::-1]
     turn = jnp.concatenate([x[2:] for x in landed] + [beside])
     turn, crossed = lax.optimization_barrier((turn, crossed))
     turned = hop(turn, 2)

time: 40.7 us -> 40.5 us (level)
  no operation moved by 1% of the time
where the time goes in v7:
time: 40.5 us; the launch traced here: 40.4 us
  Pallas kernels  14.4 us (36%)
  starting transfers between devices  14.1 us (35%)
  waiting for transfers between devices  11.5 us (28%)
    ppermute x10, starting transfers between devices, by_hops(): lax.ppermute(x, 'seq', [(i, i ^ by) for i in range(places)])  14.1 us
    pallas_call x2, Pallas kernels, run_operator(): pl.pallas_call(functools.partial(operator, (piece, pieces, sends, sliced,...  12.5 us
    ppermute x10, waiting for transfers between devices, by_hops(): lax.ppermute(x, 'seq', [(i, i ^ by) for i in range(places)])  11.5 us
    pallas_call x2, Pallas kernels, run_join(): pl.pallas_call(kernel, in_specs=[anywhere] * (len(arrays) + len(into)), o...  1.83 us
  transfers between devices with their start and end apart: 10, of which 4 were waited for; matrix products, arithmetic and copies ran while one was open for 0% of the time, Pallas kernels for 16%

profile of v7, /device:TPU:0, one launch (start us, length us, event | category | flops | bytes accessed | tf_op | source)
XLA Modules:
  0.0 40.4 jit_solution(6627532654912030478)
XLA Ops:
  0.0 6.8 %shard_map.64 = (bf16[512,128]{1,0:T(8,128)(2,1)S(1)}, bf16[512,128]{1,0:T(8,128)(2,1)S(1)}, bf16[512,128]{1,0:T(8,128)(2,1)S(1)}, bf16[512,128]{1,0:T(8,128)(2,...) custom-call(s32[16,128]{1,0:T(8,128)} %bitcast.34, ...), custom_call_target="tpu_custom_call" | custom-call | flops 2097152000 | bytes 4194304 | tf_op jit(solution)/shard_map/pallas_call | solution.py:246
  6.8 3.1 %collective-permute-start = (bf16[4,128,128]{2,1,0:T(8,128)(2,1)S(1)}, bf16[4,128,128]{2,1,0:T(8,128)(2,1)S(1)}, u32[]{:S(2)}, u32[]{:S(2)}) collective-permute-start(bf16[4,128,128]{2,1,0:T(8,128)(2,1)S(1)} %bitcast.28), channel_id=1, source_target_pairs={{0,4},{1,5},{2,6},{3,7},{4,0},{5,1},{6,2},{7,3},{8,12},{9,13},{10,... | collective-permute-start | bytes 393224 | tf_op jit(solution)/shard_map/ppermute | solution.py:299
  9.9 2.6 %collective-permute-start.1 = (bf16[4,128,128]{2,1,0:T(8,128)(2,1)S(1)}, bf16[4,128,128]{2,1,0:T(8,128)(2,1)S(1)}, u32[]{:S(2)}, u32[]{:S(2)}) collective-permute-start(bf16[4,128,128]{2,1,0:T(8,128)(2,1)S(1)} %bitcast.27), channel_id=1, source_target_pairs={{0,8},{1,9},{2,10},{3,11},{4,12},{5,13},{6,14},{7,15},{8,0},{9,1},... | collective-permute-start | bytes 393224 | tf_op jit(solution)/shard_map/ppermute | solution.py:299
  12.5 0.0 collective-permute-start.2
  12.5 5.8 %shard_map.65 = (bf16[256,128]{1,0:T(8,128)(2,1)S(1)}, bf16[256,128]{1,0:T(8,128)(2,1)S(1)}, bf16[256,128]{1,0:T(8,128)(2,1)S(1)}, bf16[256,128]{1,0:T(8,128)(2,...) custom-call(s32[16,128]{1,0:T(8,128)S(1)} %get-tuple-element.34.refs_0_, ...), custom_call_target="tpu_custom_call" | custom-call | flops 2097152000 | bytes 4194304 | tf_op jit(solution)/shard_map/pallas_call | solution.py:246
  18.2 1.8 %collective-permute-start.3 = (bf16[6,128,128]{2,1,0:T(8,128)(2,1)S(1)}, bf16[6,128,128]{2,1,0:T(8,128)(2,1)S(1)}, u32[]{:S(2)}, u32[]{:S(2)}) collective-permute-start(bf16[6,128,128]{2,1,0:T(8,128)(2,1)S(1)} %bitcast.25), channel_id=1, source_target_pairs={{0,2},{1,3},{2,0},{3,1},{4,6},{5,7},{6,4},{7,5},{8,10},{9,11},{10,... | collective-permute-start | bytes 589832 | tf_op jit(solution)/shard_map/ppermute | solution.py:299
  20.0 0.0 collective-permute-done.refs_1_
  20.0 2.8 %collective-permute-done.1.refs_2_ = bf16[4,128,128]{2,1,0:T(8,128)(2,1)S(1)} collective-permute-done((bf16[4,128,128]{2,1,0:T(8,128)(2,1)S(1)}, bf16[4,128,128]{2,1,0:T(8,128)(2,1)S(1)}, u32[]{:S(2)}, u32[]{:S(2)}) %collective-permute-start.1) | collective-permute-done | bytes 131104 | tf_op jit(solution)/shard_map/ppermute | solution.py:299
  22.8 0.0 collective-permute-done.2.refs_3_
  22.9 1.4 %collective-permute-done.3 = bf16[6,128,128]{2,1,0:T(8,128)(2,1)S(1)} collective-permute-done((bf16[6,128,128]{2,1,0:T(8,128)(2,1)S(1)}, bf16[6,128,128]{2,1,0:T(8,128)(2,1)S(1)}, u32[]{:S(2)}, u32[]{:S(2)}) %collective-permute-start.3) | collective-permute-done | bytes 196640 | tf_op jit(solution)/shard_map/ppermute | solution.py:299
  24.4 0.7 %collective-permute-start.5 = (bf16[4,128,128]{2,1,0:T(8,128)(2,1)S(1)}, bf16[4,128,128]{2,1,0:T(8,128)(2,1)S(1)}, u32[]{:S(2)}, u32[]{:S(2)}) collective-permute-start(bf16[4,128,128]{2,1,0:T(8,128)(2,1)S(1)} %pad_maximum_fusion), channel_id=1, source_target_pairs={{0,4},{1,5},{2,6},{3,7},{4,0},{5,1},{6,2},{7,3},{8,12},{9,13},{10,... | collective-permute-start | bytes 393224 | tf_op jit(solution)/shard_map/ppermute | solution.py:299
  25.1 3.6 %collective-permute-start.6 = (bf16[4,128,128]{2,1,0:T(8,128)(2,1)S(1)}, bf16[4,128,128]{2,1,0:T(8,128)(2,1)S(1)}, u32[]{:S(2)}, u32[]{:S(2)}) collective-permute-start(bf16[4,128,128]{2,1,0:T(8,128)(2,1)S(1)} %pad_maximum_fusion.1), channel_id=1, source_target_pairs={{0,8},{1,9},{2,10},{3,11},{4,12},{5,13},{6,14},{7,15},{8,0},{9,1},... | collective-permute-start | bytes 393224 | tf_op jit(solution)/shard_map/ppermute | solution.py:299
  28.7 0.3 collective-permute-start.7
  29.0 1.5 %collective-permute-start.4 = (bf16[10,128,128]{2,1,0:T(8,128)(2,1)S(1)}, bf16[10,128,128]{2,1,0:T(8,128)(2,1)S(1)}, u32[]{:S(2)}, u32[]{:S(2)}) collective-permute-start(bf16[10,128,128]{2,1,0:T(8,128)(2,1)S(1)} %constant_dynamic-update-slice_fusion), channel_id=1, source_target_pairs={{0,2},{1,3},{2,0},{3,1},{4,6},{5,7},{6,4},{7,5},{8,10},{9,11},{10,... | collective-permute-start | bytes 983048 | tf_op jit(solution)/shard_map/ppermute | solution.py:299
  30.5 0.0 collective-permute-done.5.refs_1_
  30.6 6.6 %collective-permute-done.6.refs_2_ = bf16[4,128,128]{2,1,0:T(8,128)(2,1)S(1)} collective-permute-done((bf16[4,128,128]{2,1,0:T(8,128)(2,1)S(1)}, bf16[4,128,128]{2,1,0:T(8,128)(2,1)S(1)}, u32[]{:S(2)}, u32[]{:S(2)}) %collective-permute-start.6) | collective-permute-done | bytes 131104 | tf_op jit(solution)/shard_map/ppermute | solution.py:299
  37.2 0.0 collective-permute-done.7.refs_3_
  37.2 0.0 collective-permute-done.4.refs_4_
  37.3 0.1 collective-permute-start.9
  37.4 0.5 %collective-permute-start.8 = (bf16[7,128,128]{2,1,0:T(8,128)(2,1)S(1)}, bf16[7,128,128]{2,1,0:T(8,128)(2,1)S(1)}, u32[]{:S(2)}, u32[]{:S(2)}) collective-permute-start(bf16[7,128,128]{2,1,0:T(8,128)(2,1)S(1)} %constant_dynamic-update-slice_fusion.1), channel_id=1, source_target_pairs={{0,1},{1,0},{2,3},{3,2},{4,5},{5,4},{6,7},{7,6},{8,9},{9,8},{10,11... | collective-permute-start | bytes 688136 | tf_op jit(solution)/shard_map/ppermute | solution.py:299
  37.9 0.7 %shard_map.66.refs_7_ = bf16[128,4096]{1,0:T(8,128)(2,1)} custom-call(bf16[2,128,128]{2,1,0:T(8,128)(2,1)S(1)} %bitcast.20, bf16[4,128,128]{2,1,0:T(8,128)(2,1)S(1)} %collective-permute-done.5.refs_1_, bf16[4,128,128]{2,1,0:T(8,128)(2,1)S(1)} %collective-permute-done.6.refs_2_, bf16[4,128,128]{2,1,0:T(8,128)(2,1)S(1)} %collective-permute-done.7.refs_3_), custom_call_target="tpu_custom_call" | custom-call | bytes 8388608 | tf_op jit(solution)/shard_map/pallas_call | solution.py:285
  38.6 0.6 %collective-permute-done.8.refs_5_ = bf16[7,128,128]{2,1,0:T(8,128)(2,1)S(1)} collective-permute-done((bf16[7,128,128]{2,1,0:T(8,128)(2,1)S(1)}, bf16[7,128,128]{2,1,0:T(8,128)(2,1)S(1)}, u32[]{:S(2)}, u32[]{:S(2)}) %collective-permute-start.8) | collective-permute-done | bytes 229408 | tf_op jit(solution)/shard_map/ppermute | solution.py:299
  39.3 0.0 collective-permute-done.9.refs_6_
  39.3 1.1 %shard_map.67 = bf16[128,4096]{1,0:T(8,128)(2,1)} custom-call(bf16[4,128,128]{2,1,0:T(8,128)(2,1)S(1)} %bitcast.18, bf16[4,128,128]{2,1,0:T(8,128)(2,1)S(1)} %collective-permute-done.refs_1_, bf16[4,128,128]{2,1,0:T(8,128)(2,1)S(1)} %collective-permute-done.1.refs_2_, ...), custom_call_target="tpu_custom_call", output_to_operand_aliasing={{}: (7, {})} | custom-call | bytes 8388608 | tf_op jit(solution)/shard_map/pallas_call | solution.py:285
  (24 shorter events, 0.3 us)
Async XLA Ops:
  6.8 13.2 %collective-permute-start = (bf16[4,128,128]{2,1,0:T(8,128)(2,1)S(1)}, bf16[4,128,128]{2,1,0:T(8,128)(2,1)S(1)}, u32[]{:S(2)}, u32[]{:S(2)}) collective-permute-start(bf16[4,128,128]{2,1,0:T(8,128)(2,1)S(1)} %bitcast.28), channel_id=1, source_target_pairs={{0,4},{1,5},{2,6},{3,7},{4,0},{5,1},{6,2},{7,3},{8,12},{9,13},{10,... | collective-permute-start | bytes 393224 | tf_op jit(solution)/shard_map/ppermute | solution.py:299
  9.9 12.9 %collective-permute-start.1 = (bf16[4,128,128]{2,1,0:T(8,128)(2,1)S(1)}, bf16[4,128,128]{2,1,0:T(8,128)(2,1)S(1)}, u32[]{:S(2)}, u32[]{:S(2)}) collective-permute-start(bf16[4,128,128]{2,1,0:T(8,128)(2,1)S(1)} %bitcast.27), channel_id=1, source_target_pairs={{0,8},{1,9},{2,10},{3,11},{4,12},{5,13},{6,14},{7,15},{8,0},{9,1},... | collective-permute-start | bytes 393224 | tf_op jit(solution)/shard_map/ppermute | solution.py:299
  12.5 10.3 %collective-permute-start.2 = (bf16[4,128,128]{2,1,0:T(8,128)(2,1)S(1)}, bf16[4,128,128]{2,1,0:T(8,128)(2,1)S(1)}, u32[]{:S(2)}, u32[]{:S(2)}) collective-permute-start(bf16[4,128,128]{2,1,0:T(8,128)(2,1)S(1)} %bitcast.26), channel_id=1, source_target_pairs={{0,12},{1,13},{2,14},{3,15},{4,8},{5,9},{6,10},{7,11},{8,4},{9,5},... | collective-permute-start | bytes 393224 | tf_op jit(solution)/shard_map/ppermute | solution.py:299
  18.2 6.1 %collective-permute-start.3 = (bf16[6,128,128]{2,1,0:T(8,128)(2,1)S(1)}, bf16[6,128,128]{2,1,0:T(8,128)(2,1)S(1)}, u32[]{:S(2)}, u32[]{:S(2)}) collective-permute-start(bf16[6,128,128]{2,1,0:T(8,128)(2,1)S(1)} %bitcast.25), channel_id=1, source_target_pairs={{0,2},{1,3},{2,0},{3,1},{4,6},{5,7},{6,4},{7,5},{8,10},{9,11},{10,... | collective-permute-start | bytes 589832 | tf_op jit(solution)/shard_map/ppermute | solution.py:299
  24.4 6.1 %collective-permute-start.5 = (bf16[4,128,128]{2,1,0:T(8,128)(2,1)S(1)}, bf16[4,128,128]{2,1,0:T(8,128)(2,1)S(1)}, u32[]{:S(2)}, u32[]{:S(2)}) collective-permute-start(bf16[4,128,128]{2,1,0:T(8,128)(2,1)S(1)} %pad_maximum_fusion), channel_id=1, source_target_pairs={{0,4},{1,5},{2,6},{3,7},{4,0},{5,1},{6,2},{7,3},{8,12},{9,13},{10,... | collective-permute-start | bytes 393224 | tf_op jit(solution)/shard_map/ppermute | solution.py:299
  25.1 12.0 %collective-permute-start.6 = (bf16[4,128,128]{2,1,0:T(8,128)(2,1)S(1)}, bf16[4,128,128]{2,1,0:T(8,128)(2,1)S(1)}, u32[]{:S(2)}, u32[]{:S(2)}) collective-permute-start(bf16[4,128,128]{2,1,0:T(8,128)(2,1)S(1)} %pad_maximum_fusion.1), channel_id=1, source_target_pairs={{0,8},{1,9},{2,10},{3,11},{4,12},{5,13},{6,14},{7,15},{8,0},{9,1},... | collective-permute-start | bytes 393224 | tf_op jit(solution)/shard_map/ppermute | solution.py:299
  28.7 8.5 %collective-permute-start.7 = (bf16[4,128,128]{2,1,0:T(8,128)(2,1)S(1)}, bf16[4,128,128]{2,1,0:T(8,128)(2,1)S(1)}, u32[]{:S(2)}, u32[]{:S(2)}) collective-permute-start(bf16[4,128,128]{2,1,0:T(8,128)(2,1)S(1)} %pad_maximum_fusion.2), channel_id=1, source_target_pairs={{0,12},{1,13},{2,14},{3,15},{4,8},{5,9},{6,10},{7,11},{8,4},{9,5},... | collective-permute-start | bytes 393224 | tf_op jit(solution)/shard_map/ppermute | solution.py:299
  29.0 8.2 %collective-permute-start.4 = (bf16[10,128,128]{2,1,0:T(8,128)(2,1)S(1)}, bf16[10,128,128]{2,1,0:T(8,128)(2,1)S(1)}, u32[]{:S(2)}, u32[]{:S(2)}) collective-permute-start(bf16[10,128,128]{2,1,0:T(8,128)(2,1)S(1)} %constant_dynamic-update-slice_fusion), channel_id=1, source_target_pairs={{0,2},{1,3},{2,0},{3,1},{4,6},{5,7},{6,4},{7,5},{8,10},{9,11},{10,... | collective-permute-start | bytes 983048 | tf_op jit(solution)/shard_map/ppermute | solution.py:299
  37.3 2.0 %collective-permute-start.9 = (bf16[9,128,128]{2,1,0:T(8,128)(2,1)S(1)}, bf16[9,128,128]{2,1,0:T(8,128)(2,1)S(1)}, u32[]{:S(2)}, u32[]{:S(2)}) collective-permute-start(bf16[9,128,128]{2,1,0:T(8,128)(2,1)S(1)} %constant_dynamic-update-slice_fusion.8), channel_id=1, source_target_pairs={{0,1},{1,0},{2,3},{3,2},{4,5},{5,4},{6,7},{7,6},{8,9},{9,8},{10,11... | collective-permute-start | bytes 884744 | tf_op jit(solution)/shard_map/ppermute | solution.py:299
  37.4 1.9 %collective-permute-start.8 = (bf16[7,128,128]{2,1,0:T(8,128)(2,1)S(1)}, bf16[7,128,128]{2,1,0:T(8,128)(2,1)S(1)}, u32[]{:S(2)}, u32[]{:S(2)}) collective-permute-start(bf16[7,128,128]{2,1,0:T(8,128)(2,1)S(1)} %constant_dynamic-update-slice_fusion.1), channel_id=1, source_target_pairs={{0,1},{1,0},{2,3},{3,2},{4,5},{5,4},{6,7},{7,6},{8,9},{9,8},{10,11... | collective-permute-start | bytes 688136 | tf_op jit(solution)/shard_map/ppermute | solution.py:299

commit v8 on v7

--- a/solution.py
+++ b/solution.py
@@ -318,14 +318,15 @@
     paired = hop(jnp.concatenate([straight[0][1:2]] + [x[n : n + 1] for x in final for n in (1, 3)]), 1)
     out = run_join(
         places,
-        [(straight[0], [(1, 0)])] + [(x, [(1, d), None, (1, d + 2)]) for x, d in zip(final, far[1:])],
+        [(x, [(0, d)]) for x, d in zip(landed, far)]
+        + [(straight[0], [(1, 0)])]
+        + [(x, [(1, d), None, (1, d + 2)]) for x, d in zip(final, far[1:])],
         None,
     )
     odd = [x[1:2] for x in landed] + [turned[n : n + 1] for n in range(1, turn.shape[0], 2)]
     return run_join(
         places,
-        [(x, [(0, d)]) for x, d in zip(landed, far)]
-        + [(turned, [mark for d in far for mark in ((0, d + 2), None)] + [(1, 2)])]
+        [(turned, [mark for d in far for mark in ((0, d + 2), None)] + [(1, 2)])]
         + [(paired, [(1, 1)] + [(1, d + e) for d in far[1:] for e in (1, 3)])]
         + [(hop(jnp.concatenate(odd), 1), [(0, d + 1) for d in far] + [(0, d + 3) for d in far] + [(1, 3)])],
         out,

time: 40.5 us -> 40.5 us (level)
  no operation moved by 1% of the time
where the time goes in v8:
time: 40.5 us; the launch traced here: 40.3 us
  Pallas kernels  14.4 us (36%)
  starting transfers between devices  14.1 us (35%)
  waiting for transfers between devices  11.4 us (28%)
    ppermute x10, starting transfers between devices, by_hops(): lax.ppermute(x, 'seq', [(i, i ^ by) for i in range(places)])  14.1 us
    pallas_call x2, Pallas kernels, run_operator(): pl.pallas_call(functools.partial(operator, (piece, pieces, sends, sliced,...  12.5 us
    ppermute x10, waiting for transfers between devices, by_hops(): lax.ppermute(x, 'seq', [(i, i ^ by) for i in range(places)])  11.4 us
    pallas_call x2, Pallas kernels, run_join(): pl.pallas_call(kernel, in_specs=[anywhere] * (len(arrays) + len(into)), o...  1.83 us
  transfers between devices with their start and end apart: 10, of which 4 were waited for; matrix products, arithmetic and copies ran while one was open for 0% of the time, Pallas kernels for 16%

profile of v8, /device:TPU:0, one launch (start us, length us, event | category | flops | bytes accessed | tf_op | source)
XLA Modules:
  0.0 40.3 jit_solution(11808248399606438618)
XLA Ops:
  0.0 6.8 %shard_map.64 = (bf16[512,128]{1,0:T(8,128)(2,1)S(1)}, bf16[512,128]{1,0:T(8,128)(2,1)S(1)}, bf16[512,128]{1,0:T(8,128)(2,1)S(1)}, bf16[512,128]{1,0:T(8,128)(2,...) custom-call(s32[16,128]{1,0:T(8,128)} %bitcast.34, ...), custom_call_target="tpu_custom_call" | custom-call | flops 2097152000 | bytes 4194304 | tf_op jit(solution)/shard_map/pallas_call | solution.py:246
  6.8 3.1 %collective-permute-start = (bf16[4,128,128]{2,1,0:T(8,128)(2,1)S(1)}, bf16[4,128,128]{2,1,0:T(8,128)(2,1)S(1)}, u32[]{:S(2)}, u32[]{:S(2)}) collective-permute-start(bf16[4,128,128]{2,1,0:T(8,128)(2,1)S(1)} %bitcast.28), channel_id=1, source_target_pairs={{0,4},{1,5},{2,6},{3,7},{4,0},{5,1},{6,2},{7,3},{8,12},{9,13},{10,... | collective-permute-start | bytes 393224 | tf_op jit(solution)/shard_map/ppermute | solution.py:299
  9.9 2.6 %collective-permute-start.1 = (bf16[4,128,128]{2,1,0:T(8,128)(2,1)S(1)}, bf16[4,128,128]{2,1,0:T(8,128)(2,1)S(1)}, u32[]{:S(2)}, u32[]{:S(2)}) collective-permute-start(bf16[4,128,128]{2,1,0:T(8,128)(2,1)S(1)} %bitcast.27), channel_id=1, source_target_pairs={{0,8},{1,9},{2,10},{3,11},{4,12},{5,13},{6,14},{7,15},{8,0},{9,1},... | collective-permute-start | bytes 393224 | tf_op jit(solution)/shard_map/ppermute | solution.py:299
  12.5 0.0 collective-permute-start.2
  12.5 5.8 %shard_map.65 = (bf16[256,128]{1,0:T(8,128)(2,1)S(1)}, bf16[256,128]{1,0:T(8,128)(2,1)S(1)}, bf16[256,128]{1,0:T(8,128)(2,1)S(1)}, bf16[256,128]{1,0:T(8,128)(2,...) custom-call(s32[16,128]{1,0:T(8,128)S(1)} %get-tuple-element.34.refs_0_, ...), custom_call_target="tpu_custom_call" | custom-call | flops 2097152000 | bytes 4194304 | tf_op jit(solution)/shard_map/pallas_call | solution.py:246
  18.2 1.8 %collective-permute-start.3 = (bf16[6,128,128]{2,1,0:T(8,128)(2,1)S(1)}, bf16[6,128,128]{2,1,0:T(8,128)(2,1)S(1)}, u32[]{:S(2)}, u32[]{:S(2)}) collective-permute-start(bf16[6,128,128]{2,1,0:T(8,128)(2,1)S(1)} %bitcast.25), channel_id=1, source_target_pairs={{0,2},{1,3},{2,0},{3,1},{4,6},{5,7},{6,4},{7,5},{8,10},{9,11},{10,... | collective-permute-start | bytes 589832 | tf_op jit(solution)/shard_map/ppermute | solution.py:299
  20.0 0.0 collective-permute-done.refs_1_
  20.0 2.8 %collective-permute-done.1.refs_2_ = bf16[4,128,128]{2,1,0:T(8,128)(2,1)S(1)} collective-permute-done((bf16[4,128,128]{2,1,0:T(8,128)(2,1)S(1)}, bf16[4,128,128]{2,1,0:T(8,128)(2,1)S(1)}, u32[]{:S(2)}, u32[]{:S(2)}) %collective-permute-start.1) | collective-permute-done | bytes 131104 | tf_op jit(solution)/shard_map/ppermute | solution.py:299
  22.8 0.0 collective-permute-done.2.refs_3_
  22.9 1.4 %collective-permute-done.3 = bf16[6,128,128]{2,1,0:T(8,128)(2,1)S(1)} collective-permute-done((bf16[6,128,128]{2,1,0:T(8,128)(2,1)S(1)}, bf16[6,128,128]{2,1,0:T(8,128)(2,1)S(1)}, u32[]{:S(2)}, u32[]{:S(2)}) %collective-permute-start.3) | collective-permute-done | bytes 196640 | tf_op jit(solution)/shard_map/ppermute | solution.py:299
  24.4 0.7 %collective-permute-start.5 = (bf16[4,128,128]{2,1,0:T(8,128)(2,1)S(1)}, bf16[4,128,128]{2,1,0:T(8,128)(2,1)S(1)}, u32[]{:S(2)}, u32[]{:S(2)}) collective-permute-start(bf16[4,128,128]{2,1,0:T(8,128)(2,1)S(1)} %pad_maximum_fusion), channel_id=1, source_target_pairs={{0,4},{1,5},{2,6},{3,7},{4,0},{5,1},{6,2},{7,3},{8,12},{9,13},{10,... | collective-permute-start | bytes 393224 | tf_op jit(solution)/shard_map/ppermute | solution.py:299
  25.1 3.6 %collective-permute-start.6 = (bf16[4,128,128]{2,1,0:T(8,128)(2,1)S(1)}, bf16[4,128,128]{2,1,0:T(8,128)(2,1)S(1)}, u32[]{:S(2)}, u32[]{:S(2)}) collective-permute-start(bf16[4,128,128]{2,1,0:T(8,128)(2,1)S(1)} %pad_maximum_fusion.1), channel_id=1, source_target_pairs={{0,8},{1,9},{2,10},{3,11},{4,12},{5,13},{6,14},{7,15},{8,0},{9,1},... | collective-permute-start | bytes 393224 | tf_op jit(solution)/shard_map/ppermute | solution.py:299
  28.7 0.3 collective-permute-start.7
  29.0 1.5 %collective-permute-start.4 = (bf16[10,128,128]{2,1,0:T(8,128)(2,1)S(1)}, bf16[10,128,128]{2,1,0:T(8,128)(2,1)S(1)}, u32[]{:S(2)}, u32[]{:S(2)}) collective-permute-start(bf16[10,128,128]{2,1,0:T(8,128)(2,1)S(1)} %constant_dynamic-update-slice_fusion), channel_id=1, source_target_pairs={{0,2},{1,3},{2,0},{3,1},{4,6},{5,7},{6,4},{7,5},{8,10},{9,11},{10,... | collective-permute-start | bytes 983048 | tf_op jit(solution)/shard_map/ppermute | solution.py:299
  30.5 0.0 collective-permute-done.5.refs_5_
  30.6 6.6 %collective-permute-done.6.refs_6_ = bf16[4,128,128]{2,1,0:T(8,128)(2,1)S(1)} collective-permute-done((bf16[4,128,128]{2,1,0:T(8,128)(2,1)S(1)}, bf16[4,128,128]{2,1,0:T(8,128)(2,1)S(1)}, u32[]{:S(2)}, u32[]{:S(2)}) %collective-permute-start.6) | collective-permute-done | bytes 131104 | tf_op jit(solution)/shard_map/ppermute | solution.py:299
  37.2 0.0 collective-permute-done.7.refs_7_
  37.2 0.0 collective-permute-done.4.refs_0_
  37.3 0.1 collective-permute-start.9
  37.4 0.5 %collective-permute-start.8 = (bf16[7,128,128]{2,1,0:T(8,128)(2,1)S(1)}, bf16[7,128,128]{2,1,0:T(8,128)(2,1)S(1)}, u32[]{:S(2)}, u32[]{:S(2)}) collective-permute-start(bf16[7,128,128]{2,1,0:T(8,128)(2,1)S(1)} %constant_dynamic-update-slice_fusion.1), channel_id=1, source_target_pairs={{0,1},{1,0},{2,3},{3,2},{4,5},{5,4},{6,7},{7,6},{8,9},{9,8},{10,11... | collective-permute-start | bytes 688136 | tf_op jit(solution)/shard_map/ppermute | solution.py:299
  37.9 0.8 %shard_map.66.refs_3_ = bf16[128,4096]{1,0:T(8,128)(2,1)} custom-call(bf16[4,128,128]{2,1,0:T(8,128)(2,1)S(1)} %bitcast.18, bf16[4,128,128]{2,1,0:T(8,128)(2,1)S(1)} %collective-permute-done.refs_1_, bf16[4,128,128]{2,1,0:T(8,128)(2,1)S(1)} %collective-permute-done.1.refs_2_, bf16[4,128,128]{2,1,0:T(8,128)(2,1)S(1)} %collective-permute-done.2.refs_3_, ...), custom_call_target="tpu_custom_call" | custom-call | bytes 8388608 | tf_op jit(solution)/shard_map/pallas_call | solution.py:285
  38.7 0.6 %collective-permute-done.8.refs_1_ = bf16[7,128,128]{2,1,0:T(8,128)(2,1)S(1)} collective-permute-done((bf16[7,128,128]{2,1,0:T(8,128)(2,1)S(1)}, bf16[7,128,128]{2,1,0:T(8,128)(2,1)S(1)}, u32[]{:S(2)}, u32[]{:S(2)}) %collective-permute-start.8) | collective-permute-done | bytes 229408 | tf_op jit(solution)/shard_map/ppermute | solution.py:299
  39.3 0.0 collective-permute-done.9.refs_2_
  39.3 1.0 %shard_map.67 = bf16[128,4096]{1,0:T(8,128)(2,1)} custom-call(bf16[10,128,128]{2,1,0:T(8,128)(2,1)S(1)} %collective-permute-done.4.refs_0_, bf16[7,128,128]{2,1,0:T(8,128)(2,1)S(1)} %collective-permute-done.8.refs_1_, bf16[9,128,128]{2,1,0:T(8,128)(2,1)S(1)} %collective-permute-done.9.refs_2_, ...), custom_call_target="tpu_custom_call", output_to_operand_aliasing={{}: (3, {})} | custom-call | bytes 8388608 | tf_op jit(solution)/shard_map/pallas_call | solution.py:285
  (24 shorter events, 0.3 us)
Async XLA Ops:
  6.8 13.2 %collective-permute-start = (bf16[4,128,128]{2,1,0:T(8,128)(2,1)S(1)}, bf16[4,128,128]{2,1,0:T(8,128)(2,1)S(1)}, u32[]{:S(2)}, u32[]{:S(2)}) collective-permute-start(bf16[4,128,128]{2,1,0:T(8,128)(2,1)S(1)} %bitcast.28), channel_id=1, source_target_pairs={{0,4},{1,5},{2,6},{3,7},{4,0},{5,1},{6,2},{7,3},{8,12},{9,13},{10,... | collective-permute-start | bytes 393224 | tf_op jit(solution)/shard_map/ppermute | solution.py:299
  9.9 12.9 %collective-permute-start.1 = (bf16[4,128,128]{2,1,0:T(8,128)(2,1)S(1)}, bf16[4,128,128]{2,1,0:T(8,128)(2,1)S(1)}, u32[]{:S(2)}, u32[]{:S(2)}) collective-permute-start(bf16[4,128,128]{2,1,0:T(8,128)(2,1)S(1)} %bitcast.27), channel_id=1, source_target_pairs={{0,8},{1,9},{2,10},{3,11},{4,12},{5,13},{6,14},{7,15},{8,0},{9,1},... | collective-permute-start | bytes 393224 | tf_op jit(solution)/shard_map/ppermute | solution.py:299
  12.5 10.3 %collective-permute-start.2 = (bf16[4,128,128]{2,1,0:T(8,128)(2,1)S(1)}, bf16[4,128,128]{2,1,0:T(8,128)(2,1)S(1)}, u32[]{:S(2)}, u32[]{:S(2)}) collective-permute-start(bf16[4,128,128]{2,1,0:T(8,128)(2,1)S(1)} %bitcast.26), channel_id=1, source_target_pairs={{0,12},{1,13},{2,14},{3,15},{4,8},{5,9},{6,10},{7,11},{8,4},{9,5},... | collective-permute-start | bytes 393224 | tf_op jit(solution)/shard_map/ppermute | solution.py:299
  18.2 6.1 %collective-permute-start.3 = (bf16[6,128,128]{2,1,0:T(8,128)(2,1)S(1)}, bf16[6,128,128]{2,1,0:T(8,128)(2,1)S(1)}, u32[]{:S(2)}, u32[]{:S(2)}) collective-permute-start(bf16[6,128,128]{2,1,0:T(8,128)(2,1)S(1)} %bitcast.25), channel_id=1, source_target_pairs={{0,2},{1,3},{2,0},{3,1},{4,6},{5,7},{6,4},{7,5},{8,10},{9,11},{10,... | collective-permute-start | bytes 589832 | tf_op jit(solution)/shard_map/ppermute | solution.py:299
  24.4 6.1 %collective-permute-start.5 = (bf16[4,128,128]{2,1,0:T(8,128)(2,1)S(1)}, bf16[4,128,128]{2,1,0:T(8,128)(2,1)S(1)}, u32[]{:S(2)}, u32[]{:S(2)}) collective-permute-start(bf16[4,128,128]{2,1,0:T(8,128)(2,1)S(1)} %pad_maximum_fusion), channel_id=1, source_target_pairs={{0,4},{1,5},{2,6},{3,7},{4,0},{5,1},{6,2},{7,3},{8,12},{9,13},{10,... | collective-permute-start | bytes 393224 | tf_op jit(solution)/shard_map/ppermute | solution.py:299
  25.1 12.0 %collective-permute-start.6 = (bf16[4,128,128]{2,1,0:T(8,128)(2,1)S(1)}, bf16[4,128,128]{2,1,0:T(8,128)(2,1)S(1)}, u32[]{:S(2)}, u32[]{:S(2)}) collective-permute-start(bf16[4,128,128]{2,1,0:T(8,128)(2,1)S(1)} %pad_maximum_fusion.1), channel_id=1, source_target_pairs={{0,8},{1,9},{2,10},{3,11},{4,12},{5,13},{6,14},{7,15},{8,0},{9,1},... | collective-permute-start | bytes 393224 | tf_op jit(solution)/shard_map/ppermute | solution.py:299
  28.7 8.5 %collective-permute-start.7 = (bf16[4,128,128]{2,1,0:T(8,128)(2,1)S(1)}, bf16[4,128,128]{2,1,0:T(8,128)(2,1)S(1)}, u32[]{:S(2)}, u32[]{:S(2)}) collective-permute-start(bf16[4,128,128]{2,1,0:T(8,128)(2,1)S(1)} %pad_maximum_fusion.2), channel_id=1, source_target_pairs={{0,12},{1,13},{2,14},{3,15},{4,8},{5,9},{6,10},{7,11},{8,4},{9,5},... | collective-permute-start | bytes 393224 | tf_op jit(solution)/shard_map/ppermute | solution.py:299
  29.0 8.2 %collective-permute-start.4 = (bf16[10,128,128]{2,1,0:T(8,128)(2,1)S(1)}, bf16[10,128,128]{2,1,0:T(8,128)(2,1)S(1)}, u32[]{:S(2)}, u32[]{:S(2)}) collective-permute-start(bf16[10,128,128]{2,1,0:T(8,128)(2,1)S(1)} %constant_dynamic-update-slice_fusion), channel_id=1, source_target_pairs={{0,2},{1,3},{2,0},{3,1},{4,6},{5,7},{6,4},{7,5},{8,10},{9,11},{10,... | collective-permute-start | bytes 983048 | tf_op jit(solution)/shard_map/ppermute | solution.py:299
  37.3 2.0 %collective-permute-start.9 = (bf16[9,128,128]{2,1,0:T(8,128)(2,1)S(1)}, bf16[9,128,128]{2,1,0:T(8,128)(2,1)S(1)}, u32[]{:S(2)}, u32[]{:S(2)}) collective-permute-start(bf16[9,128,128]{2,1,0:T(8,128)(2,1)S(1)} %constant_dynamic-update-slice_fusion.8), channel_id=1, source_target_pairs={{0,1},{1,0},{2,3},{3,2},{4,5},{5,4},{6,7},{7,6},{8,9},{9,8},{10,11... | collective-permute-start | bytes 884744 | tf_op jit(solution)/shard_map/ppermute | solution.py:299
  37.4 1.9 %collective-permute-start.8 = (bf16[7,128,128]{2,1,0:T(8,128)(2,1)S(1)}, bf16[7,128,128]{2,1,0:T(8,128)(2,1)S(1)}, u32[]{:S(2)}, u32[]{:S(2)}) collective-permute-start(bf16[7,128,128]{2,1,0:T(8,128)(2,1)S(1)} %constant_dynamic-update-slice_fusion.1), channel_id=1, source_target_pairs={{0,1},{1,0},{2,3},{3,2},{4,5},{5,4},{6,7},{7,6},{8,9},{9,8},{10,11... | collective-permute-start | bytes 688136 | tf_op jit(solution)/shard_map/ppermute | solution.py:299

commit v9 on v8

--- a/solution.py
+++ b/solution.py
@@ -52,18 +52,15 @@
         later = bring(piece + 1, ahead, 1) if ahead else []
         for copy in now:
             copy.start()
-        for copy in now:
-            copy.wait()
-        for copy in later:
-            copy.start()
+        now[0].wait()
     else:
-        held, later = given, []
-    compute(place, sends, held, outs, *refs)
+        held, now, later = given, [], []
+    compute(place, sends, held, outs, now[1:7], now[7:], later, *refs)
     for copy in later:
         copy.wait()
 
 
-def compute(place, sends, held, outs, halo, query, gated, inputs, gains, result, *streams):
+def compute(place, sends, held, outs, words, rows, later, halo, query, gated, inputs, gains, result, *streams):
     ids, table, taps, residue, decay, skip = held
     length = ids.shape[0] * ids.shape[1]
     steps = length // RUNS
@@ -78,7 +75,7 @@
     part = cols // len(streams)
     word = lax.broadcasted_iota(jnp.int32, (RUNS, half), 1)
 
-    def look_up(here, first, count, place_row):
+    def look_up(here, first, count, place_row, copies=()):
         upper = here >= half
         within = jnp.where(upper, here - half, here)
         hot = [
@@ -86,12 +83,14 @@
             for j in range(first, first + count)
         ]
         hot = jnp.concatenate(hot, axis=0).astype(jnp.bfloat16)
+        for copy in copies:
+            copy.wait()
         found = jnp.dot(hot, table[...], preferred_element_type=jnp.float32)
         for j in range(count):
             above = spread(here[:, first + j : first + j + 1]) >= half
-            rows = found[j * RUNS : (j + 1) * RUNS]
+            line = found[j * RUNS : (j + 1) * RUNS]
             for k in range(3):
-                low, high = (rows[:, n * LANES : (n + 1) * LANES] for n in (k, k + 3))
+                low, high = (line[:, n * LANES : (n + 1) * LANES] for n in (k, k + 3))
                 place_row(k, j, jnp.where(above, high, low))
 
     def ids_of(block):
@@ -100,7 +99,11 @@
     def place_tail(k, j, row):
         halo[k, j * RUNS : (j + 1) * RUNS, :] = delay_runs(row, 1)
 
-    look_up(ids_of(steps // cols - 1), cols - rim, rim, place_tail)
+    look_up(ids_of(steps // cols - 1), cols - rim, rim, place_tail, words)
+    for copy in rows:
+        copy.wait()
+    for copy in later:
+        copy.start()
 
     filters = [[spread(taps[k, lag : lag + 1, :]) for lag in range(width)] for k in range(3)]
 

time: 40.5 us -> 40.4 us (level)
  no operation moved by 1% of the time
where the time goes in v9:
time: 40.4 us; the launch traced here: 40.2 us
  Pallas kernels  14.3 us (35%)
  starting transfers between devices  14.1 us (35%)
  waiting for transfers between devices  11.4 us (28%)
    ppermute x10, starting transfers between devices, by_hops(): lax.ppermute(x, 'seq', [(i, i ^ by) for i in range(places)])  14.1 us
    pallas_call x2, Pallas kernels, run_operator(): pl.pallas_call(functools.partial(operator, (piece, pieces, sends, sliced,...  12.5 us
    ppermute x10, waiting for transfers between devices, by_hops(): lax.ppermute(x, 'seq', [(i, i ^ by) for i in range(places)])  11.4 us
    pallas_call x2, Pallas kernels, run_join(): pl.pallas_call(kernel, in_specs=[anywhere] * (len(arrays) + len(into)), o...  1.83 us
  transfers between devices with their start and end apart: 10, of which 4 were waited for; matrix products, arithmetic and copies ran while one was open for 0% of the time, Pallas kernels for 16%

profile of v9, /device:TPU:0, one launch (start us, length us, event | category | flops | bytes accessed | tf_op | source)
XLA Modules:
  0.0 40.2 jit_solution(15401172791699667504)
XLA Ops:
  0.0 6.7 %shard_map.64 = (bf16[512,128]{1,0:T(8,128)(2,1)S(1)}, bf16[512,128]{1,0:T(8,128)(2,1)S(1)}, bf16[512,128]{1,0:T(8,128)(2,1)S(1)}, bf16[512,128]{1,0:T(8,128)(2,...) custom-call(s32[16,128]{1,0:T(8,128)} %bitcast.34, ...), custom_call_target="tpu_custom_call" | custom-call | flops 2097152000 | bytes 4194304 | tf_op jit(solution)/shard_map/pallas_call | solution.py:249
  6.7 3.1 %collective-permute-start = (bf16[4,128,128]{2,1,0:T(8,128)(2,1)S(1)}, bf16[4,128,128]{2,1,0:T(8,128)(2,1)S(1)}, u32[]{:S(2)}, u32[]{:S(2)}) collective-permute-start(bf16[4,128,128]{2,1,0:T(8,128)(2,1)S(1)} %bitcast.28), channel_id=1, source_target_pairs={{0,4},{1,5},{2,6},{3,7},{4,0},{5,1},{6,2},{7,3},{8,12},{9,13},{10,... | collective-permute-start | bytes 393224 | tf_op jit(solution)/shard_map/ppermute | solution.py:302
  9.8 2.6 %collective-permute-start.1 = (bf16[4,128,128]{2,1,0:T(8,128)(2,1)S(1)}, bf16[4,128,128]{2,1,0:T(8,128)(2,1)S(1)}, u32[]{:S(2)}, u32[]{:S(2)}) collective-permute-start(bf16[4,128,128]{2,1,0:T(8,128)(2,1)S(1)} %bitcast.27), channel_id=1, source_target_pairs={{0,8},{1,9},{2,10},{3,11},{4,12},{5,13},{6,14},{7,15},{8,0},{9,1},... | collective-permute-start | bytes 393224 | tf_op jit(solution)/shard_map/ppermute | solution.py:302
  12.4 0.0 collective-permute-start.2
  12.4 5.8 %shard_map.65 = (bf16[256,128]{1,0:T(8,128)(2,1)S(1)}, bf16[256,128]{1,0:T(8,128)(2,1)S(1)}, bf16[256,128]{1,0:T(8,128)(2,1)S(1)}, bf16[256,128]{1,0:T(8,128)(2,...) custom-call(s32[16,128]{1,0:T(8,128)S(1)} %get-tuple-element.34.refs_0_, ...), custom_call_target="tpu_custom_call" | custom-call | flops 2097152000 | bytes 4194304 | tf_op jit(solution)/shard_map/pallas_call | solution.py:249
  18.2 1.8 %collective-permute-start.3 = (bf16[6,128,128]{2,1,0:T(8,128)(2,1)S(1)}, bf16[6,128,128]{2,1,0:T(8,128)(2,1)S(1)}, u32[]{:S(2)}, u32[]{:S(2)}) collective-permute-start(bf16[6,128,128]{2,1,0:T(8,128)(2,1)S(1)} %bitcast.25), channel_id=1, source_target_pairs={{0,2},{1,3},{2,0},{3,1},{4,6},{5,7},{6,4},{7,5},{8,10},{9,11},{10,... | collective-permute-start | bytes 589832 | tf_op jit(solution)/shard_map/ppermute | solution.py:302
  20.0 0.0 collective-permute-done.refs_1_
  20.0 2.8 %collective-permute-done.1.refs_2_ = bf16[4,128,128]{2,1,0:T(8,128)(2,1)S(1)} collective-permute-done((bf16[4,128,128]{2,1,0:T(8,128)(2,1)S(1)}, bf16[4,128,128]{2,1,0:T(8,128)(2,1)S(1)}, u32[]{:S(2)}, u32[]{:S(2)}) %collective-permute-start.1) | collective-permute-done | bytes 131104 | tf_op jit(solution)/shard_map/ppermute | solution.py:302
  22.8 0.0 collective-permute-done.2.refs_3_
  22.9 1.4 %collective-permute-done.3 = bf16[6,128,128]{2,1,0:T(8,128)(2,1)S(1)} collective-permute-done((bf16[6,128,128]{2,1,0:T(8,128)(2,1)S(1)}, bf16[6,128,128]{2,1,0:T(8,128)(2,1)S(1)}, u32[]{:S(2)}, u32[]{:S(2)}) %collective-permute-start.3) | collective-permute-done | bytes 196640 | tf_op jit(solution)/shard_map/ppermute | solution.py:302
  24.4 0.7 %collective-permute-start.5 = (bf16[4,128,128]{2,1,0:T(8,128)(2,1)S(1)}, bf16[4,128,128]{2,1,0:T(8,128)(2,1)S(1)}, u32[]{:S(2)}, u32[]{:S(2)}) collective-permute-start(bf16[4,128,128]{2,1,0:T(8,128)(2,1)S(1)} %pad_maximum_fusion), channel_id=1, source_target_pairs={{0,4},{1,5},{2,6},{3,7},{4,0},{5,1},{6,2},{7,3},{8,12},{9,13},{10,... | collective-permute-start | bytes 393224 | tf_op jit(solution)/shard_map/ppermute | solution.py:302
  25.1 3.6 %collective-permute-start.6 = (bf16[4,128,128]{2,1,0:T(8,128)(2,1)S(1)}, bf16[4,128,128]{2,1,0:T(8,128)(2,1)S(1)}, u32[]{:S(2)}, u32[]{:S(2)}) collective-permute-start(bf16[4,128,128]{2,1,0:T(8,128)(2,1)S(1)} %pad_maximum_fusion.1), channel_id=1, source_target_pairs={{0,8},{1,9},{2,10},{3,11},{4,12},{5,13},{6,14},{7,15},{8,0},{9,1},... | collective-permute-start | bytes 393224 | tf_op jit(solution)/shard_map/ppermute | solution.py:302
  28.7 0.3 collective-permute-start.7
  29.0 1.5 %collective-permute-start.4 = (bf16[10,128,128]{2,1,0:T(8,128)(2,1)S(1)}, bf16[10,128,128]{2,1,0:T(8,128)(2,1)S(1)}, u32[]{:S(2)}, u32[]{:S(2)}) collective-permute-start(bf16[10,128,128]{2,1,0:T(8,128)(2,1)S(1)} %constant_dynamic-update-slice_fusion), channel_id=1, source_target_pairs={{0,2},{1,3},{2,0},{3,1},{4,6},{5,7},{6,4},{7,5},{8,10},{9,11},{10,... | collective-permute-start | bytes 983048 | tf_op jit(solution)/shard_map/ppermute | solution.py:302
  30.5 0.0 collective-permute-done.5.refs_5_
  30.5 6.6 %collective-permute-done.6.refs_6_ = bf16[4,128,128]{2,1,0:T(8,128)(2,1)S(1)} collective-permute-done((bf16[4,128,128]{2,1,0:T(8,128)(2,1)S(1)}, bf16[4,128,128]{2,1,0:T(8,128)(2,1)S(1)}, u32[]{:S(2)}, u32[]{:S(2)}) %collective-permute-start.6) | collective-permute-done | bytes 131104 | tf_op jit(solution)/shard_map/ppermute | solution.py:302
  37.1 0.0 collective-permute-done.7.refs_7_
  37.2 0.0 collective-permute-done.4.refs_0_
  37.2 0.1 collective-permute-start.9
  37.3 0.5 %collective-permute-start.8 = (bf16[7,128,128]{2,1,0:T(8,128)(2,1)S(1)}, bf16[7,128,128]{2,1,0:T(8,128)(2,1)S(1)}, u32[]{:S(2)}, u32[]{:S(2)}) collective-permute-start(bf16[7,128,128]{2,1,0:T(8,128)(2,1)S(1)} %constant_dynamic-update-slice_fusion.1), channel_id=1, source_target_pairs={{0,1},{1,0},{2,3},{3,2},{4,5},{5,4},{6,7},{7,6},{8,9},{9,8},{10,11... | collective-permute-start | bytes 688136 | tf_op jit(solution)/shard_map/ppermute | solution.py:302
  37.8 0.8 %shard_map.66.refs_3_ = bf16[128,4096]{1,0:T(8,128)(2,1)} custom-call(bf16[4,128,128]{2,1,0:T(8,128)(2,1)S(1)} %bitcast.18, bf16[4,128,128]{2,1,0:T(8,128)(2,1)S(1)} %collective-permute-done.refs_1_, bf16[4,128,128]{2,1,0:T(8,128)(2,1)S(1)} %collective-permute-done.1.refs_2_, bf16[4,128,128]{2,1,0:T(8,128)(2,1)S(1)} %collective-permute-done.2.refs_3_, ...), custom_call_target="tpu_custom_call" | custom-call | bytes 8388608 | tf_op jit(solution)/shard_map/pallas_call | solution.py:288
  38.7 0.6 %collective-permute-done.8.refs_1_ = bf16[7,128,128]{2,1,0:T(8,128)(2,1)S(1)} collective-permute-done((bf16[7,128,128]{2,1,0:T(8,128)(2,1)S(1)}, bf16[7,128,128]{2,1,0:T(8,128)(2,1)S(1)}, u32[]{:S(2)}, u32[]{:S(2)}) %collective-permute-start.8) | collective-permute-done | bytes 229408 | tf_op jit(solution)/shard_map/ppermute | solution.py:302
  39.2 0.0 collective-permute-done.9.refs_2_
  39.2 1.0 %shard_map.67 = bf16[128,4096]{1,0:T(8,128)(2,1)} custom-call(bf16[10,128,128]{2,1,0:T(8,128)(2,1)S(1)} %collective-permute-done.4.refs_0_, bf16[7,128,128]{2,1,0:T(8,128)(2,1)S(1)} %collective-permute-done.8.refs_1_, bf16[9,128,128]{2,1,0:T(8,128)(2,1)S(1)} %collective-permute-done.9.refs_2_, ...), custom_call_target="tpu_custom_call", output_to_operand_aliasing={{}: (3, {})} | custom-call | bytes 8388608 | tf_op jit(solution)/shard_map/pallas_call | solution.py:288
  (24 shorter events, 0.3 us)
Async XLA Ops:
  6.7 13.2 %collective-permute-start = (bf16[4,128,128]{2,1,0:T(8,128)(2,1)S(1)}, bf16[4,128,128]{2,1,0:T(8,128)(2,1)S(1)}, u32[]{:S(2)}, u32[]{:S(2)}) collective-permute-start(bf16[4,128,128]{2,1,0:T(8,128)(2,1)S(1)} %bitcast.28), channel_id=1, source_target_pairs={{0,4},{1,5},{2,6},{3,7},{4,0},{5,1},{6,2},{7,3},{8,12},{9,13},{10,... | collective-permute-start | bytes 393224 | tf_op jit(solution)/shard_map/ppermute | solution.py:302
  9.8 12.9 %collective-permute-start.1 = (bf16[4,128,128]{2,1,0:T(8,128)(2,1)S(1)}, bf16[4,128,128]{2,1,0:T(8,128)(2,1)S(1)}, u32[]{:S(2)}, u32[]{:S(2)}) collective-permute-start(bf16[4,128,128]{2,1,0:T(8,128)(2,1)S(1)} %bitcast.27), channel_id=1, source_target_pairs={{0,8},{1,9},{2,10},{3,11},{4,12},{5,13},{6,14},{7,15},{8,0},{9,1},... | collective-permute-start | bytes 393224 | tf_op jit(solution)/shard_map/ppermute | solution.py:302
  12.4 10.3 %collective-permute-start.2 = (bf16[4,128,128]{2,1,0:T(8,128)(2,1)S(1)}, bf16[4,128,128]{2,1,0:T(8,128)(2,1)S(1)}, u32[]{:S(2)}, u32[]{:S(2)}) collective-permute-start(bf16[4,128,128]{2,1,0:T(8,128)(2,1)S(1)} %bitcast.26), channel_id=1, source_target_pairs={{0,12},{1,13},{2,14},{3,15},{4,8},{5,9},{6,10},{7,11},{8,4},{9,5},... | collective-permute-start | bytes 393224 | tf_op jit(solution)/shard_map/ppermute | solution.py:302
  18.2 6.1 %collective-permute-start.3 = (bf16[6,128,128]{2,1,0:T(8,128)(2,1)S(1)}, bf16[6,128,128]{2,1,0:T(8,128)(2,1)S(1)}, u32[]{:S(2)}, u32[]{:S(2)}) collective-permute-start(bf16[6,128,128]{2,1,0:T(8,128)(2,1)S(1)} %bitcast.25), channel_id=1, source_target_pairs={{0,2},{1,3},{2,0},{3,1},{4,6},{5,7},{6,4},{7,5},{8,10},{9,11},{10,... | collective-permute-start | bytes 589832 | tf_op jit(solution)/shard_map/ppermute | solution.py:302
  24.4 6.1 %collective-permute-start.5 = (bf16[4,128,128]{2,1,0:T(8,128)(2,1)S(1)}, bf16[4,128,128]{2,1,0:T(8,128)(2,1)S(1)}, u32[]{:S(2)}, u32[]{:S(2)}) collective-permute-start(bf16[4,128,128]{2,1,0:T(8,128)(2,1)S(1)} %pad_maximum_fusion), channel_id=1, source_target_pairs={{0,4},{1,5},{2,6},{3,7},{4,0},{5,1},{6,2},{7,3},{8,12},{9,13},{10,... | collective-permute-start | bytes 393224 | tf_op jit(solution)/shard_map/ppermute | solution.py:302
  25.1 12.0 %collective-permute-start.6 = (bf16[4,128,128]{2,1,0:T(8,128)(2,1)S(1)}, bf16[4,128,128]{2,1,0:T(8,128)(2,1)S(1)}, u32[]{:S(2)}, u32[]{:S(2)}) collective-permute-start(bf16[4,128,128]{2,1,0:T(8,128)(2,1)S(1)} %pad_maximum_fusion.1), channel_id=1, source_target_pairs={{0,8},{1,9},{2,10},{3,11},{4,12},{5,13},{6,14},{7,15},{8,0},{9,1},... | collective-permute-start | bytes 393224 | tf_op jit(solution)/shard_map/ppermute | solution.py:302
  28.7 8.5 %collective-permute-start.7 = (bf16[4,128,128]{2,1,0:T(8,128)(2,1)S(1)}, bf16[4,128,128]{2,1,0:T(8,128)(2,1)S(1)}, u32[]{:S(2)}, u32[]{:S(2)}) collective-permute-start(bf16[4,128,128]{2,1,0:T(8,128)(2,1)S(1)} %pad_maximum_fusion.2), channel_id=1, source_target_pairs={{0,12},{1,13},{2,14},{3,15},{4,8},{5,9},{6,10},{7,11},{8,4},{9,5},... | collective-permute-start | bytes 393224 | tf_op jit(solution)/shard_map/ppermute | solution.py:302
  29.0 8.2 %collective-permute-start.4 = (bf16[10,128,128]{2,1,0:T(8,128)(2,1)S(1)}, bf16[10,128,128]{2,1,0:T(8,128)(2,1)S(1)}, u32[]{:S(2)}, u32[]{:S(2)}) collective-permute-start(bf16[10,128,128]{2,1,0:T(8,128)(2,1)S(1)} %constant_dynamic-update-slice_fusion), channel_id=1, source_target_pairs={{0,2},{1,3},{2,0},{3,1},{4,6},{5,7},{6,4},{7,5},{8,10},{9,11},{10,... | collective-permute-start | bytes 983048 | tf_op jit(solution)/shard_map/ppermute | solution.py:302
  37.2 2.0 %collective-permute-start.9 = (bf16[9,128,128]{2,1,0:T(8,128)(2,1)S(1)}, bf16[9,128,128]{2,1,0:T(8,128)(2,1)S(1)}, u32[]{:S(2)}, u32[]{:S(2)}) collective-permute-start(bf16[9,128,128]{2,1,0:T(8,128)(2,1)S(1)} %constant_dynamic-update-slice_fusion.8), channel_id=1, source_target_pairs={{0,1},{1,0},{2,3},{3,2},{4,5},{5,4},{6,7},{7,6},{8,9},{9,8},{10,11... | collective-permute-start | bytes 884744 | tf_op jit(solution)/shard_map/ppermute | solution.py:302
  37.3 1.9 %collective-permute-start.8 = (bf16[7,128,128]{2,1,0:T(8,128)(2,1)S(1)}, bf16[7,128,128]{2,1,0:T(8,128)(2,1)S(1)}, u32[]{:S(2)}, u32[]{:S(2)}) collective-permute-start(bf16[7,128,128]{2,1,0:T(8,128)(2,1)S(1)} %constant_dynamic-update-slice_fusion.1), channel_id=1, source_target_pairs={{0,1},{1,0},{2,3},{3,2},{4,5},{5,4},{6,7},{7,6},{8,9},{9,8},{10,11... | collective-permute-start | bytes 688136 | tf_op jit(solution)/shard_map/ppermute | solution.py:302
